TPU v7x, 32 devices: a whole 2x2x4 slice. The times are simulated.
32 devices in a mesh: slab: 4 (over y, x), dev: 8 (over z, core).
Axes of the slice: x: 2, y: 2, z: 4, core: 2. Of those that a mesh axis runs over, the one named last changes fastest.
Arguments:
- layer_input: bfloat16 [8, 2048, 1152], P('dev', 'slab'), may hold values from -6 to 6
- output_grad: bfloat16 [8, 2048, 1152], P('dev', 'slab'), may hold values from -6 to 6
- expert_lists: int32 [4, 8, 512], P('slab'), may hold values from 0 to 4095, as said below
- gate_values: float32 [4, 8, 512], P('slab', 'dev'), may hold values from 0.1 to 1
- weight_in: bfloat16 [8, 1152, 2304], P('dev'), may hold values from -0.1875 to 0.1875
- weight_out: bfloat16 [8, 2304, 1152], P('dev'), may hold values from -0.125 to 0.125
- query_rows: bfloat16 [8, 2048, 1152], P(None, ('slab', 'dev')), may hold values from -8 to 8
- key_rows: bfloat16 [8, 2048, 1152], P(None, ('slab', 'dev')), may hold values from -8 to 8
- value_rows: bfloat16 [8, 2048, 1152], P(None, ('slab', 'dev')), may hold values from -6 to 6
Outputs:
- gate_grad: float32 [4, 8, 512], P('slab', 'dev')
- weight_in_grad: float32 [8, 1152, 2304], P('dev', 'slab')
- weight_out_grad: float32 [8, 2304, 1152], P('dev', 'slab')
- query_grad: bfloat16 [8, 2048, 1152], P('dev', 'slab')
- key_grad: bfloat16 [8, 2048, 1152], P('dev', 'slab')
- value_grad: bfloat16 [8, 2048, 1152], P('dev', 'slab')
Inputs may be any that keep to these rules, and one draw needn't show every extreme that they name: `expert_lists`: each row of a slab holds 512 distinct slab tokens. Of the 512 tokens i * 512 to (i + 1) * 512 - 1 of any frame shard i, one row takes at most 128, and every row takes exactly 128 from some frame shard.
All inputs are finite; a program needn't handle non-finite values.
Results may differ from a plain program's by a relative error of at most 0.012.
Values may be sent and summed in bfloat16 or wider, within the bound.
No kernel may reach another device: no remote copies, remote signals or barrier semaphores. Data moves between devices by JAX's collectives and lax.ppermute only.
A program may use at most 128 MiB of HBM per device.

v0:
```python
import jax
import jax.numpy as jnp
from jax import lax
from jax.sharding import PartitionSpec as P

D = 1152
HEADS = 16
HEAD_DIM = 72


def gelu_tanh(values):
    return jax.nn.gelu(values, approximate=True)


def attention_grad(query_part, key_part, value_part, grad_out):
    frame_count = query_part.shape[0]
    patch_count = query_part.shape[1]
    split_shape = (frame_count, patch_count, HEADS, HEAD_DIM)
    query_full = query_part.reshape(split_shape)
    key_full = key_part.reshape(split_shape)
    value_full = value_part.reshape(split_shape)
    grad_full = grad_out.reshape(split_shape)
    scale_factor = HEAD_DIM ** (-0.5)
    scores = (
        jnp.einsum("fphd,gphd->phfg", query_full, key_full, preferred_element_type=jnp.float32)
        * scale_factor
    )
    attn_probs = jax.nn.softmax(scores, axis=-1)
    probs_low = attn_probs.astype(jnp.bfloat16)
    value_grad = jnp.einsum(
        "phfg,fphd->gphd", probs_low, grad_full, preferred_element_type=jnp.float32
    )
    prob_grad = jnp.einsum(
        "fphd,gphd->phfg", grad_full, value_full, preferred_element_type=jnp.float32
    )
    row_delta = jnp.sum(attn_probs * prob_grad, axis=-1, keepdims=True)
    score_grad = (attn_probs * (prob_grad - row_delta)).astype(jnp.bfloat16)
    query_grad = (
        jnp.einsum("phfg,gphd->fphd", score_grad, key_full, preferred_element_type=jnp.float32)
        * scale_factor
    )
    key_grad = (
        jnp.einsum("phfg,fphd->gphd", score_grad, query_full, preferred_element_type=jnp.float32)
        * scale_factor
    )
    flat_shape = (frame_count, patch_count, D)
    return (
        query_grad.reshape(flat_shape).astype(jnp.bfloat16),
        key_grad.reshape(flat_shape).astype(jnp.bfloat16),
        value_grad.reshape(flat_shape).astype(jnp.bfloat16),
    )


def body(
    layer_input,
    output_grad,
    expert_lists,
    gate_values,
    weight_in,
    weight_out,
    query_rows,
    key_rows,
    value_rows,
):
    dev_count = lax.axis_size("dev")
    my_index = lax.axis_index("dev")
    frames_here, patches, model_width = layer_input.shape
    tok_local = frames_here * patches
    capacity = expert_lists.shape[2]
    slot_count = 2 * capacity // dev_count
    list_table = expert_lists[0]
    owner_dev = list_table // tok_local
    offset = list_table - owner_dev * tok_local
    is_mine = owner_dev == my_index
    slot_rank = jnp.cumsum(is_mine.astype(jnp.int32), axis=1) - 1
    slot_ids = jnp.arange(slot_count, dtype=jnp.int32)
    slot_hit = is_mine[:, :, None] & (slot_rank[:, :, None] == slot_ids[None, None, :])
    send_index = jnp.sum(jnp.where(slot_hit, offset[:, :, None], 0), axis=1)
    send_valid = jnp.any(slot_hit, axis=1)
    flat_input = layer_input.reshape(tok_local, model_width)
    flat_grad = output_grad.reshape(tok_local, model_width)
    keep_mask = send_valid[:, :, None]
    empty_low = jnp.zeros((), jnp.bfloat16)
    input_send = jnp.where(keep_mask, flat_input[send_index], empty_low)
    grad_send = jnp.where(keep_mask, flat_grad[send_index], empty_low)
    input_recv, grad_recv = (
        lax.all_to_all(input_send, "dev", split_axis=0, concat_axis=0, tiled=True),
        lax.all_to_all(grad_send, "dev", split_axis=0, concat_axis=0, tiled=True),
    )
    my_owners = lax.dynamic_index_in_dim(owner_dev, my_index, 0, keepdims=False)
    onehot = (my_owners[:, None] == jnp.arange(dev_count, dtype=jnp.int32)[None, :]).astype(
        jnp.int32
    )
    my_rank = jnp.sum((jnp.cumsum(onehot, axis=0) - 1) * onehot, axis=1)
    position = my_owners * slot_count + my_rank
    input_rows = input_recv.reshape(-1, model_width)[position]
    grad_rows = grad_recv.reshape(-1, model_width)[position]
    gate_row = gate_values[0, 0]
    weight_first = weight_in[0]
    weight_second = weight_out[0]
    pre_act = jnp.dot(input_rows, weight_first, preferred_element_type=jnp.float32)
    act_full, pullback = jax.vjp(gelu_tanh, pre_act)
    act_rows = act_full.astype(jnp.bfloat16)
    back_proj = lax.dot_general(
        grad_rows, weight_second, (((1,), (1,)), ((), ())), preferred_element_type=jnp.float32
    )
    gate_grad = jnp.sum(act_rows.astype(jnp.float32) * back_proj, axis=1)
    scaled = (gate_row[:, None] * grad_rows.astype(jnp.float32)).astype(jnp.bfloat16)
    pre_grad = pullback(gate_row[:, None] * back_proj)[0].astype(jnp.bfloat16)
    in_share = lax.psum_scatter(
        lax.dot_general(
            input_rows, pre_grad, (((0,), (0,)), ((), ())), preferred_element_type=jnp.float32
        ).astype(jnp.bfloat16),
        "slab",
        scatter_dimension=0,
        tiled=True,
    ).astype(jnp.float32)
    out_share = lax.psum_scatter(
        lax.dot_general(
            act_rows, scaled, (((0,), (0,)), ((), ())), preferred_element_type=jnp.float32
        ).astype(jnp.bfloat16),
        "slab",
        scatter_dimension=0,
        tiled=True,
    ).astype(jnp.float32)
    row_grad = lax.dot_general(
        pre_grad, weight_first, (((1,), (1,)), ((), ())), preferred_element_type=jnp.float32
    ).astype(jnp.bfloat16)
    return_send = (
        jnp.zeros((dev_count * slot_count, model_width), jnp.bfloat16).at[position].set(row_grad)
    )
    return_send = return_send.reshape(dev_count, slot_count, model_width)
    returned = lax.all_to_all(return_send, "dev", split_axis=0, concat_axis=0, tiled=True)
    combined = jax.ops.segment_sum(
        returned.reshape(-1, model_width).astype(jnp.float32),
        send_index.reshape(-1),
        num_segments=tok_local,
    ).astype(jnp.bfloat16)
    combined = combined.reshape(frames_here, patches, model_width)
    grad_frames = (output_grad.astype(jnp.float32) + combined.astype(jnp.float32)).astype(
        jnp.bfloat16
    )
    grad_attn = lax.all_to_all(grad_frames, "dev", split_axis=1, concat_axis=0, tiled=True)
    query_grad, key_grad, value_grad = attention_grad(query_rows, key_rows, value_rows, grad_attn)
    query_back, key_back, value_back = (
        lax.all_to_all(query_grad, "dev", split_axis=0, concat_axis=1, tiled=True),
        lax.all_to_all(key_grad, "dev", split_axis=0, concat_axis=1, tiled=True),
        lax.all_to_all(value_grad, "dev", split_axis=0, concat_axis=1, tiled=True),
    )
    return (
        gate_grad.reshape(1, 1, capacity),
        in_share[None],
        out_share[None],
        query_back,
        key_back,
        value_back,
    )


def solution(mesh):
    return jax.shard_map(
        body,
        mesh=mesh,
        in_specs=(
            P("dev", "slab", None),
            P("dev", "slab", None),
            P("slab", None, None),
            P("slab", "dev", None),
            P("dev", None, None),
            P("dev", None, None),
            P(None, ("slab", "dev"), None),
            P(None, ("slab", "dev"), None),
            P(None, ("slab", "dev"), None),
        ),
        out_specs=(
            P("slab", "dev", None),
            P("dev", "slab", None),
            P("dev", "slab", None),
            P("dev", "slab", None),
            P("dev", "slab", None),
            P("dev", "slab", None),
        ),
        check_vma=False,
    )
```

profile of v0, /device:TPU:0, one launch (start us, length us, event | category | flops | bytes accessed | tf_op | source)
XLA Modules:
  0.0 459.4 jit_solution(12962999823093855278)
XLA Ops:
  14.8 5.4 %gather_fusion = bf16[1024,1152]{1,0:T(8,128)(2,1)} fusion(bf16[512,1152]{1,0:T(8,128)(2,1)S(1)} %bitcast.121, s32[1024]{0:T(1024)S(1)} %fusion.60), kind=kCustom, calls=%fused_computation | custom fusion | bytes 4722688 | tf_op jit(solution)/shard_map/gather | solution.py:84
  20.2 5.4 %gather_fusion.2 = bf16[1024,1152]{1,0:T(8,128)(2,1)} fusion(bf16[512,1152]{1,0:T(8,128)(2,1)S(1)} %bitcast.122, s32[1024]{0:T(1024)S(1)} %fusion.60), kind=kCustom, calls=%fused_computation.2 | custom fusion | bytes 4722688 | tf_op jit(solution)/shard_map/gather | solution.py:85
  29.9 60.9 %all_to_all.60 = bf16[8,128,1152]{2,1,0:T(8,128)(2,1)} all-to-all(bf16[8,128,1152]{2,1,0:T(8,128)(2,1)S(1)} %get-tuple-element.11), channel_id=1, replica_groups=mesh['slab'=4,'dev'=8] {'dev'}, dimensions={0} | all-to-all | bytes 4718592 | tf_op jit(solution)/shard_map/all_to_all | solution.py:88
  97.0 4.9 %gather_fusion.3 = bf16[512,1152]{1,0:T(8,128)(2,1)S(1)} fusion(bf16[1024,1152]{1,0:T(8,128)(2,1)} %bitcast.123, s32[1024]{0:T(1024)S(1)} %pad_clamp_fusion), kind=kCustom, calls=%fused_computation.3 | custom fusion | bytes 2361344 | tf_op jit(solution)/shard_map/gather | solution.py:97
  102.0 47.9 %all-to-all-done = bf16[8,128,1152]{2,1,0:T(8,128)(2,1)} async-done(((bf16[8,128,1152]{2,1,0:T(8,128)(2,1)}), bf16[8,128,1152]{2,1,0:T(8,128)(2,1)}, u32[]{:S(2)}, u32[]{:S(2)}) %all-to-all-start) | async-done | bytes 2359328 | tf_op jit(solution)/shard_map/all_to_all | solution.py:87
  149.9 4.9 %gather_fusion.1 = bf16[512,1152]{1,0:T(8,128)(2,1)S(1)} fusion(bf16[1024,1152]{1,0:T(8,128)(2,1)} %bitcast.7, s32[1024]{0:T(1024)S(1)} %pad_clamp_fusion), kind=kCustom, calls=%fused_computation.1 | custom fusion | bytes 2361344 | tf_op jit(solution)/shard_map/gather | solution.py:96
  154.8 5.8 %fusion.1 = f32[512,2304]{1,0:T(8,128)S(1)} fusion(bf16[512,1152]{1,0:T(8,128)(2,1)S(1)} %gather_fusion.3, bf16[1,2304,1152]{2,1,0:T(8,128)(2,1)} %param.14), kind=kOutput, calls=%fused_computation.11 | convolution fusion | flops 2717908992 | bytes 11206656 | tf_op jit(solution)/shard_map/dot_general | solution.py:104
  160.6 9.4 %fusion.13 = (bf16[512,2304]{1,0:T(8,128)(2,1)S(1)}, f32[512]{0:T(512)}, f32[512,2304]{1,0:T(8,128)}) fusion(f32[512,2304]{1,0:T(8,128)S(1)} %fusion.1, f32[512]{0:T(512)S(1)} %bitcast.137, bf16[512,1152]{1,0:T(8,128)(2,1)S(1)} %gather_fusion.1, bf16[1,1152,2304]{2,1,0:T(8,128)(2,1)} %param.13), kind=kOutput, calls=%fused_computation.23 | convolution fusion | flops 2748579328 | bytes 18288640 | tf_op jit(solution)/shard_map/dot_general | solution.py:101
  171.4 5.3 %convolution_convert_fusion.1 = bf16[1152,2304]{1,0:T(8,128)(2,1)} fusion(bf16[512,1152]{1,0:T(8,128)(2,1)S(1)} %gather_fusion.1, bf16[512,2304]{1,0:T(8,128)(2,1)S(1)} %get-tuple-element.6), kind=kOutput, calls=%fused_computation.8 | convolution fusion | flops 2720563200 | bytes 8847360 | tf_op jit(solution)/shard_map/dot_general | solution.py:111
  176.6 6.5 %fusion.19 = bf16[512,1152]{1,0:T(8,128)(2,1)S(1)} fusion(bf16[512,2304]{1,0:T(8,128)(2,1)} %copy-done.14, bf16[1,1152,2304]{2,1,0:T(8,128)(2,1)} %param.13), kind=kOutput, calls=%fused_computation.35 | convolution fusion | flops 2718498816 | bytes 8847360 | tf_op jit(solution)/shard_map/dot_general | solution.py:126
  187.6 59.1 %all_to_all.61 = bf16[8,128,1152]{2,1,0:T(8,128)(2,1)} all-to-all(bf16[8,128,1152]{2,1,0:T(8,128)(2,1)} %bitcast.126), channel_id=1, replica_groups=mesh['slab'=4,'dev'=8] {'dev'}, dimensions={0} | all-to-all | bytes 4718592 | tf_op jit(solution)/shard_map/all_to_all | solution.py:133
  246.7 12.8 %scatter_custom_fusion.1 = f32[512,1152]{1,0:T(8,128)} fusion(s32[1024]{0:T(1024)S(1)} %bitcast.133, bf16[1024,1152]{1,0:T(8,128)(2,1)} %bitcast.127, f32[]{:T(128)} %constant.67.clone.1), kind=kCustom, calls=%fused_computation.24 | custom fusion | flops 2359296 | bytes 4718596 | tf_op jit(solution)/shard_map/scatter-add | solution.py:134
  263.7 7.8 %reduce.6 = bf16[512,1152]{1,0:T(8,128)(2,1)S(1)} reduce(bf16[512,1,1152]{2,1,0:T(2,128)(2,1)S(1)} %bitcast.128, bf16[]{:T(256)} %broadcast.253), dimensions={1}, to_apply=%bitcast.120.reduce_sub_computation | reduce | bytes 2359298
  276.5 8.6 %convolution_convert_fusion = bf16[2304,1152]{1,0:T(8,128)(2,1)} fusion(bf16[512,1152]{1,0:T(8,128)(2,1)S(1)} %copy-done.11, f32[512]{0:T(512)S(1)} %bitcast.138, f32[512,2304]{1,0:T(8,128)} %get-tuple-element.12), kind=kOutput, calls=%fused_computation.7 | convolution fusion | flops 2732949504 | bytes 11208704 | tf_op jit(solution)/shard_map/dot_general | solution.py:119
  290.9 5.0 %reshape.212 = bf16[8,64,16,72]{3,2,1,0:T(8,128)(2,1)S(1)} reshape(bf16[8,64,1152]{2,1,0:T(8,128)(2,1)} %param.15) | data formatting | bytes 2359296 | tf_op jit(solution)/shard_map/reshape | solution.py:19
  295.9 6.0 %reshape.216 = bf16[8,64,16,72]{3,2,1,0:T(8,128)(2,1)} reshape(bf16[8,64,1152]{2,1,0:T(8,128)(2,1)} %param.17) | data formatting | bytes 2359296 | tf_op jit(solution)/shard_map/reshape | solution.py:21
  306.1 4.8 %fusion.62 = (f32[64,16,8]{2,1,0:T(8,128)}, f32[64,16,8,8]{2,3,1,0:T(8,128)}) fusion(f32[64,16,8,8]{2,3,1,0:T(8,128)S(1)} %fusion.35), kind=kOutput, calls=%fused_computation.105 | output fusion | flops 262151 | bytes 557056 | tf_op jit(solution)/shard_map/sub | solution.py:28
  312.2 6.9 %bitcast_reduce_fusion = bf16[512,1152]{1,0:T(8,128)(2,1)S(1)} fusion(bf16[512,1,1152]{2,1,0:T(2,128)(2,1)S(1)} %reshape.280), kind=kLoop, calls=%fused_computation.106 | loop fusion | bytes 2359296 | tf_op jit(solution)/shard_map/all_to_all | solution.py:143
  323.0 7.3 %multiply_reduce_fusion.1 = (f32[64,16,8]{2,1,0:T(8,128)S(1)}, f32[64,16,8,8]{2,3,1,0:T(8,128)S(1)}) fusion(f32[64,16,8,8]{2,3,1,0:T(8,128)} %get-tuple-element.14, f32[64,16,8]{2,1,0:T(8,128)} %get-tuple-element.13, bf16[8,64,16,72]{3,2,1,0:T(8,128)(2,1)} %reshape.216, bf16[8,64,16,72]{3,2,1,0:T(8,128)(2,1)S(1)} %reshape.215), kind=kOutput, calls=%fused_computation.31 | convolution fusion | flops 9625600 | bytes 2949120 | tf_op jit(solution)/shard_map/fphd,gphd->phfg/dot_general | solution.py:33
  340.3 5.0 %all-to-all-start.4 = ((bf16[8,64,1152]{2,1,0:T(8,128)(2,1)}), bf16[8,64,1152]{2,1,0:T(8,128)(2,1)S(1)}, u32[]{:S(2)}, u32[]{:S(2)}) async-start(bf16[8,64,1152]{2,1,0:T(8,128)(2,1)} %convert_element_type.109), calls=%async_computation.6 | async-start | bytes 2359296 | tf_op jit(solution)/shard_map/all_to_all | solution.py:146
  352.2 22.4 %all-to-all-done.4 = bf16[8,64,1152]{2,1,0:T(8,128)(2,1)S(1)} async-done(((bf16[8,64,1152]{2,1,0:T(8,128)(2,1)}), bf16[8,64,1152]{2,1,0:T(8,128)(2,1)S(1)}, u32[]{:S(2)}, u32[]{:S(2)}) %all-to-all-start.4) | async-done | bytes 1179680 | tf_op jit(solution)/shard_map/all_to_all | solution.py:146
  379.2 4.7 %convert_bitcast_fusion = bf16[8,64,16,72]{3,0,2,1:T(8,128)(2,1)S(1)} fusion(bf16[8,64,16,72]{3,2,1,0:T(8,128)(2,1)} %copy-done.8, f32[64,16,8,8]{2,3,1,0:T(8,128)} %get-tuple-element.14, f32[64,16,8]{2,1,0:T(8,128)} %get-tuple-element.13), kind=kOutput, calls=%fused_computation.43 | convolution fusion | flops 10158080 | bytes 2654208 | tf_op jit(solution)/shard_map/phfg,fphd->gphd/dot_general | solution.py:30
  387.7 20.9 %all-to-all-done.5 = bf16[8,64,1152]{2,1,0:T(8,128)(2,1)} async-done(((bf16[8,64,1152]{2,1,0:T(8,128)(2,1)}), bf16[8,64,1152]{2,1,0:T(8,128)(2,1)}, u32[]{:S(2)}, u32[]{:S(2)}) %all-to-all-start.5) | async-done | bytes 1179680 | tf_op jit(solution)/shard_map/all_to_all | solution.py:147
  412.2 29.3 %all-to-all-done.6 = bf16[8,64,1152]{2,1,0:T(8,128)(2,1)S(1)} async-done(((bf16[8,64,1152]{2,1,0:T(8,128)(2,1)}), bf16[8,64,1152]{2,1,0:T(8,128)(2,1)S(1)}, u32[]{:S(2)}, u32[]{:S(2)}) %all-to-all-start.6) | async-done | bytes 1179680 | tf_op jit(solution)/shard_map/all_to_all | solution.py:148
  (85 shorter events, 87.6 us)
Async XLA Ops:
  7.2 7.6 %copy-start = (bf16[1,512,1152]{2,1,0:T(8,128)(2,1)S(1)}, bf16[1,512,1152]{2,1,0:T(8,128)(2,1)}, u32[]{:S(2)}) copy-start(bf16[1,512,1152]{2,1,0:T(8,128)(2,1)} %param.9) | copy-start | bytes 3538948
  14.8 5.4 %copy-start.2 = (bf16[1,512,1152]{2,1,0:T(8,128)(2,1)S(1)}, bf16[1,512,1152]{2,1,0:T(8,128)(2,1)}, u32[]{:S(2)}) copy-start(bf16[1,512,1152]{2,1,0:T(8,128)(2,1)} %param.10) | copy-start | bytes 3538948
  90.8 59.1 %all-to-all-start = ((bf16[8,128,1152]{2,1,0:T(8,128)(2,1)}), bf16[8,128,1152]{2,1,0:T(8,128)(2,1)}, u32[]{:S(2)}, u32[]{:S(2)}) async-start(bf16[8,128,1152]{2,1,0:T(8,128)(2,1)} %get-tuple-element.10), calls=%async_computation | async-start | bytes 4718592 | tf_op jit(solution)/shard_map/all_to_all | solution.py:87
  95.2 346.3 %reduce-scatter.3.cloned.1.call-start = ((), (), s32[]{:S(2)}) async-start(), calls=%async_computation.9 | async-start | bytes 6635520 | tf_op jit(solution)/shard_map/reduce_scatter | solution.py:110
  101.9 52.9 %copy-start.10 = (bf16[512,1152]{1,0:T(8,128)(2,1)}, bf16[512,1152]{1,0:T(8,128)(2,1)S(1)}, u32[]{:S(2)}) copy-start(bf16[512,1152]{1,0:T(8,128)(2,1)S(1)} %gather_fusion.3) | copy-start | bytes 3538948
  154.8 5.8 %copy-start.13 = (f32[1,1,512]{2,1,0:T(1,128)S(1)}, f32[1,1,512]{2,1,0:T(1,128)}, u32[]{:S(2)}) copy-start(f32[1,1,512]{2,1,0:T(1,128)} %param.12) | copy-start | bytes 6148
  169.9 1.4 copy-start.14
  271.5 5.0 %copy-start.11 = (bf16[512,1152]{1,0:T(8,128)(2,1)S(1)}, bf16[512,1152]{1,0:T(8,128)(2,1)}, u32[]{:S(2)}) copy-start(bf16[512,1152]{1,0:T(8,128)(2,1)} %copy-done.10) | copy-start | bytes 3538948
  272.7 38.1 %all-to-all-start.3 = ((bf16[8,2,36864]{2,1,0:T(2,128)(2,1)}), bf16[8,2,36864]{2,1,0:T(2,128)(2,1)S(1)}, u32[]{:S(2)}, u32[]{:S(2)}) async-start(bf16[8,2,36864]{2,1,0:T(2,128)(2,1)} %reshape.279), calls=%async_computation.5 | async-start | bytes 2359296 | tf_op jit(solution)/shard_map/all_to_all | solution.py:143
  276.3 168.3 %reduce-scatter.5.cloned.1.call-start = ((), (), s32[]{:S(2)}) async-start(), calls=%async_computation.10 | async-start | bytes 6635520 | tf_op jit(solution)/shard_map/reduce_scatter | solution.py:118
  285.0 1.3 copy-start.9
  295.9 10.1 %copy-start.3 = (bf16[8,64,16,72]{3,2,1,0:T(8,128)(2,1)}, bf16[8,64,16,72]{3,2,1,0:T(8,128)(2,1)S(1)}, u32[]{:S(2)}) copy-start(bf16[8,64,16,72]{3,2,1,0:T(8,128)(2,1)S(1)} %reshape.212) | copy-start | bytes 3538948
  323.0 7.3 %copy-start.8 = (bf16[8,64,16,72]{3,2,1,0:T(8,128)(2,1)}, bf16[8,64,16,72]{3,2,1,0:T(8,128)(2,1)S(1)}, u32[]{:S(2)}) copy-start(bf16[8,64,16,72]{3,2,1,0:T(8,128)(2,1)S(1)} %reshape.215) | copy-start | bytes 3538948
  323.0 7.3 %copy-start.7 = (f32[64,16,8,8]{2,3,1,0:T(8,128)S(1)}, f32[64,16,8,8]{2,3,1,0:T(8,128)}, u32[]{:S(2)}) copy-start(f32[64,16,8,8]{2,3,1,0:T(8,128)} %get-tuple-element.14) | copy-start | bytes 786436
  323.0 7.3 %copy-start.12 = (f32[64,16,8]{2,1,0:T(8,128)S(1)}, f32[64,16,8]{2,1,0:T(8,128)}, u32[]{:S(2)}) copy-start(f32[64,16,8]{2,1,0:T(8,128)} %get-tuple-element.13) | copy-start | bytes 98308
  330.4 1.9 copy-start.4
  340.3 34.4 %all-to-all-start.4 = ((bf16[8,64,1152]{2,1,0:T(8,128)(2,1)}), bf16[8,64,1152]{2,1,0:T(8,128)(2,1)S(1)}, u32[]{:S(2)}, u32[]{:S(2)}) async-start(bf16[8,64,1152]{2,1,0:T(8,128)(2,1)} %convert_element_type.109), calls=%async_computation.6 | async-start | bytes 2359296 | tf_op jit(solution)/shard_map/all_to_all | solution.py:146
  374.7 9.3 %copy-start.5 = (bf16[8,64,1152]{2,1,0:T(8,128)(2,1)}, bf16[8,64,1152]{2,1,0:T(8,128)(2,1)S(1)}, u32[]{:S(2)}) copy-start(bf16[8,64,1152]{2,1,0:T(8,128)(2,1)S(1)} %all-to-all-done.4) | copy-start | bytes 3538948
  374.7 34.0 %all-to-all-start.5 = ((bf16[8,64,1152]{2,1,0:T(8,128)(2,1)}), bf16[8,64,1152]{2,1,0:T(8,128)(2,1)}, u32[]{:S(2)}, u32[]{:S(2)}) async-start(bf16[8,64,1152]{2,1,0:T(8,128)(2,1)} %convert_element_type.112), calls=%async_computation.7 | async-start | bytes 2359296 | tf_op jit(solution)/shard_map/all_to_all | solution.py:147
  408.6 32.9 %all-to-all-start.6 = ((bf16[8,64,1152]{2,1,0:T(8,128)(2,1)}), bf16[8,64,1152]{2,1,0:T(8,128)(2,1)S(1)}, u32[]{:S(2)}, u32[]{:S(2)}) async-start(bf16[8,64,1152]{2,1,0:T(8,128)(2,1)} %convert_element_type.116), calls=%async_computation.8 | async-start | bytes 2359296 | tf_op jit(solution)/shard_map/all_to_all | solution.py:148
  444.5 3.1 copy-start.6
  447.6 4.4 copy-start.1
Sparse Core Ops, SparseCore 0:
  176.8 60.8 reduce-scatter.2
  285.2 63.2 reduce-scatter.4
where the time goes:
time: 463 us; the launch traced here: 459 us
  waiting for transfers between devices  121 us (26%)
  blocking collectives  120 us (26%)
  local copies, waits for them, and re-layouts  78.1 us (17%)
  matrix products  56.6 us (12%)
  other arithmetic  47.7 us (10%)
  starting transfers between devices  21.5 us (5%)
  between operations  14.9 us (3%)
    all_to_all x1, blocking collectives, body(): lax.all_to_all(grad_send, 'dev', split_axis=0, concat_axis=0, tiled=True)  60.9 us
    all_to_all x1, blocking collectives, body(): lax.all_to_all(return_send, 'dev', split_axis=0, concat_axis=0, tiled=True)  59.1 us
    all_to_all x1, waiting for transfers between devices, body(): lax.all_to_all(input_send, 'dev', split_axis=0, concat_axis=0, tiled=True)  47.9 us
    all_to_all x1, waiting for transfers between devices, body(): lax.all_to_all(value_grad, 'dev', split_axis=0, concat_axis=1, tiled=True)  29.3 us
    all_to_all x1, waiting for transfers between devices, body(): lax.all_to_all(query_grad, 'dev', split_axis=0, concat_axis=1, tiled=True)  22.4 us
    all_to_all x1, waiting for transfers between devices, body(): lax.all_to_all(key_grad, 'dev', split_axis=0, concat_axis=1, tiled=True)  20.9 us
    scatter-add x1, other arithmetic, body(): jax.ops.segment_sum(returned.reshape(-1, model_width).astype(jnp.float32)...  12.8 us
    unnamed x36, local copies, waits for them, and re-layouts  10.6 us
  transfers between devices with their start and end apart: 7, of which 4 were waited for; matrix products, arithmetic and copies ran while one was open for 27% of the time, Pallas kernels for 0%

commit v1 on v0

v1 whole, which is shorter than its diff:
```python
import functools

import jax
import jax.numpy as jnp
from jax import lax
from jax.experimental import pallas as pl
from jax.experimental.pallas import tpu as pltpu
from jax.sharding import PartitionSpec as P

HEADS = 16
LANES = 128
ROOT = 0.7978845608028654
CUBE = 0.044715
BF = jnp.bfloat16
F32 = jnp.float32
VMEM_LIMIT = 56 * 1024 * 1024

ROWS_COLS = (((1,), (0,)), ((), ()))
LAST_LAST = (((1,), (1,)), ((), ()))
FIRST_FIRST = (((0,), (0,)), ((), ()))


def dot(left, right, dims=ROWS_COLS):
    return lax.dot_general(left, right, dims, preferred_element_type=F32)


def call(kernel, out_shape, in_specs, args, out_specs, after=(), carry=None, flops=0, nbytes=0, **kwargs):
    held = list(after) if carry is None else [*after, carry]
    skip = len(args)
    aliases = {}
    if carry is not None:
        aliases = {skip + len(held) - 1: len(out_shape)}
        out_shape = [*out_shape, jax.ShapeDtypeStruct(carry.shape, carry.dtype)]
        out_specs = [*out_specs, ANY]

    def run(*refs):
        refs = [*refs[:skip], *refs[skip + len(held) :]]
        if carry is not None:
            del refs[skip + len(out_shape) - 1]
        kernel(*refs)

    return pl.pallas_call(
        run,
        out_shape=out_shape,
        in_specs=list(in_specs) + [ANY] * len(held),
        out_specs=out_specs,
        input_output_aliases=aliases,
        compiler_params=pltpu.CompilerParams(vmem_limit_bytes=VMEM_LIMIT),
        cost_estimate=pl.CostEstimate(flops=flops, bytes_accessed=nbytes, transcendentals=0),
        **kwargs,
    )(*args, *held)


ANY = pl.BlockSpec(memory_space=pl.ANY)
SMEM = pl.BlockSpec(memory_space=pltpu.SMEM)
WHOLE = pl.BlockSpec(memory_space=pltpu.VMEM)


def shape(dims, dtype=BF):
    return jax.ShapeDtypeStruct(dims, dtype)


def exchange_all(blocks, which, me, count):
    size = len(which)
    first = which[0]
    order = me ^ first
    groups = None
    if size < count:
        groups = [[g * size + j for j in range(size)] for g in range(count // size)]
    places = (order % size) ^ jnp.arange(size, dtype=jnp.int32)
    stacked = jnp.stack(blocks)[places]
    if first:
        across = [(i, i ^ first) for i in range(count)]
        stacked = lax.ppermute(stacked, "dev", across)
        places = (me % size) ^ jnp.arange(size, dtype=jnp.int32)
    got = lax.all_to_all(stacked, "dev", 0, 0, axis_index_groups=groups, tiled=True)[places]
    return [got[i] for i in range(size)]


def exchange_pairs(pairs, me, count):
    if count > 8:
        blocks = exchange_all([pair[j] for pair in pairs for j in range(2)], list(range(count)), me, count)
        mates = other_core(jnp.stack(blocks[1::2]), count)
        return [jnp.stack([block, mates[i]]) for i, block in enumerate(blocks[::2])]
    return [
        lax.ppermute(pair, "dev", [(d, d ^ (2 * i)) for d in range(count)]) if i else pair
        for i, pair in enumerate(pairs)
    ]


def other_core(array, count):
    return lax.ppermute(array, "dev", [(d, d ^ 1) for d in range(count)])


def exchange_single(blocks, first, me, count):
    which = list(range(first, first + len(blocks)))
    if count > 8:
        got = exchange_all([b[0] for b in blocks], which, me, count)
        return [(block[None], 0) for block in got]
    pairs = {k: [(d, d ^ k) for d in range(count)] for k in which}
    return [(lax.ppermute(b, "dev", pairs[k]) if k else b, 0) for b, k in zip(blocks, which)]


def arrays(got):
    return [array for array, _ in got]


def block_specs(got, block, index_map):
    return [
        pl.BlockSpec((None, *block), lambda *i, at=at: (at, *index_map(*i))) for _, at in got
    ]


def prep_kernel(count, group, slots, tok, me_ref, table_ref, gate_ref, x_ref, y_ref, *refs):
    send_refs = refs[:count]
    mine_ref, other_ref, gate_out, key_out, rank_ref = refs[count:]
    me = me_ref[0]
    cap = table_ref.shape[1]
    width = table_ref.shape[0]
    upper = lax.broadcasted_iota(jnp.int32, (cap, cap), 0) < lax.broadcasted_iota(
        jnp.int32, (cap, cap), 1
    )
    upper = upper.astype(F32).astype(BF)
    table = table_ref[...]
    slot_ids = lax.broadcasted_iota(jnp.int32, (slots, cap), 0)
    tok_ids = lax.broadcasted_iota(jnp.int32, (slots, tok), 1)

    def ranked(inside):
        rank = dot(inside.astype(F32).astype(BF), upper).astype(jnp.int32)
        return jnp.where(inside, rank, -1)

    def hits(frame, ks, out_ref):
        low = frame * tok
        rank_ref[...] = ranked((table >= low) & (table < low + tok))
        for place, k in enumerate(ks):
            row = rank_ref[pl.ds(me ^ k, 1), :]
            offset = table_ref[pl.ds(me ^ k, 1), :] - low
            found = jnp.where(row == slot_ids, (offset + 1).astype(F32), 0.0)
            column = (jnp.sum(found, axis=1, keepdims=True) - 1.0).astype(jnp.int32)
            out_ref[place * slots : (place + 1) * slots, :] = (
                (column == tok_ids).astype(F32).astype(BF)
            )

    hits(me, range(count), mine_ref)
    for half, source in enumerate((x_ref, y_ref)):
        rows = dot(mine_ref[...], source[...]).astype(BF)
        for k in range(count):
            send_refs[k][0, half * slots : (half + 1) * slots, :] = rows[
                k * slots : (k + 1) * slots
            ]
    hits(me ^ group, range(group), other_ref)

    mine_row = table_ref[pl.ds(me, 1), :]
    frames = (lax.broadcasted_iota(jnp.int32, (width, cap), 0) ^ me) * tok
    key = ranked((mine_row >= frames) & (mine_row < frames + tok))
    key_out[...] = key
    for k in range(count):
        found = jnp.where(key[k : k + 1, :] == slot_ids, gate_ref[...], 0.0)
        gate_out[k * slots : (k + 1) * slots, :] = jnp.sum(found, axis=1, keepdims=True)


def prep(me, table, gate_row, x, y, group):
    count, cap = table.shape
    tok, width = x.shape
    slots = 2 * cap // count
    return call(
        functools.partial(prep_kernel, count, group, slots, tok),
        [shape((1, 2 * slots, width))] * count
        + [
            shape((count * slots, tok)),
            shape((group * slots, tok)),
            shape((count * slots, 1), F32),
            shape((count, cap), jnp.int32),
        ],
        [SMEM, WHOLE, WHOLE, WHOLE, WHOLE],
        [me, table, gate_row, x, y],
        flops=4 * count * slots * tok * width,
        nbytes=8 * count * slots * width,
        out_specs=[WHOLE] * (count + 4),
        scratch_shapes=[pltpu.VMEM((count, cap), jnp.int32)],
        name="prep",
    )


def expert_kernel(parts, steps, gate_ref, first_ref, second_ref, *refs):
    in_refs = refs[:parts]
    outs = refs[parts:]
    row_refs = outs[:parts]
    x_all, scaled, act_ref, pre_ref, gg_ref, y_all, total = outs[parts:]
    step = pl.program_id(0)
    slots = in_refs[0].shape[0] // 2
    rows = parts * slots

    @pl.when(step == 0)
    def _():
        for k in range(parts):
            place = slice(k * slots, (k + 1) * slots)
            x_all[place, :] = in_refs[k][:slots, :]
            y_rows = in_refs[k][slots:, :]
            y_all[place, :] = y_rows
            scaled[place, :] = (gate_ref[place, :] * y_rows.astype(F32)).astype(BF)
        gg_ref[...] = jnp.zeros_like(gg_ref)
        total[...] = jnp.zeros_like(total)

    first = first_ref[...]
    second = second_ref[...]
    some = 128 if rows % 128 == 0 else rows
    for start in range(0, rows, some):
        place = slice(start, start + some)
        u = dot(x_all[place, :], first)
        back = dot(y_all[place, :], second, LAST_LAST)
        square = u * u
        t = jnp.tanh(u * (ROOT + (ROOT * CUBE) * square))
        half = 0.5 + 0.5 * t
        act = (u * half).astype(BF)
        slope = half + u * (1.0 - t * t) * (0.5 * ROOT + (1.5 * ROOT * CUBE) * square)
        act_ref[place, :] = act
        gg_ref[place, :] += jnp.sum(act.astype(F32) * back, axis=1, keepdims=True)
        pre = (gate_ref[place, :] * back * slope).astype(BF)
        pre_ref[place, :] = pre
        total[place, :] += dot(pre, first, LAST_LAST)

    @pl.when(step == steps - 1)
    def _():
        for k in range(parts):
            row_refs[k][0] = total[k * slots : (k + 1) * slots, :].astype(BF)


def expert(blocks, gates, weight_in, weight_out, after=()):
    parts = len(blocks)
    _, slots, width = blocks[0][0].shape
    slots //= 2
    rows = parts * slots
    hidden = weight_in.shape[1]
    tile = 768 if hidden % 768 == 0 else hidden
    steps = hidden // tile
    fixed = lambda dims: pl.BlockSpec(dims, lambda i: (0, 0))
    outs = call(
        functools.partial(expert_kernel, parts, steps),
        [shape((1, slots, width))] * parts
        + [
            shape((rows, width)),
            shape((rows, width)),
            shape((rows, hidden)),
            shape((rows, hidden)),
            shape((rows, 1), F32),
        ],
        [
            fixed((rows, 1)),
            pl.BlockSpec((width, tile), lambda i: (0, i)),
            pl.BlockSpec((tile, width), lambda i: (i, 0)),
        ]
        + block_specs(blocks, (2 * slots, width), lambda i: (0, 0)),
        [gates, weight_in, weight_out, *arrays(blocks)],
        flops=6 * rows * width * hidden,
        nbytes=4 * width * hidden + 4 * rows * hidden + 8 * rows * width,
        after=after,
        grid=(steps,),
        out_specs=[pl.BlockSpec((1, slots, width), lambda i: (0, 0, 0))] * parts
        + [
            fixed((rows, width)),
            fixed((rows, width)),
            pl.BlockSpec((rows, tile), lambda i: (0, i)),
            pl.BlockSpec((rows, tile), lambda i: (0, i)),
            fixed((rows, 1)),
        ],
        scratch_shapes=[pltpu.VMEM((rows, width), BF), pltpu.VMEM((rows, width), F32)],
        name="expert",
    )
    return outs[:parts], outs[parts:]


def weight_kernel(turn, near_left, near_right, far_left, far_right, out_ref):
    left, right = (near_left, far_left), (near_right, far_right)
    value = sum(dot(a[...], b[...], FIRST_FIRST) for a, b in zip(left, right))
    out_ref[...] = value.astype(BF)


def weight_gradient(near, far, hidden_first, after=()):
    width, hidden = near[0].shape[1], near[1].shape[1]
    tile = 768 if hidden % 768 == 0 else hidden
    args, specs = [], []
    for rows, units in (near, far):
        all_rows = pl.BlockSpec(rows.shape, lambda i: (0, 0))
        some = pl.BlockSpec((units.shape[0], tile), lambda i: (0, i))
        args += [units, rows] if hidden_first else [rows, units]
        specs += [some, all_rows] if hidden_first else [all_rows, some]
    out, out_spec = (width, hidden), pl.BlockSpec((width, tile), lambda i: (0, i))
    if hidden_first:
        out, out_spec = (hidden, width), pl.BlockSpec((tile, width), lambda i: (i, 0))
    return call(
        functools.partial(weight_kernel, hidden_first),
        shape(out),
        specs,
        args,
        flops=4 * near[0].shape[0] * width * hidden,
        nbytes=2 * width * hidden,
        after=after,
        grid=(hidden // tile,),
        out_specs=out_spec,
        name="weight_gradient",
    )


def combine_kernel(count, parts, plus, me_ref, hit_ref, *refs):
    rows = jnp.concatenate([ref[...] for ref in refs[:parts]], axis=0)
    refs = refs[parts:]
    if plus:
        y_ref, refs = refs[0], refs[1:]
    outs, total = refs[: count // 2], refs[count // 2]
    total[...] = dot(hit_ref[...], rows, FIRST_FIRST)
    piece = outs[0].shape[1]
    for k in range(count):
        place = pl.ds(pl.multiple_of((me_ref[0] ^ k) * piece, piece), piece)
        value = total[place, :]
        if plus:
            value = value + y_ref[place, :].astype(F32)
        outs[k // 2][k % 2] = value.astype(BF)


def combine(me, hit, blocks, y, count, after=(), carry=None):
    parts = len(blocks)
    _, slots, width = blocks[0][0].shape
    tok = hit.shape[1]
    plus = [] if y is None else [y]
    rows = parts * slots
    return call(
        functools.partial(combine_kernel, count, parts, bool(plus)),
        [shape((2, tok // count, width))] * (count // 2),
        [SMEM, pl.BlockSpec((rows, tok), lambda i: (0, 0))]
        + block_specs(blocks, (slots, width), lambda i: (0, 0))
        + [pl.BlockSpec(b.shape, lambda i: (0, 0)) for b in plus],
        [me, hit, *arrays(blocks), *plus],
        flops=2 * rows * tok * width,
        nbytes=6 * tok * width,
        after=after,
        carry=carry,
        grid=(1,),
        out_specs=[pl.BlockSpec((2, tok // count, width), lambda i: (0, 0, 0))] * (count // 2),
        scratch_shapes=[pltpu.VMEM((tok, width), F32)],
        name="combine",
    )


def windows(width):
    size = width // HEADS
    for head in range(HEADS):
        start, stop = head * size, (head + 1) * size
        low, high = start // LANES, -(-stop // LANES)
        yield head, start, stop, low, high, slice(low * LANES, min(high * LANES, width))


def head_lanes(start, stop, window):
    lane = lax.broadcasted_iota(jnp.int32, (1, window.stop - window.start), 1) + window.start
    return (lane >= start) & (lane < stop)


def keep(held, part, inside, low, high):
    for tile in range(low, high):
        lanes = slice((tile - low) * LANES, min((tile - low + 1) * LANES, part.shape[1]))
        new = part[:, lanes]
        if held[tile] is not None:
            new = jnp.where(inside[:, lanes], new, held[tile])
        held[tile] = new


def probs_kernel(q_ref, k_ref, probs_ref, turned_ref):
    frames, patches, width = q_ref.shape
    rows = frames * patches
    scale = (width // HEADS) ** -0.5
    query = q_ref[...].reshape(rows, width)
    keys = k_ref[...].reshape(rows, width)
    same = (lax.broadcasted_iota(jnp.int32, (rows, rows), 0) % patches) == (
        lax.broadcasted_iota(jnp.int32, (rows, rows), 1) % patches
    )
    for head, start, stop, low, high, window in windows(width):
        inside = head_lanes(start, stop, window)
        q_win = jnp.where(inside, query[:, window], jnp.zeros((), BF))
        scores = jnp.where(same, dot(q_win, keys[:, window], LAST_LAST) * scale, -1e30)
        probs = jnp.exp(scores - jnp.max(scores, axis=1, keepdims=True))
        probs = probs / jnp.sum(probs, axis=1, keepdims=True)
        probs_ref[0, head] = probs
        turned_ref[0, head] = probs.T.astype(BF)


def patch_tile(frames, patches):
    return 16 if patches % 16 == 0 else patches


def probabilities(query, keys, after=()):
    frames, patches, width = query.shape
    tile = patch_tile(frames, patches)
    steps = patches // tile
    rows = frames * tile
    wide = pl.BlockSpec((frames, tile, width), lambda i: (0, i, 0))
    square = pl.BlockSpec((1, HEADS, rows, rows), lambda i: (i, 0, 0, 0))
    return call(
        probs_kernel,
        [shape((steps, HEADS, rows, rows), F32), shape((steps, HEADS, rows, rows))],
        [wide, wide],
        [query, keys],
        flops=8 * frames * patches * rows * width,
        nbytes=4 * frames * patches * width + 6 * steps * HEADS * rows * rows,
        after=after,
        grid=(steps,),
        out_specs=[square, square],
        name="probs",
    )


def meet_kernel(chips, *refs):
    near, far, out_ref = refs[:chips], refs[chips : 2 * chips], refs[2 * chips]
    for i in range(chips):
        value = near[i][...].astype(F32) + far[i ^ (chips // 2)][...].astype(F32)
        out_ref[i] = value.astype(BF)


def meet(near, far, carry):
    chips = len(near)
    _, piece, width = near[0].shape
    spec = pl.BlockSpec((None, piece, width), lambda i: (1, 0, 0))
    return call(
        functools.partial(meet_kernel, chips),
        [shape((chips, piece, width))],
        [spec] * (2 * chips),
        [*near, *far],
        nbytes=6 * chips * piece * width,
        carry=carry,
        grid=(1,),
        out_specs=[pl.BlockSpec((chips, piece, width), lambda i: (0, 0, 0))],
        name="meet",
    )


def value_kernel(count, me_ref, turned_ref, odd_ref, *refs):
    chips = count // 2
    near, far, refs = refs[:chips], refs[chips : 2 * chips], refs[2 * chips :]
    outs = refs[:count]
    grad_ref, result = refs[count:]
    me = me_ref[0]
    frames, patches, width = grad_ref.shape
    rows = frames * patches
    for i in range(chips):
        value = near[i][...].astype(F32) + far[i ^ (chips // 2)][...].astype(F32)
        grad_ref[me ^ (2 * i)] = value.astype(BF)
        grad_ref[me ^ (2 * i + 1)] = odd_ref[i]
    grad = grad_ref[...].reshape(rows, width)
    held = [None] * -(-width // LANES)
    for head, start, stop, low, high, window in windows(width):
        inside = head_lanes(start, stop, window)
        keep(held, dot(turned_ref[0, head], grad[:, window]), inside, low, high)
    for tile, value in enumerate(held):
        lanes = slice(tile * LANES, tile * LANES + value.shape[1])
        result[:, :, lanes] = value.astype(BF).reshape(frames, patches, value.shape[1])
    for k in range(count):
        outs[k][0] = result[me ^ k]


def value_gradient(me, turned, odd, near, far, count, after=()):
    _, piece, width = near[0].shape
    steps, _, rows, _ = turned.shape
    tile = piece // steps
    frames = rows // tile
    wide = pl.BlockSpec((frames, tile, width), lambda i: (0, i, 0))
    even = pl.BlockSpec((None, tile, width), lambda i: (0, i, 0))
    outs = call(
        functools.partial(value_kernel, count),
        [shape((1, piece, width))] * count + [shape((frames, piece, width))],
        [
            SMEM,
            pl.BlockSpec((1, HEADS, rows, rows), lambda i: (i, 0, 0, 0)),
            pl.BlockSpec((count // 2, tile, width), lambda i: (0, i, 0)),
        ]
        + [even] * (2 * len(near)),
        [me, turned, odd, *near, *far],
        flops=4 * frames * piece * rows * width,
        nbytes=8 * frames * piece * width,
        after=after,
        grid=(steps,),
        out_specs=[pl.BlockSpec((1, tile, width), lambda i: (0, i, 0))] * count + [wide],
        scratch_shapes=[pltpu.VMEM((frames, tile, width), BF)],
        name="value_gradient",
    )
    return outs[:count], outs[count]


def pair_kernel(count, me_ref, probs_ref, grad_ref, q_ref, k_ref, v_ref, *refs):
    outs, result = refs[:count], refs[count]
    me = me_ref[0]
    frames, patches, width = q_ref.shape
    rows = frames * patches
    scale = (width // HEADS) ** -0.5
    query, keys, values, grad = (
        ref[...].reshape(rows, width) for ref in (q_ref, k_ref, v_ref, grad_ref)
    )
    tiles = -(-width // LANES)
    held = [[None] * tiles for _ in range(2)]
    for head, start, stop, low, high, window in windows(width):
        inside = head_lanes(start, stop, window)
        g_win = jnp.where(inside, grad[:, window], jnp.zeros((), BF))
        prob_grad = dot(g_win, values[:, window], LAST_LAST)
        probs = probs_ref[0, head]
        delta = jnp.sum(probs * prob_grad, axis=1, keepdims=True)
        score_grad = (probs * (prob_grad - delta)).astype(BF)
        keep(held[0], dot(score_grad, keys[:, window]) * scale, inside, low, high)
        keep(held[1], dot(score_grad, query[:, window], FIRST_FIRST) * scale, inside, low, high)
    for which in range(2):
        for tile, value in enumerate(held[which]):
            lanes = slice(tile * LANES, tile * LANES + value.shape[1])
            value = value.astype(BF).reshape(frames, patches, value.shape[1])
            result[which, :, :, lanes] = value
    for k in range(count):
        for which in range(2):
            outs[k][0, which] = result[which, me ^ k]


def pair_gradients(me, probs, grad, query, keys, values, count, after=()):
    frames, piece, width = query.shape
    steps, _, rows, _ = probs.shape
    tile = piece // steps
    wide = pl.BlockSpec((frames, tile, width), lambda i: (0, i, 0))
    return call(
        functools.partial(pair_kernel, count),
        [shape((1, 2, piece, width))] * count,
        [SMEM, pl.BlockSpec((1, HEADS, rows, rows), lambda i: (i, 0, 0, 0))] + [wide] * 4,
        [me, probs, grad, query, keys, values],
        flops=12 * frames * piece * rows * width,
        nbytes=16 * frames * piece * width,
        after=after,
        grid=(steps,),
        out_specs=[pl.BlockSpec((1, 2, tile, width), lambda i: (0, 0, i, 0))] * count,
        scratch_shapes=[pltpu.VMEM((2, frames, tile, width), BF)],
        name="pair_gradients",
    )


def place_kernel(count, outs_count, me_ref, *refs):
    blocks, outs = refs[:count][::-1], refs[count:]
    piece = blocks[0].shape[-2]
    for k in range(count):
        place = pl.ds(pl.multiple_of((me_ref[0] ^ k) * piece, piece), piece)
        if outs_count == 1:
            outs[0][place, :] = blocks[k][...]
        else:
            for which in range(outs_count):
                outs[which][place, :] = blocks[k][which]


def place(me, blocks, after=()):
    count = len(blocks)
    dims = blocks[0][0].shape[1:]
    tok = count * dims[-2]
    outs_count = dims[0] if len(dims) == 3 else 1
    return call(
        functools.partial(place_kernel, count, outs_count),
        [shape((tok, dims[-1]))] * outs_count,
        [SMEM] + block_specs(blocks[::-1], dims, lambda i: (0,) * len(dims)),
        [me, *arrays(blocks[::-1])],
        nbytes=4 * outs_count * tok * dims[-1],
        after=after,
        grid=(1,),
        out_specs=[pl.BlockSpec((tok, dims[-1]), lambda i: (0, 0))] * outs_count,
        name="place",
    )


def body(
    layer_input,
    output_grad,
    expert_lists,
    gate_values,
    weight_in,
    weight_out,
    query_rows,
    key_rows,
    value_rows,
):
    count = lax.axis_size("dev")
    index = lax.axis_index("dev").astype(jnp.int32)
    me = index.reshape(1)
    frames_here, patches, width = layer_input.shape
    tok = frames_here * patches
    cap = expert_lists.shape[2]
    group = count // 2
    x = layer_input.reshape(tok, width)
    y = output_grad.reshape(tok, width)
    first, second = weight_in[0], weight_out[0]
    pairs = functools.partial(exchange_pairs, me=index, count=count)

    *send, hit_mine, hit_other, gates, key = prep(
        me, expert_lists[0], gate_values[0], x, y, group
    )
    slots = send[0].shape[1] // 2
    half = group * slots
    single = functools.partial(exchange_single, me=index, count=count)
    got_near = single(send[:group], 0)
    got_far = single(send[group:], group)

    probs, turned = probabilities(query_rows, key_rows, after=[hit_mine])
    rows_near, rest_near = expert(
        got_near, gates[:half], first, second, after=[turned, *arrays(got_far[: group // 2])]
    )
    back_near = single(rows_near, 0)
    send_near = combine(me, hit_mine, back_near, y, count, after=arrays(got_far[group // 2 :]))
    grad_near = pairs(send_near)
    rows_far, rest_far = expert(got_far, gates[half:], first, second, after=send_near[:1])
    back_far = single(rows_far, 0)

    x_near, scaled_near, act_near, pre_near, sums_near = rest_near
    x_far, scaled_far, act_far, pre_far, sums_far = rest_far
    crossed = grad_near[1:]
    in_term = weight_gradient((x_near, pre_near), (x_far, pre_far), False, after=crossed)
    *send_far, in_term = combine(me, hit_other, back_far, None, count, carry=in_term)
    in_share = lax.psum_scatter(in_term, "slab", scatter_dimension=0, tiled=True).astype(F32)
    grad_far = pairs(send_far)
    out_term = weight_gradient(
        (scaled_near, act_near), (scaled_far, act_far), True, after=send_far[:1]
    )
    slot_sums = jnp.concatenate([sums_near, sums_far]).reshape(count, slots, 1)
    slot_ids = jnp.arange(slots, dtype=jnp.int32)[None, :, None]
    gate_grad = jnp.sum(jnp.where(key[:, None, :] == slot_ids, slot_sums, 0.0), axis=(0, 1))

    odd, out_term = meet(grad_near, grad_far, out_term)
    out_share = lax.psum_scatter(out_term, "slab", scatter_dimension=0, tiled=True).astype(F32)
    odd = other_core(odd, count)
    value_send, grad_attn = value_gradient(me, turned, odd, grad_near, grad_far, count)
    pair_send = pair_gradients(me, probs, grad_attn, query_rows, key_rows, value_rows, count)
    (value_grad,) = place(me, single(value_send, 0), after=pair_send[:1])
    query_grad, key_grad = place(me, single(pair_send, 0))
    whole = (frames_here, patches, width)
    return (
        gate_grad.reshape(1, 1, cap),
        in_share[None],
        out_share[None],
        query_grad.reshape(whole),
        key_grad.reshape(whole),
        value_grad.reshape(whole),
    )


def solution(mesh):
    return jax.shard_map(
        body,
        mesh=mesh,
        in_specs=(
            P("dev", "slab", None),
            P("dev", "slab", None),
            P("slab", None, None),
            P("slab", "dev", None),
            P("dev", None, None),
            P("dev", None, None),
            P(None, ("slab", "dev"), None),
            P(None, ("slab", "dev"), None),
            P(None, ("slab", "dev"), None),
        ),
        out_specs=(
            P("slab", "dev", None),
            P("dev", "slab", None),
            P("dev", "slab", None),
            P("dev", "slab", None),
            P("dev", "slab", None),
            P("dev", "slab", None),
        ),
        check_vma=False,
    )
```

time: 463 us -> 327 us (0.71)
  blocking collectives: 120 us -> 0 us
  Pallas kernels: 0 us -> 114 us
  local copies, waits for them, and re-layouts: 78.1 us -> 10.7 us
  matrix products: 56.6 us -> 0 us
  starting transfers between devices: 21.5 us -> 67.4 us
  other arithmetic: 47.7 us -> 6.97 us
  waiting for transfers between devices: 121 us -> 112 us
    all_to_all x5 -> x0, waiting for transfers between devices: 121 us -> none  [the longest x1 47.9 us: body(): lax.all_to_all(input_send, 'dev', split_axis=0, concat_axis=0, tiled=True)]
    all_to_all x2 -> x0, blocking collectives: 120 us -> none  [the longest x1 60.9 us: body(): lax.all_to_all(grad_send, 'dev', split_axis=0, concat_axis=0, tiled=True)]
    pallas_call x0 -> x13, Pallas kernels: none -> 114 us  [call(): pl.pallas_call(run, out_shape=out_shape, in_specs=list(in_specs) + [ANY]...]
    ppermute x0 -> x34, waiting for transfers between devices: none -> 111 us  [the longest x27 98.5 us: exchange_single(): lax.ppermute(b, 'dev', pairs[k])]
    ppermute x0 -> x34, starting transfers between devices: none -> 67.3 us  [the longest x27 58.6 us: exchange_single(): lax.ppermute(b, 'dev', pairs[k])]
    dot_general x10 -> x0, matrix products: 56.6 us -> none  [the longest x1 9.36 us: body(): jnp.dot(input_rows, weight_first, preferred_element_type=jnp.float32)]
    all_to_all x5 -> x0, starting transfers between devices: 21 us -> none  [the longest x1 4.96 us: body(): lax.all_to_all(query_grad, 'dev', split_axis=0, concat_axis=1, tiled=True)]
    gather x4 -> x0, local copies, waits for them, and re-layouts: 20.7 us -> none  [the longest x1 5.41 us: body(): input_send = jnp.where(keep_mask, flat_input[send_index], empty_low)]
  transfers between devices with their start and end apart: 7 -> 36, of which waited for: 4 -> 16; matrix products, arithmetic and copies ran while one was open for 27% -> 2% of each run, Pallas kernels for 0% -> 31%
where the time goes in v1:
time: 327 us; the launch traced here: 326 us
  Pallas kernels  114 us (35%)
  waiting for transfers between devices  112 us (34%)
  starting transfers between devices  67.4 us (21%)
  between operations  14.3 us (4%)
  local copies, waits for them, and re-layouts  10.7 us (3%)
  other arithmetic  6.97 us (2%)
    pallas_call x13, Pallas kernels, call(): pl.pallas_call(run, out_shape=out_shape, in_specs=list(in_specs) + [ANY]...  114 us
    ppermute x27, waiting for transfers between devices, exchange_single(): lax.ppermute(b, 'dev', pairs[k])  98.5 us
    ppermute x27, starting transfers between devices, exchange_single(): lax.ppermute(b, 'dev', pairs[k])  58.6 us
    ppermute x6, waiting for transfers between devices, exchange_pairs(): lax.ppermute(pair, 'dev', [(d, d ^ 2 * i) for d in range(count)])  10.2 us
    unnamed x94, local copies, waits for them, and re-layouts  9.7 us
    ppermute x6, starting transfers between devices, exchange_pairs(): lax.ppermute(pair, 'dev', [(d, d ^ 2 * i) for d in range(count)])  8.77 us
  transfers between devices with their start and end apart: 36, of which 16 were waited for; matrix products, arithmetic and copies ran while one was open for 2% of the time, Pallas kernels for 31%

profile of v1, /device:TPU:0, one launch (start us, length us, event | category | flops | bytes accessed | tf_op | source)
XLA Modules:
  0.0 326.2 jit_solution(8996246636393135122)
XLA Ops:
  7.2 7.8 %prep.1 = (bf16[1,256,1152]{2,1,0:T(8,128)(2,1)}, bf16[1,256,1152]{2,1,0:T(8,128)(2,1)}, bf16[1,256,1152]{2,1,0:T(8,128)(2,1)}, bf16[1,256,1152]{2,1,0:T(8,128)(...) custom-call(s32[1]{0:T(128)} %bitcast.refs_0_, ...), custom_call_target="tpu_custom_call" | custom-call | flops 2415919104 | bytes 9437184 | tf_op jit(solution)/shard_map/prep/pallas_call | solution.py:42
  21.0 9.2 %probs.1 = (f32[4,16,128,128]{3,2,1,0:T(8,128)}, bf16[4,16,128,128]{3,2,1,0:T(8,128)(2,1)}) custom-call(bf16[8,64,1152]{2,1,0:T(8,128)(2,1)} %refs_3_.1, bf16[8,64,1152]{2,1,0:T(8,128)(2,1)} %refs_4_.1, bf16[1024,512]{1,0:T(8,128)(2,1)} %get-tuple-element.74.refs_2_.refs_1_), custom_call_target="tpu_custom_call" | custom-call | flops 603979776 | bytes 8650752 | tf_op jit(solution)/shard_map/probs/pallas_call | solution.py:42
  31.0 3.6 %collective-permute-start.5 = (bf16[1,256,1152]{2,1,0:T(8,128)(2,1)S(1)}, bf16[1,256,1152]{2,1,0:T(8,128)(2,1)S(1)}, u32[]{:S(2)}, u32[]{:S(2)}) collective-permute-start(bf16[1,256,1152]{2,1,0:T(8,128)(2,1)S(1)} %copy-done.36), channel_id=1, source_target_pairs={{0,6},{1,7},{2,4},{3,5},{4,2},{5,3},{6,0},{7,1},{8,14},{9,15},{10,... | collective-permute-start | bytes 1769480 | tf_op jit(solution)/shard_map/ppermute | solution.py:101
  34.7 22.7 %collective-permute-done.1.refs_5_ = bf16[1,256,1152]{2,1,0:T(8,128)(2,1)S(1)} collective-permute-done((bf16[1,256,1152]{2,1,0:T(8,128)(2,1)}, bf16[1,256,1152]{2,1,0:T(8,128)(2,1)S(1)}, u32[]{:S(2)}, u32[]{:S(2)}) %collective-permute-start.1) | collective-permute-done | bytes 589856 | tf_op jit(solution)/shard_map/ppermute | solution.py:101
  57.9 11.6 %collective-permute-done.2.refs_6_ = bf16[1,256,1152]{2,1,0:T(8,128)(2,1)S(1)} collective-permute-done((bf16[1,256,1152]{2,1,0:T(8,128)(2,1)}, bf16[1,256,1152]{2,1,0:T(8,128)(2,1)S(1)}, u32[]{:S(2)}, u32[]{:S(2)}) %collective-permute-start.2) | collective-permute-done | bytes 589856 | tf_op jit(solution)/shard_map/ppermute | solution.py:101
  71.0 22.4 %expert.2 = (bf16[1,128,1152]{2,1,0:T(8,128)(2,1)}, bf16[1,128,1152]{2,1,0:T(8,128)(2,1)}, bf16[1,128,1152]{2,1,0:T(8,128)(2,1)}, bf16[1,128,1152]{2,1,0:T(8,128...) custom-call(f32[512,1]{1,0:T(8,128)} %get-tuple-element.130.refs_0_,, ...), custom_call_target="tpu_custom_call" | custom-call | flops 8153726976 | bytes 20054016 | tf_op jit(solution)/shard_map/expert/pallas_call | solution.py:42
  93.4 28.5 %collective-permute-start.7 = (bf16[1,128,1152]{2,1,0:T(8,128)(2,1)}, bf16[1,128,1152]{2,1,0:T(8,128)(2,1)S(1)}, u32[]{:S(2)}, u32[]{:S(2)}) collective-permute-start(bf16[1,128,1152]{2,1,0:T(8,128)(2,1)} %get-tuple-element.82), channel_id=1, source_target_pairs={{0,1},{1,0},{2,3},{3,2},{4,5},{5,4},{6,7},{7,6},{8,9},{9,8},{10,11... | collective-permute-start | bytes 884744 | tf_op jit(solution)/shard_map/ppermute | solution.py:101
  123.4 8.6 %collective-permute-done.8.refs_4_ = bf16[1,128,1152]{2,1,0:T(8,128)(2,1)S(1)} collective-permute-done((bf16[1,128,1152]{2,1,0:T(8,128)(2,1)}, bf16[1,128,1152]{2,1,0:T(8,128)(2,1)S(1)}, u32[]{:S(2)}, u32[]{:S(2)}) %collective-permute-start.8) | collective-permute-done | bytes 294944 | tf_op jit(solution)/shard_map/ppermute | solution.py:101
  132.0 4.7 %collective-permute-done.9.refs_5_ = bf16[1,128,1152]{2,1,0:T(8,128)(2,1)S(1)} collective-permute-done((bf16[1,128,1152]{2,1,0:T(8,128)(2,1)}, bf16[1,128,1152]{2,1,0:T(8,128)(2,1)S(1)}, u32[]{:S(2)}, u32[]{:S(2)}) %collective-permute-start.9) | collective-permute-done | bytes 294944 | tf_op jit(solution)/shard_map/ppermute | solution.py:101
  137.5 3.8 %combine.2 = (bf16[2,64,1152]{2,1,0:T(8,128)(2,1)}, bf16[2,64,1152]{2,1,0:T(8,128)(2,1)}, bf16[2,64,1152]{2,1,0:T(8,128)(2,1)}, bf16[2,64,1152]{2,1,0:T(8,128)(2,1)}) custom-call(s32[1]{0:T(128)} %bitcast.refs_0_, bf16[1024,512]{1,0:T(8,128)(2,1)} %get-tuple-element.74.refs_2_.refs_1_, bf16[1,128,1152]{2,1,0:T(8,128)(2,1)} %get-tuple-element.81.refs_2_, ...), custom_call_target="tpu_custom_call" | custom-call | flops 603979776 | bytes 3538944 | tf_op jit(solution)/shard_map/combine/pallas_call | solution.py:42
  145.7 22.6 %expert.3 = (bf16[1,128,1152]{2,1,0:T(8,128)(2,1)}, bf16[1,128,1152]{2,1,0:T(8,128)(2,1)}, bf16[1,128,1152]{2,1,0:T(8,128)(2,1)}, bf16[1,128,1152]{2,1,0:T(8,128...) custom-call(f32[512,1]{1,0:T(8,128)} %get-tuple-element.131.refs_0_,, ...), custom_call_target="tpu_custom_call" | custom-call | flops 8153726976 | bytes 20054016 | tf_op jit(solution)/shard_map/expert/pallas_call | solution.py:42
  171.1 9.6 %weight_gradient.2.refs_6_ = bf16[1152,2304]{1,0:T(8,128)(2,1)} custom-call(bf16[512,1152]{1,0:T(8,128)(2,1)} %get-tuple-element.92.refs_0_, bf16[512,2304]{1,0:T(8,128)(2,1)} %get-tuple-element.93.refs_1_, bf16[512,1152]{1,0:T(8,128)(2,1)} %get-tuple-element.94.refs_2_, bf16[512,2304]{1,0:T(8,128)(2,1)} %get-tuple-element.95.refs_3_, ...), custom_call_target="tpu_custom_call" | custom-call | flops 5435817984 | bytes 5308416 | tf_op jit(solution)/shard_map/weight_gradient/pallas_call | solution.py:42
  180.7 3.2 collective-permute-done.12.refs_5_
  184.6 3.4 %combine.3 = (bf16[2,64,1152]{2,1,0:T(8,128)(2,1)}, bf16[2,64,1152]{2,1,0:T(8,128)(2,1)}, bf16[2,64,1152]{2,1,0:T(8,128)(2,1)}, bf16[2,64,1152]{2,1,0:T(8,128)(2,1)}, bf16[1152,2304]{1,0:T(8,128)(2,1)}) custom-call(s32[1]{0:T(128)} %bitcast.refs_0_, bf16[512,512]{1,0:T(8,128)(2,1)} %get-tuple-element.87.refs_1_, ...), custom_call_target="tpu_custom_call", output_to_operand_aliasing={{4}: (6, {})} | custom-call | flops 603979776 | bytes 3538944 | tf_op jit(solution)/shard_map/combine/pallas_call | solution.py:42
  189.9 3.1 collective-permute-start.17
  193.3 10.1 %weight_gradient.3.refs_8_ = bf16[2304,1152]{1,0:T(8,128)(2,1)} custom-call(bf16[512,2304]{1,0:T(8,128)(2,1)} %get-tuple-element.104.refs_0_, bf16[512,1152]{1,0:T(8,128)(2,1)} %get-tuple-element.105.refs_1_, bf16[512,2304]{1,0:T(8,128)(2,1)} %get-tuple-element.106.refs_2_, bf16[512,1152]{1,0:T(8,128)(2,1)} %get-tuple-element.107.refs_3_, ...), custom_call_target="tpu_custom_call" | custom-call | flops 5435817984 | bytes 5308416 | tf_op jit(solution)/shard_map/weight_gradient/pallas_call | solution.py:42
  204.0 9.6 %collective-permute-done.17.refs_6_.refs_9_ = bf16[2,64,1152]{2,1,0:T(8,128)(2,1)S(1)} collective-permute-done((bf16[2,64,1152]{2,1,0:T(8,128)(2,1)S(1)}, bf16[2,64,1152]{2,1,0:T(8,128)(2,1)S(1)}, u32[]{:S(2)}, u32[]{:S(2)}) %collective-permute-start.17) | collective-permute-done | bytes 294944 | tf_op jit(solution)/shard_map/ppermute | solution.py:86
  221.2 4.7 %value_gradient.1 = (bf16[1,64,1152]{2,1,0:T(8,128)(2,1)}, bf16[1,64,1152]{2,1,0:T(8,128)(2,1)}, bf16[1,64,1152]{2,1,0:T(8,128)(2,1)}, bf16[1,64,1152]{2,1,0:T(8...) custom-call(s32[1]{0:T(128)} %bitcast.refs_0_, ...), custom_call_target="tpu_custom_call" | custom-call | flops 301989888 | bytes 4718592 | tf_op jit(solution)/shard_map/value_gradient/pallas_call | solution.py:42
  229.5 4.4 %collective-permute-start.29 = (bf16[1,64,1152]{2,1,0:T(8,128)(2,1)}, bf16[1,64,1152]{2,1,0:T(8,128)(2,1)S(1)}, u32[]{:S(2)}, u32[]{:S(2)}) collective-permute-start(bf16[1,64,1152]{2,1,0:T(8,128)(2,1)} %get-tuple-element.124), channel_id=1, source_target_pairs={{0,5},{1,4},{2,7},{3,6},{4,1},{5,0},{6,3},{7,2},{8,13},{9,12},{10,... | collective-permute-start | bytes 442376 | tf_op jit(solution)/shard_map/ppermute | solution.py:101
  234.3 12.9 %pair_gradients.1 = (bf16[1,2,64,1152]{3,2,1,0:T(8,128)(2,1)}, bf16[1,2,64,1152]{3,2,1,0:T(8,128)(2,1)}, bf16[1,2,64,1152]{3,2,1,0:T(8,128)(2,1)}, bf16[1,2,64,1...) custom-call(s32[1]{0:T(128)} %bitcast.refs_0_, ...), custom_call_target="tpu_custom_call" | custom-call | flops 905969664 | bytes 9437184 | tf_op jit(solution)/shard_map/pair_gradients/pallas_call | solution.py:42
  251.0 14.8 %collective-permute-done.29.refs_3_ = bf16[1,64,1152]{2,1,0:T(8,128)(2,1)S(1)} collective-permute-done((bf16[1,64,1152]{2,1,0:T(8,128)(2,1)}, bf16[1,64,1152]{2,1,0:T(8,128)(2,1)S(1)}, u32[]{:S(2)}, u32[]{:S(2)}) %collective-permute-start.29) | collective-permute-done | bytes 147488 | tf_op jit(solution)/shard_map/ppermute | solution.py:101
  283.2 17.3 %collective-permute-done.22.refs_3_ = bf16[1,2,64,1152]{3,2,1,0:T(8,128)(2,1)S(1)} collective-permute-done((bf16[1,2,64,1152]{3,2,1,0:T(8,128)(2,1)}, bf16[1,2,64,1152]{3,2,1,0:T(8,128)(2,1)S(1)}, u32[]{:S(2)}, u32[]{:S(2)}) %collective-permute-start.22) | collective-permute-done | bytes 294944 | tf_op jit(solution)/shard_map/ppermute | solution.py:101
  300.5 6.3 %collective-permute-done.23.refs_4_ = bf16[1,2,64,1152]{3,2,1,0:T(8,128)(2,1)S(1)} collective-permute-done((bf16[1,2,64,1152]{3,2,1,0:T(8,128)(2,1)}, bf16[1,2,64,1152]{3,2,1,0:T(8,128)(2,1)S(1)}, u32[]{:S(2)}, u32[]{:S(2)}) %collective-permute-start.23) | collective-permute-done | bytes 294944 | tf_op jit(solution)/shard_map/ppermute | solution.py:101
  308.5 3.2 place.2
  (164 shorter events, 63.6 us)
Async XLA Ops:
  7.2 304.6 %reduce-scatter.3.cloned.1.call-start = ((), (), s32[]{:S(2)}) async-start(), calls=%async_computation.2 | async-start | bytes 6635520 | tf_op jit(solution)/shard_map/reduce_scatter | solution.py:614
  15.5 41.9 %collective-permute-start.1 = (bf16[1,256,1152]{2,1,0:T(8,128)(2,1)}, bf16[1,256,1152]{2,1,0:T(8,128)(2,1)S(1)}, u32[]{:S(2)}, u32[]{:S(2)}) collective-permute-start(bf16[1,256,1152]{2,1,0:T(8,128)(2,1)} %get-tuple-element.72), channel_id=1, source_target_pairs={{0,2},{1,3},{2,0},{3,1},{4,6},{5,7},{6,4},{7,5},{8,10},{9,11},{10,... | collective-permute-start | bytes 1769480 | tf_op jit(solution)/shard_map/ppermute | solution.py:101
  18.2 51.3 %collective-permute-start.2 = (bf16[1,256,1152]{2,1,0:T(8,128)(2,1)}, bf16[1,256,1152]{2,1,0:T(8,128)(2,1)S(1)}, u32[]{:S(2)}, u32[]{:S(2)}) collective-permute-start(bf16[1,256,1152]{2,1,0:T(8,128)(2,1)} %get-tuple-element.73), channel_id=1, source_target_pairs={{0,3},{1,2},{2,1},{3,0},{4,7},{5,6},{6,5},{7,4},{8,11},{9,10},{10,... | collective-permute-start | bytes 1769480 | tf_op jit(solution)/shard_map/ppermute | solution.py:101
  18.3 51.3 %collective-permute-start.3 = (bf16[1,256,1152]{2,1,0:T(8,128)(2,1)}, bf16[1,256,1152]{2,1,0:T(8,128)(2,1)S(1)}, u32[]{:S(2)}, u32[]{:S(2)}) collective-permute-start(bf16[1,256,1152]{2,1,0:T(8,128)(2,1)} %get-tuple-element.76), channel_id=1, source_target_pairs={{0,4},{1,5},{2,6},{3,7},{4,0},{5,1},{6,2},{7,3},{8,12},{9,13},{10,... | collective-permute-start | bytes 1769480 | tf_op jit(solution)/shard_map/ppermute | solution.py:101
  21.0 49.1 %collective-permute-start.4 = (bf16[1,256,1152]{2,1,0:T(8,128)(2,1)}, bf16[1,256,1152]{2,1,0:T(8,128)(2,1)S(1)}, u32[]{:S(2)}, u32[]{:S(2)}) collective-permute-start(bf16[1,256,1152]{2,1,0:T(8,128)(2,1)} %get-tuple-element.77), channel_id=1, source_target_pairs={{0,5},{1,4},{2,7},{3,6},{4,1},{5,0},{6,3},{7,2},{8,13},{9,12},{10,... | collective-permute-start | bytes 1769480 | tf_op jit(solution)/shard_map/ppermute | solution.py:101
  31.0 92.4 %collective-permute-start.5 = (bf16[1,256,1152]{2,1,0:T(8,128)(2,1)S(1)}, bf16[1,256,1152]{2,1,0:T(8,128)(2,1)S(1)}, u32[]{:S(2)}, u32[]{:S(2)}) collective-permute-start(bf16[1,256,1152]{2,1,0:T(8,128)(2,1)S(1)} %copy-done.36), channel_id=1, source_target_pairs={{0,6},{1,7},{2,4},{3,5},{4,2},{5,3},{6,0},{7,1},{8,14},{9,15},{10,... | collective-permute-start | bytes 1769480 | tf_op jit(solution)/shard_map/ppermute | solution.py:101
  57.4 66.0 %collective-permute-start.6 = (bf16[1,256,1152]{2,1,0:T(8,128)(2,1)S(1)}, bf16[1,256,1152]{2,1,0:T(8,128)(2,1)S(1)}, u32[]{:S(2)}, u32[]{:S(2)}) collective-permute-start(bf16[1,256,1152]{2,1,0:T(8,128)(2,1)S(1)} %copy-done.35), channel_id=1, source_target_pairs={{0,7},{1,6},{2,5},{3,4},{4,3},{5,2},{6,1},{7,0},{8,15},{9,14},{10,... | collective-permute-start | bytes 1769480 | tf_op jit(solution)/shard_map/ppermute | solution.py:101
  93.4 30.0 %collective-permute-start.7 = (bf16[1,128,1152]{2,1,0:T(8,128)(2,1)}, bf16[1,128,1152]{2,1,0:T(8,128)(2,1)S(1)}, u32[]{:S(2)}, u32[]{:S(2)}) collective-permute-start(bf16[1,128,1152]{2,1,0:T(8,128)(2,1)} %get-tuple-element.82), channel_id=1, source_target_pairs={{0,1},{1,0},{2,3},{3,2},{4,5},{5,4},{6,7},{7,6},{8,9},{9,8},{10,11... | collective-permute-start | bytes 884744 | tf_op jit(solution)/shard_map/ppermute | solution.py:101
  141.3 28.2 %collective-permute-start.13 = (bf16[2,64,1152]{2,1,0:T(8,128)(2,1)}, bf16[2,64,1152]{2,1,0:T(8,128)(2,1)S(1)}, u32[]{:S(2)}, u32[]{:S(2)}) collective-permute-start(bf16[2,64,1152]{2,1,0:T(8,128)(2,1)} %get-tuple-element.96), channel_id=1, source_target_pairs={{0,2},{1,3},{2,0},{3,1},{4,6},{5,7},{6,4},{7,5},{8,10},{9,11},{10,... | collective-permute-start | bytes 884744 | tf_op jit(solution)/shard_map/ppermute | solution.py:86
  143.2 27.1 %collective-permute-start.14 = (bf16[2,64,1152]{2,1,0:T(8,128)(2,1)}, bf16[2,64,1152]{2,1,0:T(8,128)(2,1)S(1)}, u32[]{:S(2)}, u32[]{:S(2)}) collective-permute-start(bf16[2,64,1152]{2,1,0:T(8,128)(2,1)} %get-tuple-element.97), channel_id=1, source_target_pairs={{0,4},{1,5},{2,6},{3,7},{4,0},{5,1},{6,2},{7,3},{8,12},{9,13},{10,... | collective-permute-start | bytes 884744 | tf_op jit(solution)/shard_map/ppermute | solution.py:86
  145.4 24.8 %collective-permute-start.15 = (bf16[2,64,1152]{2,1,0:T(8,128)(2,1)}, bf16[2,64,1152]{2,1,0:T(8,128)(2,1)S(1)}, u32[]{:S(2)}, u32[]{:S(2)}) collective-permute-start(bf16[2,64,1152]{2,1,0:T(8,128)(2,1)} %get-tuple-element.98), channel_id=1, source_target_pairs={{0,6},{1,7},{2,4},{3,5},{4,2},{5,3},{6,0},{7,1},{8,14},{9,15},{10,... | collective-permute-start | bytes 884744 | tf_op jit(solution)/shard_map/ppermute | solution.py:86
  188.0 128.4 %reduce-scatter.5.cloned.1.call-start = ((), (), s32[]{:S(2)}) async-start(), calls=%async_computation.3 | async-start | bytes 6635520 | tf_op jit(solution)/shard_map/reduce_scatter | solution.py:624
  189.9 23.6 %collective-permute-start.17 = (bf16[2,64,1152]{2,1,0:T(8,128)(2,1)S(1)}, bf16[2,64,1152]{2,1,0:T(8,128)(2,1)S(1)}, u32[]{:S(2)}, u32[]{:S(2)}) collective-permute-start(bf16[2,64,1152]{2,1,0:T(8,128)(2,1)S(1)} %copy-done.42), channel_id=1, source_target_pairs={{0,4},{1,5},{2,6},{3,7},{4,0},{5,1},{6,2},{7,3},{8,12},{9,13},{10,... | collective-permute-start | bytes 884744 | tf_op jit(solution)/shard_map/ppermute | solution.py:86
  225.9 22.8 %collective-permute-start.27 = (bf16[1,64,1152]{2,1,0:T(8,128)(2,1)}, bf16[1,64,1152]{2,1,0:T(8,128)(2,1)S(1)}, u32[]{:S(2)}, u32[]{:S(2)}) collective-permute-start(bf16[1,64,1152]{2,1,0:T(8,128)(2,1)} %get-tuple-element.122), channel_id=1, source_target_pairs={{0,7},{1,6},{2,5},{3,4},{4,3},{5,2},{6,1},{7,0},{8,15},{9,14},{10,... | collective-permute-start | bytes 442376 | tf_op jit(solution)/shard_map/ppermute | solution.py:101
  228.6 22.4 %collective-permute-start.28 = (bf16[1,64,1152]{2,1,0:T(8,128)(2,1)}, bf16[1,64,1152]{2,1,0:T(8,128)(2,1)S(1)}, u32[]{:S(2)}, u32[]{:S(2)}) collective-permute-start(bf16[1,64,1152]{2,1,0:T(8,128)(2,1)} %get-tuple-element.123), channel_id=1, source_target_pairs={{0,6},{1,7},{2,4},{3,5},{4,2},{5,3},{6,0},{7,1},{8,14},{9,15},{10,... | collective-permute-start | bytes 442376 | tf_op jit(solution)/shard_map/ppermute | solution.py:101
  229.5 36.2 %collective-permute-start.29 = (bf16[1,64,1152]{2,1,0:T(8,128)(2,1)}, bf16[1,64,1152]{2,1,0:T(8,128)(2,1)S(1)}, u32[]{:S(2)}, u32[]{:S(2)}) collective-permute-start(bf16[1,64,1152]{2,1,0:T(8,128)(2,1)} %get-tuple-element.124), channel_id=1, source_target_pairs={{0,5},{1,4},{2,7},{3,6},{4,1},{5,0},{6,3},{7,2},{8,13},{9,12},{10,... | collective-permute-start | bytes 442376 | tf_op jit(solution)/shard_map/ppermute | solution.py:101
  233.9 35.0 %collective-permute-start.30 = (bf16[1,64,1152]{2,1,0:T(8,128)(2,1)}, bf16[1,64,1152]{2,1,0:T(8,128)(2,1)S(1)}, u32[]{:S(2)}, u32[]{:S(2)}) collective-permute-start(bf16[1,64,1152]{2,1,0:T(8,128)(2,1)} %get-tuple-element.125), channel_id=1, source_target_pairs={{0,4},{1,5},{2,6},{3,7},{4,0},{5,1},{6,2},{7,3},{8,12},{9,13},{10,... | collective-permute-start | bytes 442376 | tf_op jit(solution)/shard_map/ppermute | solution.py:101
  247.3 31.5 %collective-permute-start.20 = (bf16[1,2,64,1152]{3,2,1,0:T(8,128)(2,1)}, bf16[1,2,64,1152]{3,2,1,0:T(8,128)(2,1)S(1)}, u32[]{:S(2)}, u32[]{:S(2)}) collective-permute-start(bf16[1,2,64,1152]{3,2,1,0:T(8,128)(2,1)} %get-tuple-element.112), channel_id=1, source_target_pairs={{0,7},{1,6},{2,5},{3,4},{4,3},{5,2},{6,1},{7,0},{8,15},{9,14},{10,... | collective-permute-start | bytes 884744 | tf_op jit(solution)/shard_map/ppermute | solution.py:101
  248.7 30.7 %collective-permute-start.21 = (bf16[1,2,64,1152]{3,2,1,0:T(8,128)(2,1)}, bf16[1,2,64,1152]{3,2,1,0:T(8,128)(2,1)S(1)}, u32[]{:S(2)}, u32[]{:S(2)}) collective-permute-start(bf16[1,2,64,1152]{3,2,1,0:T(8,128)(2,1)} %get-tuple-element.113), channel_id=1, source_target_pairs={{0,6},{1,7},{2,4},{3,5},{4,2},{5,3},{6,0},{7,1},{8,14},{9,15},{10,... | collective-permute-start | bytes 884744 | tf_op jit(solution)/shard_map/ppermute | solution.py:101
  272.0 28.5 %collective-permute-start.22 = (bf16[1,2,64,1152]{3,2,1,0:T(8,128)(2,1)}, bf16[1,2,64,1152]{3,2,1,0:T(8,128)(2,1)S(1)}, u32[]{:S(2)}, u32[]{:S(2)}) collective-permute-start(bf16[1,2,64,1152]{3,2,1,0:T(8,128)(2,1)} %get-tuple-element.114), channel_id=1, source_target_pairs={{0,5},{1,4},{2,7},{3,6},{4,1},{5,0},{6,3},{7,2},{8,13},{9,12},{10,... | collective-permute-start | bytes 884744 | tf_op jit(solution)/shard_map/ppermute | solution.py:101
  275.2 31.6 %collective-permute-start.23 = (bf16[1,2,64,1152]{3,2,1,0:T(8,128)(2,1)}, bf16[1,2,64,1152]{3,2,1,0:T(8,128)(2,1)S(1)}, u32[]{:S(2)}, u32[]{:S(2)}) collective-permute-start(bf16[1,2,64,1152]{3,2,1,0:T(8,128)(2,1)} %get-tuple-element.115), channel_id=1, source_target_pairs={{0,4},{1,5},{2,6},{3,7},{4,0},{5,1},{6,2},{7,3},{8,12},{9,13},{10,... | collective-permute-start | bytes 884744 | tf_op jit(solution)/shard_map/ppermute | solution.py:101
  276.8 30.0 %collective-permute-start.24 = (bf16[1,2,64,1152]{3,2,1,0:T(8,128)(2,1)}, bf16[1,2,64,1152]{3,2,1,0:T(8,128)(2,1)S(1)}, u32[]{:S(2)}, u32[]{:S(2)}) collective-permute-start(bf16[1,2,64,1152]{3,2,1,0:T(8,128)(2,1)} %get-tuple-element.116), channel_id=1, source_target_pairs={{0,3},{1,2},{2,1},{3,0},{4,7},{5,6},{6,5},{7,4},{8,11},{9,10},{10,... | collective-permute-start | bytes 884744 | tf_op jit(solution)/shard_map/ppermute | solution.py:101
  278.8 28.0 %collective-permute-start.25 = (bf16[1,2,64,1152]{3,2,1,0:T(8,128)(2,1)}, bf16[1,2,64,1152]{3,2,1,0:T(8,128)(2,1)S(1)}, u32[]{:S(2)}, u32[]{:S(2)}) collective-permute-start(bf16[1,2,64,1152]{3,2,1,0:T(8,128)(2,1)} %get-tuple-element.117), channel_id=1, source_target_pairs={{0,2},{1,3},{2,0},{3,1},{4,6},{5,7},{6,4},{7,5},{8,10},{9,11},{10,... | collective-permute-start | bytes 884744 | tf_op jit(solution)/shard_map/ppermute | solution.py:101
  279.4 27.5 %collective-permute-start.26 = (bf16[1,2,64,1152]{3,2,1,0:T(8,128)(2,1)}, bf16[1,2,64,1152]{3,2,1,0:T(8,128)(2,1)S(1)}, u32[]{:S(2)}, u32[]{:S(2)}) collective-permute-start(bf16[1,2,64,1152]{3,2,1,0:T(8,128)(2,1)} %get-tuple-element.118), channel_id=1, source_target_pairs={{0,1},{1,0},{2,3},{3,2},{4,5},{5,4},{6,7},{7,6},{8,9},{9,8},{10,11... | collective-permute-start | bytes 884744 | tf_op jit(solution)/shard_map/ppermute | solution.py:101
  (59 other events, 733.4 us)
Sparse Core Ops, SparseCore 0:
  188.1 63.2 reduce-scatter.2
  254.4 61.9 reduce-scatter.4

commit v2 on v1

--- a/solution.py
+++ b/solution.py
@@ -99,6 +99,13 @@
         return [(block[None], 0) for block in got]
     pairs = {k: [(d, d ^ k) for d in range(count)] for k in which}
     return [(lax.ppermute(b, "dev", pairs[k]) if k else b, 0) for b, k in zip(blocks, which)]
+
+
+def exchange_apart(block, k, count):
+    pairs = [(d, d ^ k) for d in range(count)]
+    far = [(d, e) for d, e in pairs if abs(d - e) > count // 2]
+    near = [(d, e) for d, e in pairs if abs(d - e) <= count // 2]
+    return lax.ppermute(block, "dev", far), lax.ppermute(block, "dev", near)
 
 
 def arrays(got):
@@ -182,21 +189,24 @@
     )
 
 
-def expert_kernel(parts, steps, gate_ref, first_ref, second_ref, *refs):
+def expert_kernel(parts, steps, apart, gate_ref, first_ref, second_ref, *refs):
     in_refs = refs[:parts]
-    outs = refs[parts:]
+    more_refs = dict(zip(apart, refs[parts:]))
+    outs = refs[parts + len(apart) :]
     row_refs = outs[:parts]
     x_all, scaled, act_ref, pre_ref, gg_ref, y_all, total = outs[parts:]
     step = pl.program_id(0)
     slots = in_refs[0].shape[0] // 2
-    rows = parts * slots
 
     @pl.when(step == 0)
     def _():
         for k in range(parts):
             place = slice(k * slots, (k + 1) * slots)
-            x_all[place, :] = in_refs[k][:slots, :]
-            y_rows = in_refs[k][slots:, :]
+            value = in_refs[k][...]
+            if k in more_refs:
+                value = value + more_refs[k][...]
+            x_all[place, :] = value[:slots, :]
+            y_rows = value[slots:, :]
             y_all[place, :] = y_rows
             scaled[place, :] = (gate_ref[place, :] * y_rows.astype(F32)).astype(BF)
         gg_ref[...] = jnp.zeros_like(gg_ref)
@@ -204,21 +214,18 @@
 
     first = first_ref[...]
     second = second_ref[...]
-    some = 128 if rows % 128 == 0 else rows
-    for start in range(0, rows, some):
-        place = slice(start, start + some)
-        u = dot(x_all[place, :], first)
-        back = dot(y_all[place, :], second, LAST_LAST)
-        square = u * u
-        t = jnp.tanh(u * (ROOT + (ROOT * CUBE) * square))
-        half = 0.5 + 0.5 * t
-        act = (u * half).astype(BF)
-        slope = half + u * (1.0 - t * t) * (0.5 * ROOT + (1.5 * ROOT * CUBE) * square)
-        act_ref[place, :] = act
-        gg_ref[place, :] += jnp.sum(act.astype(F32) * back, axis=1, keepdims=True)
-        pre = (gate_ref[place, :] * back * slope).astype(BF)
-        pre_ref[place, :] = pre
-        total[place, :] += dot(pre, first, LAST_LAST)
+    u = dot(x_all[...], first)
+    back = dot(y_all[...], second, LAST_LAST)
+    square = u * u
+    t = jnp.tanh(u * (ROOT + (ROOT * CUBE) * square))
+    half = 0.5 + 0.5 * t
+    act = (u * half).astype(BF)
+    slope = half + u * (1.0 - t * t) * (0.5 * ROOT + (1.5 * ROOT * CUBE) * square)
+    act_ref[...] = act
+    gg_ref[...] += jnp.sum(act.astype(F32) * back, axis=1, keepdims=True)
+    pre = (gate_ref[...] * back * slope).astype(BF)
+    pre_ref[...] = pre
+    total[...] += dot(pre, first, LAST_LAST)
 
     @pl.when(step == steps - 1)
     def _():
@@ -226,7 +233,8 @@
             row_refs[k][0] = total[k * slots : (k + 1) * slots, :].astype(BF)
 
 
-def expert(blocks, gates, weight_in, weight_out, after=()):
+def expert(blocks, gates, weight_in, weight_out, more=(), after=()):
+    more = dict(more)
     parts = len(blocks)
     _, slots, width = blocks[0][0].shape
     slots //= 2
@@ -236,7 +244,7 @@
     steps = hidden // tile
     fixed = lambda dims: pl.BlockSpec(dims, lambda i: (0, 0))
     outs = call(
-        functools.partial(expert_kernel, parts, steps),
+        functools.partial(expert_kernel, parts, steps, tuple(more)),
         [shape((1, slots, width))] * parts
         + [
             shape((rows, width)),
@@ -250,8 +258,8 @@
             pl.BlockSpec((width, tile), lambda i: (0, i)),
             pl.BlockSpec((tile, width), lambda i: (i, 0)),
         ]
-        + block_specs(blocks, (2 * slots, width), lambda i: (0, 0)),
-        [gates, weight_in, weight_out, *arrays(blocks)],
+        + block_specs([*blocks, *more.values()], (2 * slots, width), lambda i: (0, 0)),
+        [gates, weight_in, weight_out, *arrays(blocks), *arrays(more.values())],
         flops=6 * rows * width * hidden,
         nbytes=4 * width * hidden + 4 * rows * hidden + 8 * rows * width,
         after=after,
@@ -534,16 +542,22 @@
     )
 
 
-def place_kernel(count, outs_count, me_ref, *refs):
-    blocks, outs = refs[:count][::-1], refs[count:]
+def spread(count):
+    half, quarter = count // 2, count // 4
+    far = [k for i in range(quarter) for k in (half + quarter + i, half + i)]
+    return far + list(range(half - 1, -1, -1))
+
+
+def place_kernel(order, outs_count, me_ref, *refs):
+    blocks, outs = refs[: len(order)], refs[len(order) :]
     piece = blocks[0].shape[-2]
-    for k in range(count):
+    for k, block in zip(order, blocks):
         place = pl.ds(pl.multiple_of((me_ref[0] ^ k) * piece, piece), piece)
         if outs_count == 1:
-            outs[0][place, :] = blocks[k][...]
+            outs[0][place, :] = block[...]
         else:
             for which in range(outs_count):
-                outs[which][place, :] = blocks[k][which]
+                outs[which][place, :] = block[which]
 
 
 def place(me, blocks, after=()):
@@ -551,11 +565,13 @@
     dims = blocks[0][0].shape[1:]
     tok = count * dims[-2]
     outs_count = dims[0] if len(dims) == 3 else 1
+    order = spread(count)
+    blocks = [blocks[k] for k in order]
     return call(
-        functools.partial(place_kernel, count, outs_count),
+        functools.partial(place_kernel, order, outs_count),
         [shape((tok, dims[-1]))] * outs_count,
-        [SMEM] + block_specs(blocks[::-1], dims, lambda i: (0,) * len(dims)),
-        [me, *arrays(blocks[::-1])],
+        [SMEM] + block_specs(blocks, dims, lambda i: (0,) * len(dims)),
+        [me, *arrays(blocks)],
         nbytes=4 * outs_count * tok * dims[-1],
         after=after,
         grid=(1,),
@@ -595,15 +611,24 @@
     single = functools.partial(exchange_single, me=index, count=count)
     got_near = single(send[:group], 0)
     got_far = single(send[group:], group)
+    more, early = {}, got_far[::2]
+    if count == 8:
+        split = group // 2
+        away, close = exchange_apart(send[group + split], group + split, count)
+        got_far[split], more[split] = (away, 0), (close, 0)
+        early = [got_far[0], got_far[split]]
 
     probs, turned = probabilities(query_rows, key_rows, after=[hit_mine])
     rows_near, rest_near = expert(
-        got_near, gates[:half], first, second, after=[turned, *arrays(got_far[: group // 2])]
+        got_near, gates[:half], first, second, after=[turned, *arrays(early)]
     )
     back_near = single(rows_near, 0)
-    send_near = combine(me, hit_mine, back_near, y, count, after=arrays(got_far[group // 2 :]))
+    late = arrays(got_far[1::2]) + arrays(more.values())
+    send_near = combine(me, hit_mine, back_near, y, count, after=late)
     grad_near = pairs(send_near)
-    rows_far, rest_far = expert(got_far, gates[half:], first, second, after=send_near[:1])
+    rows_far, rest_far = expert(
+        got_far, gates[half:], first, second, more=more, after=send_near[:1]
+    )
     back_far = single(rows_far, 0)
 
     x_near, scaled_near, act_near, pre_near, sums_near = rest_near
@@ -626,7 +651,7 @@
     value_send, grad_attn = value_gradient(me, turned, odd, grad_near, grad_far, count)
     pair_send = pair_gradients(me, probs, grad_attn, query_rows, key_rows, value_rows, count)
     (value_grad,) = place(me, single(value_send, 0), after=pair_send[:1])
-    query_grad, key_grad = place(me, single(pair_send, 0))
+    query_grad, key_grad = place(me, single(pair_send, 0), after=[in_share])
     whole = (frames_here, patches, width)
     return (
         gate_grad.reshape(1, 1, cap),

time: 327 us -> 310 us (0.948)
  waiting for transfers between devices: 112 us -> 91.7 us
  starting transfers between devices: 67.4 us -> 84.6 us
  Pallas kernels: 114 us -> 102 us
    ppermute x27 -> x26, waiting for transfers between devices: 98.5 us -> 72.8 us  [exchange_single(): lax.ppermute(b, 'dev', pairs[k])]
    pallas_call x13, Pallas kernels: 114 us -> 102 us  [call(): pl.pallas_call(run, out_shape=out_shape, in_specs=list(in_specs) + [ANY]...]
    ppermute x27 -> x26, starting transfers between devices: 58.6 us -> 66.9 us  [exchange_single(): lax.ppermute(b, 'dev', pairs[k])]
    ppermute x6, starting transfers between devices: 8.77 us -> 13.2 us  [exchange_pairs(): lax.ppermute(pair, 'dev', [(d, d ^ 2 * i) for d in range(count)])]
    convert_element_type x0 -> x1, other arithmetic: none -> 4.13 us  [body(): lax.psum_scatter(in_term, 'slab', scatter_dimension=0, tiled=True)]
    ppermute x0 -> x2, starting transfers between devices: none -> 4.13 us  [exchange_apart(): return (lax.ppermute(block, 'dev', far), lax.ppermute(block, 'dev', near))]
    ppermute x6, waiting for transfers between devices: 10.2 us -> 13.5 us  [exchange_pairs(): lax.ppermute(pair, 'dev', [(d, d ^ 2 * i) for d in range(count)])]
    unnamed x94 -> x102, local copies, waits for them, and re-layouts: 9.7 us -> 8.27 us
  transfers between devices with their start and end apart: 36 -> 37, of which waited for: 16 -> 14; matrix products, arithmetic and copies ran while one was open for 2% -> 2% of each run, Pallas kernels for 31% -> 28%
where the time goes in v2:
time: 310 us
  Pallas kernels  102 us (33%)
  waiting for transfers between devices  91.7 us (30%)
  starting transfers between devices  84.6 us (27%)
  between operations  14.5 us (5%)
  local copies, waits for them, and re-layouts  9.34 us (3%)
  other arithmetic  8.08 us (3%)
    pallas_call x13, Pallas kernels, call(): pl.pallas_call(run, out_shape=out_shape, in_specs=list(in_specs) + [ANY]...  102 us
    ppermute x26, waiting for transfers between devices, exchange_single(): lax.ppermute(b, 'dev', pairs[k])  72.8 us
    ppermute x26, starting transfers between devices, exchange_single(): lax.ppermute(b, 'dev', pairs[k])  66.9 us
    ppermute x6, waiting for transfers between devices, exchange_pairs(): lax.ppermute(pair, 'dev', [(d, d ^ 2 * i) for d in range(count)])  13.5 us
    ppermute x6, starting transfers between devices, exchange_pairs(): lax.ppermute(pair, 'dev', [(d, d ^ 2 * i) for d in range(count)])  13.2 us
    unnamed x102, local copies, waits for them, and re-layouts  8.27 us
  transfers between devices with their start and end apart: 37, of which 14 were waited for; matrix products, arithmetic and copies ran while one was open for 2% of the time, Pallas kernels for 28%

profile of v2, /device:TPU:0, one launch (start us, length us, event | category | flops | bytes accessed | tf_op | source)
XLA Modules:
  0.0 309.9 jit_solution(12449388623145989719)
XLA Ops:
  7.2 7.8 %prep.1 = (bf16[1,256,1152]{2,1,0:T(8,128)(2,1)}, bf16[1,256,1152]{2,1,0:T(8,128)(2,1)}, bf16[1,256,1152]{2,1,0:T(8,128)(2,1)}, bf16[1,256,1152]{2,1,0:T(8,128)(...) custom-call(s32[1]{0:T(128)} %bitcast.refs_0_, ...), custom_call_target="tpu_custom_call" | custom-call | flops 2415919104 | bytes 9437184 | tf_op jit(solution)/shard_map/prep/pallas_call | solution.py:42
  24.3 9.2 %probs.1 = (f32[4,16,128,128]{3,2,1,0:T(8,128)}, bf16[4,16,128,128]{3,2,1,0:T(8,128)(2,1)}) custom-call(bf16[8,64,1152]{2,1,0:T(8,128)(2,1)} %refs_3_.1, bf16[8,64,1152]{2,1,0:T(8,128)(2,1)} %refs_4_.1, bf16[1024,512]{1,0:T(8,128)(2,1)} %get-tuple-element.74.refs_2_.refs_1_), custom_call_target="tpu_custom_call" | custom-call | flops 603979776 | bytes 8650752 | tf_op jit(solution)/shard_map/probs/pallas_call | solution.py:42
  35.2 10.0 %collective-permute-done.1.refs_5_ = bf16[1,256,1152]{2,1,0:T(8,128)(2,1)S(1)} collective-permute-done((bf16[1,256,1152]{2,1,0:T(8,128)(2,1)}, bf16[1,256,1152]{2,1,0:T(8,128)(2,1)S(1)}, u32[]{:S(2)}, u32[]{:S(2)}) %collective-permute-start.1) | collective-permute-done | bytes 589856 | tf_op jit(solution)/shard_map/ppermute | solution.py:101
  46.2 11.1 %collective-permute-done.2.refs_6_ = bf16[1,256,1152]{2,1,0:T(8,128)(2,1)S(1)} collective-permute-done((bf16[1,256,1152]{2,1,0:T(8,128)(2,1)}, bf16[1,256,1152]{2,1,0:T(8,128)(2,1)S(1)}, u32[]{:S(2)}, u32[]{:S(2)}) %collective-permute-start.2) | collective-permute-done | bytes 589856 | tf_op jit(solution)/shard_map/ppermute | solution.py:101
  57.3 16.0 %collective-permute-start.6 = (bf16[1,256,1152]{2,1,0:T(8,128)(2,1)S(1)}, bf16[1,256,1152]{2,1,0:T(8,128)(2,1)S(1)}, u32[]{:S(2)}, u32[]{:S(2)}) collective-permute-start(bf16[1,256,1152]{2,1,0:T(8,128)(2,1)S(1)} %copy-done.37), channel_id=1, source_target_pairs={{0,7},{1,6},{2,5},{3,4},{4,3},{5,2},{6,1},{7,0},{8,15},{9,14},{10,... | collective-permute-start | bytes 1769480 | tf_op jit(solution)/shard_map/ppermute | solution.py:101
  74.4 15.7 %expert.2 = (bf16[1,128,1152]{2,1,0:T(8,128)(2,1)}, bf16[1,128,1152]{2,1,0:T(8,128)(2,1)}, bf16[1,128,1152]{2,1,0:T(8,128)(2,1)}, bf16[1,128,1152]{2,1,0:T(8,128...) custom-call(f32[512,1]{1,0:T(8,128)} %get-tuple-element.132.refs_0_,, ...), custom_call_target="tpu_custom_call" | custom-call | flops 8153726976 | bytes 20054016 | tf_op jit(solution)/shard_map/expert/pallas_call | solution.py:42
  90.3 22.1 %collective-permute-done.5.refs_7_.refs_4_ = bf16[1,256,1152]{2,1,0:T(8,128)(2,1)S(1)} collective-permute-done((bf16[1,256,1152]{2,1,0:T(8,128)(2,1)S(1)}, bf16[1,256,1152]{2,1,0:T(8,128)(2,1)S(1)}, u32[]{:S(2)}, u32[]{:S(2)}) %collective-permute-start.5) | collective-permute-done | bytes 589856 | tf_op jit(solution)/shard_map/ppermute | solution.py:101
  112.4 4.4 %collective-permute-done.9.refs_4_ = bf16[1,128,1152]{2,1,0:T(8,128)(2,1)S(1)} collective-permute-done((bf16[1,128,1152]{2,1,0:T(8,128)(2,1)}, bf16[1,128,1152]{2,1,0:T(8,128)(2,1)S(1)}, u32[]{:S(2)}, u32[]{:S(2)}) %collective-permute-start.9) | collective-permute-done | bytes 294944 | tf_op jit(solution)/shard_map/ppermute | solution.py:101
  116.8 5.7 %collective-permute-done.10.refs_5_ = bf16[1,128,1152]{2,1,0:T(8,128)(2,1)S(1)} collective-permute-done((bf16[1,128,1152]{2,1,0:T(8,128)(2,1)}, bf16[1,128,1152]{2,1,0:T(8,128)(2,1)S(1)}, u32[]{:S(2)}, u32[]{:S(2)}) %collective-permute-start.10) | collective-permute-done | bytes 294944 | tf_op jit(solution)/shard_map/ppermute | solution.py:101
  123.2 3.8 %combine.2 = (bf16[2,64,1152]{2,1,0:T(8,128)(2,1)}, bf16[2,64,1152]{2,1,0:T(8,128)(2,1)}, bf16[2,64,1152]{2,1,0:T(8,128)(2,1)}, bf16[2,64,1152]{2,1,0:T(8,128)(2,1)}) custom-call(s32[1]{0:T(128)} %bitcast.refs_0_, bf16[1024,512]{1,0:T(8,128)(2,1)} %get-tuple-element.74.refs_2_.refs_1_, bf16[1,128,1152]{2,1,0:T(8,128)(2,1)} %get-tuple-element.81.refs_2_, ...), custom_call_target="tpu_custom_call" | custom-call | flops 603979776 | bytes 3538944 | tf_op jit(solution)/shard_map/combine/pallas_call | solution.py:42
  127.0 3.7 %collective-permute-start.14 = (bf16[2,64,1152]{2,1,0:T(8,128)(2,1)}, bf16[2,64,1152]{2,1,0:T(8,128)(2,1)S(1)}, u32[]{:S(2)}, u32[]{:S(2)}) collective-permute-start(bf16[2,64,1152]{2,1,0:T(8,128)(2,1)} %get-tuple-element.96), channel_id=1, source_target_pairs={{0,2},{1,3},{2,0},{3,1},{4,6},{5,7},{6,4},{7,5},{8,10},{9,11},{10,... | collective-permute-start | bytes 884744 | tf_op jit(solution)/shard_map/ppermute | solution.py:86
  133.0 15.9 %expert.3 = (bf16[1,128,1152]{2,1,0:T(8,128)(2,1)}, bf16[1,128,1152]{2,1,0:T(8,128)(2,1)}, bf16[1,128,1152]{2,1,0:T(8,128)(2,1)}, bf16[1,128,1152]{2,1,0:T(8,128...) custom-call(f32[512,1]{1,0:T(8,128)} %get-tuple-element.133.refs_0_,, ...), custom_call_target="tpu_custom_call" | custom-call | flops 8153726976 | bytes 20054016 | tf_op jit(solution)/shard_map/expert/pallas_call | solution.py:42
  155.1 9.5 %weight_gradient.2.refs_6_ = bf16[1152,2304]{1,0:T(8,128)(2,1)} custom-call(bf16[512,1152]{1,0:T(8,128)(2,1)} %get-tuple-element.92.refs_0_, bf16[512,2304]{1,0:T(8,128)(2,1)} %get-tuple-element.93.refs_1_, bf16[512,1152]{1,0:T(8,128)(2,1)} %get-tuple-element.94.refs_2_, bf16[512,2304]{1,0:T(8,128)(2,1)} %get-tuple-element.95.refs_3_, ...), custom_call_target="tpu_custom_call" | custom-call | flops 5435817984 | bytes 5308416 | tf_op jit(solution)/shard_map/weight_gradient/pallas_call | solution.py:42
  171.4 4.7 %collective-permute-start.17 = (bf16[2,64,1152]{2,1,0:T(8,128)(2,1)S(1)}, bf16[2,64,1152]{2,1,0:T(8,128)(2,1)S(1)}, u32[]{:S(2)}, u32[]{:S(2)}) collective-permute-start(bf16[2,64,1152]{2,1,0:T(8,128)(2,1)S(1)} %copy-done.47), channel_id=1, source_target_pairs={{0,2},{1,3},{2,0},{3,1},{4,6},{5,7},{6,4},{7,5},{8,10},{9,11},{10,... | collective-permute-start | bytes 884744 | tf_op jit(solution)/shard_map/ppermute | solution.py:86
  178.6 10.9 %weight_gradient.3.refs_8_ = bf16[2304,1152]{1,0:T(8,128)(2,1)} custom-call(bf16[512,2304]{1,0:T(8,128)(2,1)} %get-tuple-element.104.refs_0_, bf16[512,1152]{1,0:T(8,128)(2,1)} %get-tuple-element.105.refs_1_, bf16[512,2304]{1,0:T(8,128)(2,1)} %get-tuple-element.106.refs_2_, bf16[512,1152]{1,0:T(8,128)(2,1)} %get-tuple-element.107.refs_3_, ...), custom_call_target="tpu_custom_call" | custom-call | flops 5435817984 | bytes 5308416 | tf_op jit(solution)/shard_map/weight_gradient/pallas_call | solution.py:42
  189.5 10.1 %collective-permute-done.18.refs_6_.refs_9_ = bf16[2,64,1152]{2,1,0:T(8,128)(2,1)S(1)} collective-permute-done((bf16[2,64,1152]{2,1,0:T(8,128)(2,1)S(1)}, bf16[2,64,1152]{2,1,0:T(8,128)(2,1)S(1)}, u32[]{:S(2)}, u32[]{:S(2)}) %collective-permute-start.18) | collective-permute-done | bytes 294944 | tf_op jit(solution)/shard_map/ppermute | solution.py:86
  207.2 4.7 %value_gradient.1 = (bf16[1,64,1152]{2,1,0:T(8,128)(2,1)}, bf16[1,64,1152]{2,1,0:T(8,128)(2,1)}, bf16[1,64,1152]{2,1,0:T(8,128)(2,1)}, bf16[1,64,1152]{2,1,0:T(8...) custom-call(s32[1]{0:T(128)} %bitcast.refs_0_, ...), custom_call_target="tpu_custom_call" | custom-call | flops 301989888 | bytes 4718592 | tf_op jit(solution)/shard_map/value_gradient/pallas_call | solution.py:42
  213.4 4.6 %collective-permute-start.29 = (bf16[1,64,1152]{2,1,0:T(8,128)(2,1)}, bf16[1,64,1152]{2,1,0:T(8,128)(2,1)S(1)}, u32[]{:S(2)}, u32[]{:S(2)}) collective-permute-start(bf16[1,64,1152]{2,1,0:T(8,128)(2,1)} %get-tuple-element.123), channel_id=1, source_target_pairs={{0,4},{1,5},{2,6},{3,7},{4,0},{5,1},{6,2},{7,3},{8,12},{9,13},{10,... | collective-permute-start | bytes 442376 | tf_op jit(solution)/shard_map/ppermute | solution.py:101
  218.6 12.9 %pair_gradients.1 = (bf16[1,2,64,1152]{3,2,1,0:T(8,128)(2,1)}, bf16[1,2,64,1152]{3,2,1,0:T(8,128)(2,1)}, bf16[1,2,64,1152]{3,2,1,0:T(8,128)(2,1)}, bf16[1,2,64,1...) custom-call(s32[1]{0:T(128)} %bitcast.refs_0_, ...), custom_call_target="tpu_custom_call" | custom-call | flops 905969664 | bytes 9437184 | tf_op jit(solution)/shard_map/pair_gradients/pallas_call | solution.py:42
  237.0 15.0 %collective-permute-start.33 = (bf16[1,64,1152]{2,1,0:T(8,128)(2,1)S(1)}, bf16[1,64,1152]{2,1,0:T(8,128)(2,1)S(1)}, u32[]{:S(2)}, u32[]{:S(2)}) collective-permute-start(bf16[1,64,1152]{2,1,0:T(8,128)(2,1)S(1)} %copy-done.49), channel_id=1, source_target_pairs={{0,2},{1,3},{2,0},{3,1},{4,6},{5,7},{6,4},{7,5},{8,10},{9,11},{10,... | collective-permute-start | bytes 442376 | tf_op jit(solution)/shard_map/ppermute | solution.py:101
  262.4 11.6 %collective-permute-start.26 = (bf16[1,2,64,1152]{3,2,1,0:T(8,128)(2,1)S(1)}, bf16[1,2,64,1152]{3,2,1,0:T(8,128)(2,1)S(1)}, u32[]{:S(2)}, u32[]{:S(2)}) collective-permute-start(bf16[1,2,64,1152]{3,2,1,0:T(8,128)(2,1)S(1)} %copy-done.44), channel_id=1, source_target_pairs={{0,2},{1,3},{2,0},{3,1},{4,6},{5,7},{6,4},{7,5},{8,10},{9,11},{10,... | collective-permute-start | bytes 884744 | tf_op jit(solution)/shard_map/ppermute | solution.py:101
  273.9 6.1 %collective-permute-done.22.refs_2_ = bf16[1,2,64,1152]{3,2,1,0:T(8,128)(2,1)S(1)} collective-permute-done((bf16[1,2,64,1152]{3,2,1,0:T(8,128)(2,1)}, bf16[1,2,64,1152]{3,2,1,0:T(8,128)(2,1)S(1)}, u32[]{:S(2)}, u32[]{:S(2)}) %collective-permute-start.22) | collective-permute-done | bytes 294944 | tf_op jit(solution)/shard_map/ppermute | solution.py:101
  280.1 4.1 %fusion = (f32[288,2304]{1,0:T(8,128)}, f32[1,288,2304]{2,1,0:T(8,128)}) fusion(bf16[288,2304]{1,0:T(8,128)(2,1)} %reduce-scatter.3.cloned.1.call-done), kind=kLoop, calls=%fused_computation.5 | loop fusion | flops 663552 | bytes 6635520 | tf_op jit(solution)/shard_map/convert_element_type | solution.py:639
  284.2 8.3 %collective-permute-done.24.refs_4_ = bf16[1,2,64,1152]{3,2,1,0:T(8,128)(2,1)S(1)} collective-permute-done((bf16[1,2,64,1152]{3,2,1,0:T(8,128)(2,1)}, bf16[1,2,64,1152]{3,2,1,0:T(8,128)(2,1)S(1)}, u32[]{:S(2)}, u32[]{:S(2)}) %collective-permute-start.24) | collective-permute-done | bytes 294944 | tf_op jit(solution)/shard_map/ppermute | solution.py:101
  (174 shorter events, 67.3 us)
Async XLA Ops:
  7.2 272.9 %reduce-scatter.3.cloned.1.call-start = ((), (), s32[]{:S(2)}) async-start(), calls=%async_computation.2 | async-start | bytes 6635520 | tf_op jit(solution)/shard_map/reduce_scatter | solution.py:639
  15.5 29.7 %collective-permute-start.1 = (bf16[1,256,1152]{2,1,0:T(8,128)(2,1)}, bf16[1,256,1152]{2,1,0:T(8,128)(2,1)S(1)}, u32[]{:S(2)}, u32[]{:S(2)}) collective-permute-start(bf16[1,256,1152]{2,1,0:T(8,128)(2,1)} %get-tuple-element.72), channel_id=1, source_target_pairs={{0,2},{1,3},{2,0},{3,1},{4,6},{5,7},{6,4},{7,5},{8,10},{9,11},{10,... | collective-permute-start | bytes 1769480 | tf_op jit(solution)/shard_map/ppermute | solution.py:101
  18.2 39.1 %collective-permute-start.2 = (bf16[1,256,1152]{2,1,0:T(8,128)(2,1)}, bf16[1,256,1152]{2,1,0:T(8,128)(2,1)S(1)}, u32[]{:S(2)}, u32[]{:S(2)}) collective-permute-start(bf16[1,256,1152]{2,1,0:T(8,128)(2,1)} %get-tuple-element.73), channel_id=1, source_target_pairs={{0,3},{1,2},{2,1},{3,0},{4,7},{5,6},{6,5},{7,4},{8,11},{9,10},{10,... | collective-permute-start | bytes 1769480 | tf_op jit(solution)/shard_map/ppermute | solution.py:101
  18.2 55.1 %collective-permute-start.3 = (bf16[1,256,1152]{2,1,0:T(8,128)(2,1)}, bf16[1,256,1152]{2,1,0:T(8,128)(2,1)S(1)}, u32[]{:S(2)}, u32[]{:S(2)}) collective-permute-start(bf16[1,256,1152]{2,1,0:T(8,128)(2,1)} %get-tuple-element.76), channel_id=1, source_target_pairs={{0,4},{1,5},{2,6},{3,7},{4,0},{5,1},{6,2},{7,3},{8,12},{9,13},{10,... | collective-permute-start | bytes 1769480 | tf_op jit(solution)/shard_map/ppermute | solution.py:101
  21.0 52.4 %collective-permute-start.4 = (bf16[1,256,1152]{2,1,0:T(8,128)(2,1)}, bf16[1,256,1152]{2,1,0:T(8,128)(2,1)S(1)}, u32[]{:S(2)}, u32[]{:S(2)}) collective-permute-start(bf16[1,256,1152]{2,1,0:T(8,128)(2,1)} %get-tuple-element.77), channel_id=1, source_target_pairs={{0,6},{1,7},{6,0},{7,1},{8,14},{9,15},{14,8},{15,9},{16,22},{17,23... | collective-permute-start | bytes 1769480 | tf_op jit(solution)/shard_map/ppermute | solution.py:108
  34.3 78.1 %collective-permute-start.7 = (bf16[1,256,1152]{2,1,0:T(8,128)(2,1)S(1)}, bf16[1,256,1152]{2,1,0:T(8,128)(2,1)S(1)}, u32[]{:S(2)}, u32[]{:S(2)}) collective-permute-start(bf16[1,256,1152]{2,1,0:T(8,128)(2,1)S(1)} %copy-done.36), channel_id=1, source_target_pairs={{2,4},{3,5},{4,2},{5,3},{10,12},{11,13},{12,10},{13,11},{18,20},{1... | collective-permute-start | bytes 1769480 | tf_op jit(solution)/shard_map/ppermute | solution.py:108
  45.2 67.2 %collective-permute-start.5 = (bf16[1,256,1152]{2,1,0:T(8,128)(2,1)S(1)}, bf16[1,256,1152]{2,1,0:T(8,128)(2,1)S(1)}, u32[]{:S(2)}, u32[]{:S(2)}) collective-permute-start(bf16[1,256,1152]{2,1,0:T(8,128)(2,1)S(1)} %copy-done.38), channel_id=1, source_target_pairs={{0,5},{1,4},{2,7},{3,6},{4,1},{5,0},{6,3},{7,2},{8,13},{9,12},{10,... | collective-permute-start | bytes 1769480 | tf_op jit(solution)/shard_map/ppermute | solution.py:101
  57.3 55.1 %collective-permute-start.6 = (bf16[1,256,1152]{2,1,0:T(8,128)(2,1)S(1)}, bf16[1,256,1152]{2,1,0:T(8,128)(2,1)S(1)}, u32[]{:S(2)}, u32[]{:S(2)}) collective-permute-start(bf16[1,256,1152]{2,1,0:T(8,128)(2,1)S(1)} %copy-done.37), channel_id=1, source_target_pairs={{0,7},{1,6},{2,5},{3,4},{4,3},{5,2},{6,1},{7,0},{8,15},{9,14},{10,... | collective-permute-start | bytes 1769480 | tf_op jit(solution)/shard_map/ppermute | solution.py:101
  90.1 22.3 %collective-permute-start.8 = (bf16[1,128,1152]{2,1,0:T(8,128)(2,1)}, bf16[1,128,1152]{2,1,0:T(8,128)(2,1)S(1)}, u32[]{:S(2)}, u32[]{:S(2)}) collective-permute-start(bf16[1,128,1152]{2,1,0:T(8,128)(2,1)} %get-tuple-element.82), channel_id=1, source_target_pairs={{0,1},{1,0},{2,3},{3,2},{4,5},{5,4},{6,7},{7,6},{8,9},{9,8},{10,11... | collective-permute-start | bytes 884744 | tf_op jit(solution)/shard_map/ppermute | solution.py:101
  90.2 26.6 %collective-permute-start.9 = (bf16[1,128,1152]{2,1,0:T(8,128)(2,1)}, bf16[1,128,1152]{2,1,0:T(8,128)(2,1)S(1)}, u32[]{:S(2)}, u32[]{:S(2)}) collective-permute-start(bf16[1,128,1152]{2,1,0:T(8,128)(2,1)} %get-tuple-element.83), channel_id=1, source_target_pairs={{0,2},{1,3},{2,0},{3,1},{4,6},{5,7},{6,4},{7,5},{8,10},{9,11},{10,... | collective-permute-start | bytes 884744 | tf_op jit(solution)/shard_map/ppermute | solution.py:101
  127.0 23.2 %collective-permute-start.14 = (bf16[2,64,1152]{2,1,0:T(8,128)(2,1)}, bf16[2,64,1152]{2,1,0:T(8,128)(2,1)S(1)}, u32[]{:S(2)}, u32[]{:S(2)}) collective-permute-start(bf16[2,64,1152]{2,1,0:T(8,128)(2,1)} %get-tuple-element.96), channel_id=1, source_target_pairs={{0,2},{1,3},{2,0},{3,1},{4,6},{5,7},{6,4},{7,5},{8,10},{9,11},{10,... | collective-permute-start | bytes 884744 | tf_op jit(solution)/shard_map/ppermute | solution.py:86
  130.6 23.6 %collective-permute-start.15 = (bf16[2,64,1152]{2,1,0:T(8,128)(2,1)}, bf16[2,64,1152]{2,1,0:T(8,128)(2,1)S(1)}, u32[]{:S(2)}, u32[]{:S(2)}) collective-permute-start(bf16[2,64,1152]{2,1,0:T(8,128)(2,1)} %get-tuple-element.97), channel_id=1, source_target_pairs={{0,4},{1,5},{2,6},{3,7},{4,0},{5,1},{6,2},{7,3},{8,12},{9,13},{10,... | collective-permute-start | bytes 884744 | tf_op jit(solution)/shard_map/ppermute | solution.py:86
  131.1 23.2 %collective-permute-start.16 = (bf16[2,64,1152]{2,1,0:T(8,128)(2,1)}, bf16[2,64,1152]{2,1,0:T(8,128)(2,1)S(1)}, u32[]{:S(2)}, u32[]{:S(2)}) collective-permute-start(bf16[2,64,1152]{2,1,0:T(8,128)(2,1)} %get-tuple-element.98), channel_id=1, source_target_pairs={{0,6},{1,7},{2,4},{3,5},{4,2},{5,3},{6,0},{7,1},{8,14},{9,15},{10,... | collective-permute-start | bytes 884744 | tf_op jit(solution)/shard_map/ppermute | solution.py:86
  170.4 129.6 %reduce-scatter.5.cloned.1.call-start = ((), (), s32[]{:S(2)}) async-start(), calls=%async_computation.3 | async-start | bytes 6635520 | tf_op jit(solution)/shard_map/reduce_scatter | solution.py:649
  176.1 23.5 %collective-permute-start.18 = (bf16[2,64,1152]{2,1,0:T(8,128)(2,1)S(1)}, bf16[2,64,1152]{2,1,0:T(8,128)(2,1)S(1)}, u32[]{:S(2)}, u32[]{:S(2)}) collective-permute-start(bf16[2,64,1152]{2,1,0:T(8,128)(2,1)S(1)} %copy-done.46), channel_id=1, source_target_pairs={{0,4},{1,5},{2,6},{3,7},{4,0},{5,1},{6,2},{7,3},{8,12},{9,13},{10,... | collective-permute-start | bytes 884744 | tf_op jit(solution)/shard_map/ppermute | solution.py:86
  176.1 23.5 %collective-permute-start.19 = (bf16[2,64,1152]{2,1,0:T(8,128)(2,1)S(1)}, bf16[2,64,1152]{2,1,0:T(8,128)(2,1)S(1)}, u32[]{:S(2)}, u32[]{:S(2)}) collective-permute-start(bf16[2,64,1152]{2,1,0:T(8,128)(2,1)S(1)} %copy-done.45), channel_id=1, source_target_pairs={{0,6},{1,7},{2,4},{3,5},{4,2},{5,3},{6,0},{7,1},{8,14},{9,15},{10,... | collective-permute-start | bytes 884744 | tf_op jit(solution)/shard_map/ppermute | solution.py:86
  213.4 23.5 %collective-permute-start.29 = (bf16[1,64,1152]{2,1,0:T(8,128)(2,1)}, bf16[1,64,1152]{2,1,0:T(8,128)(2,1)S(1)}, u32[]{:S(2)}, u32[]{:S(2)}) collective-permute-start(bf16[1,64,1152]{2,1,0:T(8,128)(2,1)} %get-tuple-element.123), channel_id=1, source_target_pairs={{0,4},{1,5},{2,6},{3,7},{4,0},{5,1},{6,2},{7,3},{8,12},{9,13},{10,... | collective-permute-start | bytes 442376 | tf_op jit(solution)/shard_map/ppermute | solution.py:101
  218.5 36.2 %collective-permute-start.31 = (bf16[1,64,1152]{2,1,0:T(8,128)(2,1)}, bf16[1,64,1152]{2,1,0:T(8,128)(2,1)S(1)}, u32[]{:S(2)}, u32[]{:S(2)}) collective-permute-start(bf16[1,64,1152]{2,1,0:T(8,128)(2,1)} %get-tuple-element.125), channel_id=1, source_target_pairs={{0,5},{1,4},{2,7},{3,6},{4,1},{5,0},{6,3},{7,2},{8,13},{9,12},{10,... | collective-permute-start | bytes 442376 | tf_op jit(solution)/shard_map/ppermute | solution.py:101
  231.5 30.8 %collective-permute-start.21 = (bf16[1,2,64,1152]{3,2,1,0:T(8,128)(2,1)}, bf16[1,2,64,1152]{3,2,1,0:T(8,128)(2,1)S(1)}, u32[]{:S(2)}, u32[]{:S(2)}) collective-permute-start(bf16[1,2,64,1152]{3,2,1,0:T(8,128)(2,1)} %get-tuple-element.112), channel_id=1, source_target_pairs={{0,6},{1,7},{2,4},{3,5},{4,2},{5,3},{6,0},{7,1},{8,14},{9,15},{10,... | collective-permute-start | bytes 884744 | tf_op jit(solution)/shard_map/ppermute | solution.py:101
  234.2 45.9 %collective-permute-start.22 = (bf16[1,2,64,1152]{3,2,1,0:T(8,128)(2,1)}, bf16[1,2,64,1152]{3,2,1,0:T(8,128)(2,1)S(1)}, u32[]{:S(2)}, u32[]{:S(2)}) collective-permute-start(bf16[1,2,64,1152]{3,2,1,0:T(8,128)(2,1)} %get-tuple-element.113), channel_id=1, source_target_pairs={{0,4},{1,5},{2,6},{3,7},{4,0},{5,1},{6,2},{7,3},{8,12},{9,13},{10,... | collective-permute-start | bytes 884744 | tf_op jit(solution)/shard_map/ppermute | solution.py:101
  255.6 28.6 %collective-permute-start.23 = (bf16[1,2,64,1152]{3,2,1,0:T(8,128)(2,1)}, bf16[1,2,64,1152]{3,2,1,0:T(8,128)(2,1)S(1)}, u32[]{:S(2)}, u32[]{:S(2)}) collective-permute-start(bf16[1,2,64,1152]{3,2,1,0:T(8,128)(2,1)} %get-tuple-element.114), channel_id=1, source_target_pairs={{0,7},{1,6},{2,5},{3,4},{4,3},{5,2},{6,1},{7,0},{8,15},{9,14},{10,... | collective-permute-start | bytes 884744 | tf_op jit(solution)/shard_map/ppermute | solution.py:101
  257.8 34.7 %collective-permute-start.24 = (bf16[1,2,64,1152]{3,2,1,0:T(8,128)(2,1)}, bf16[1,2,64,1152]{3,2,1,0:T(8,128)(2,1)S(1)}, u32[]{:S(2)}, u32[]{:S(2)}) collective-permute-start(bf16[1,2,64,1152]{3,2,1,0:T(8,128)(2,1)} %get-tuple-element.115), channel_id=1, source_target_pairs={{0,5},{1,4},{2,7},{3,6},{4,1},{5,0},{6,3},{7,2},{8,13},{9,12},{10,... | collective-permute-start | bytes 884744 | tf_op jit(solution)/shard_map/ppermute | solution.py:101
  257.8 34.7 %collective-permute-start.25 = (bf16[1,2,64,1152]{3,2,1,0:T(8,128)(2,1)}, bf16[1,2,64,1152]{3,2,1,0:T(8,128)(2,1)S(1)}, u32[]{:S(2)}, u32[]{:S(2)}) collective-permute-start(bf16[1,2,64,1152]{3,2,1,0:T(8,128)(2,1)} %get-tuple-element.116), channel_id=1, source_target_pairs={{0,3},{1,2},{2,1},{3,0},{4,7},{5,6},{6,5},{7,4},{8,11},{9,10},{10,... | collective-permute-start | bytes 884744 | tf_op jit(solution)/shard_map/ppermute | solution.py:101
  262.4 30.2 %collective-permute-start.26 = (bf16[1,2,64,1152]{3,2,1,0:T(8,128)(2,1)S(1)}, bf16[1,2,64,1152]{3,2,1,0:T(8,128)(2,1)S(1)}, u32[]{:S(2)}, u32[]{:S(2)}) collective-permute-start(bf16[1,2,64,1152]{3,2,1,0:T(8,128)(2,1)S(1)} %copy-done.44), channel_id=1, source_target_pairs={{0,2},{1,3},{2,0},{3,1},{4,6},{5,7},{6,4},{7,5},{8,10},{9,11},{10,... | collective-permute-start | bytes 884744 | tf_op jit(solution)/shard_map/ppermute | solution.py:101
  (64 other events, 791.5 us)
Sparse Core Ops, SparseCore 0:
  170.6 64.4 reduce-scatter.2
  238.0 61.9 reduce-scatter.4

commit v3 on v2

--- a/solution.py
+++ b/solution.py
@@ -633,9 +633,11 @@
 
     x_near, scaled_near, act_near, pre_near, sums_near = rest_near
     x_far, scaled_far, act_far, pre_far, sums_far = rest_far
-    crossed = grad_near[1:]
-    in_term = weight_gradient((x_near, pre_near), (x_far, pre_far), False, after=crossed)
-    *send_far, in_term = combine(me, hit_other, back_far, None, count, carry=in_term)
+    crossed = grad_near[2:]
+    in_term = weight_gradient((x_near, pre_near), (x_far, pre_far), False)
+    *send_far, in_term = combine(
+        me, hit_other, back_far, None, count, after=crossed, carry=in_term
+    )
     in_share = lax.psum_scatter(in_term, "slab", scatter_dimension=0, tiled=True).astype(F32)
     grad_far = pairs(send_far)
     out_term = weight_gradient(

time: 310 us -> 306 us (0.987)
    unnamed x102 -> x104, local copies, waits for them, and re-layouts: 8.27 us -> 6.78 us
  transfers between devices with their start and end apart: 37 -> 37, of which waited for: 14 -> 15; matrix products, arithmetic and copies ran while one was open for 2% -> 2% of each run, Pallas kernels for 28% -> 28%
where the time goes in v3:
time: 306 us; the launch traced here: 305 us
  Pallas kernels  102 us (33%)
  waiting for transfers between devices  90.8 us (30%)
  starting transfers between devices  82.3 us (27%)
  between operations  14.5 us (5%)
  other arithmetic  8.11 us (3%)
  local copies, waits for them, and re-layouts  7.85 us (3%)
    pallas_call x13, Pallas kernels, call(): pl.pallas_call(run, out_shape=out_shape, in_specs=list(in_specs) + [ANY]...  102 us
    ppermute x26, waiting for transfers between devices, exchange_single(): lax.ppermute(b, 'dev', pairs[k])  74.8 us
    ppermute x26, starting transfers between devices, exchange_single(): lax.ppermute(b, 'dev', pairs[k])  66.9 us
    ppermute x6, waiting for transfers between devices, exchange_pairs(): lax.ppermute(pair, 'dev', [(d, d ^ 2 * i) for d in range(count)])  12.9 us
    ppermute x6, starting transfers between devices, exchange_pairs(): lax.ppermute(pair, 'dev', [(d, d ^ 2 * i) for d in range(count)])  11 us
    unnamed x104, local copies, waits for them, and re-layouts  6.78 us
  transfers between devices with their start and end apart: 37, of which 15 were waited for; matrix products, arithmetic and copies ran while one was open for 2% of the time, Pallas kernels for 28%

profile of v3, /device:TPU:0, one launch (start us, length us, event | category | flops | bytes accessed | tf_op | source)
XLA Modules:
  0.0 305.1 jit_solution(7691673134552054576)
XLA Ops:
  7.2 7.8 %prep.1 = (bf16[1,256,1152]{2,1,0:T(8,128)(2,1)}, bf16[1,256,1152]{2,1,0:T(8,128)(2,1)}, bf16[1,256,1152]{2,1,0:T(8,128)(2,1)}, bf16[1,256,1152]{2,1,0:T(8,128)(...) custom-call(s32[1]{0:T(128)} %bitcast.refs_0_, ...), custom_call_target="tpu_custom_call" | custom-call | flops 2415919104 | bytes 9437184 | tf_op jit(solution)/shard_map/prep/pallas_call | solution.py:42
  24.3 9.2 %probs.1 = (f32[4,16,128,128]{3,2,1,0:T(8,128)}, bf16[4,16,128,128]{3,2,1,0:T(8,128)(2,1)}) custom-call(bf16[8,64,1152]{2,1,0:T(8,128)(2,1)} %refs_3_.1, bf16[8,64,1152]{2,1,0:T(8,128)(2,1)} %refs_4_.1, bf16[1024,512]{1,0:T(8,128)(2,1)} %get-tuple-element.74.refs_2_.refs_1_), custom_call_target="tpu_custom_call" | custom-call | flops 603979776 | bytes 8650752 | tf_op jit(solution)/shard_map/probs/pallas_call | solution.py:42
  35.3 10.0 %collective-permute-done.1.refs_5_ = bf16[1,256,1152]{2,1,0:T(8,128)(2,1)S(1)} collective-permute-done((bf16[1,256,1152]{2,1,0:T(8,128)(2,1)}, bf16[1,256,1152]{2,1,0:T(8,128)(2,1)S(1)}, u32[]{:S(2)}, u32[]{:S(2)}) %collective-permute-start.1) | collective-permute-done | bytes 589856 | tf_op jit(solution)/shard_map/ppermute | solution.py:101
  46.2 11.1 %collective-permute-done.2.refs_6_ = bf16[1,256,1152]{2,1,0:T(8,128)(2,1)S(1)} collective-permute-done((bf16[1,256,1152]{2,1,0:T(8,128)(2,1)}, bf16[1,256,1152]{2,1,0:T(8,128)(2,1)S(1)}, u32[]{:S(2)}, u32[]{:S(2)}) %collective-permute-start.2) | collective-permute-done | bytes 589856 | tf_op jit(solution)/shard_map/ppermute | solution.py:101
  57.4 16.0 %collective-permute-start.6 = (bf16[1,256,1152]{2,1,0:T(8,128)(2,1)S(1)}, bf16[1,256,1152]{2,1,0:T(8,128)(2,1)S(1)}, u32[]{:S(2)}, u32[]{:S(2)}) collective-permute-start(bf16[1,256,1152]{2,1,0:T(8,128)(2,1)S(1)} %copy-done.37), channel_id=1, source_target_pairs={{0,7},{1,6},{2,5},{3,4},{4,3},{5,2},{6,1},{7,0},{8,15},{9,14},{10,... | collective-permute-start | bytes 1769480 | tf_op jit(solution)/shard_map/ppermute | solution.py:101
  74.5 15.7 %expert.2 = (bf16[1,128,1152]{2,1,0:T(8,128)(2,1)}, bf16[1,128,1152]{2,1,0:T(8,128)(2,1)}, bf16[1,128,1152]{2,1,0:T(8,128)(2,1)}, bf16[1,128,1152]{2,1,0:T(8,128...) custom-call(f32[512,1]{1,0:T(8,128)} %get-tuple-element.132.refs_0_,, ...), custom_call_target="tpu_custom_call" | custom-call | flops 8153726976 | bytes 20054016 | tf_op jit(solution)/shard_map/expert/pallas_call | solution.py:42
  90.3 22.1 %collective-permute-done.5.refs_7_.refs_4_ = bf16[1,256,1152]{2,1,0:T(8,128)(2,1)S(1)} collective-permute-done((bf16[1,256,1152]{2,1,0:T(8,128)(2,1)S(1)}, bf16[1,256,1152]{2,1,0:T(8,128)(2,1)S(1)}, u32[]{:S(2)}, u32[]{:S(2)}) %collective-permute-start.5) | collective-permute-done | bytes 589856 | tf_op jit(solution)/shard_map/ppermute | solution.py:101
  112.5 4.4 %collective-permute-done.9.refs_4_ = bf16[1,128,1152]{2,1,0:T(8,128)(2,1)S(1)} collective-permute-done((bf16[1,128,1152]{2,1,0:T(8,128)(2,1)}, bf16[1,128,1152]{2,1,0:T(8,128)(2,1)S(1)}, u32[]{:S(2)}, u32[]{:S(2)}) %collective-permute-start.9) | collective-permute-done | bytes 294944 | tf_op jit(solution)/shard_map/ppermute | solution.py:101
  116.9 5.7 %collective-permute-done.10.refs_5_ = bf16[1,128,1152]{2,1,0:T(8,128)(2,1)S(1)} collective-permute-done((bf16[1,128,1152]{2,1,0:T(8,128)(2,1)}, bf16[1,128,1152]{2,1,0:T(8,128)(2,1)S(1)}, u32[]{:S(2)}, u32[]{:S(2)}) %collective-permute-start.10) | collective-permute-done | bytes 294944 | tf_op jit(solution)/shard_map/ppermute | solution.py:101
  123.2 3.7 %combine.2 = (bf16[2,64,1152]{2,1,0:T(8,128)(2,1)}, bf16[2,64,1152]{2,1,0:T(8,128)(2,1)}, bf16[2,64,1152]{2,1,0:T(8,128)(2,1)}, bf16[2,64,1152]{2,1,0:T(8,128)(2,1)}) custom-call(s32[1]{0:T(128)} %bitcast.refs_0_, bf16[1024,512]{1,0:T(8,128)(2,1)} %get-tuple-element.74.refs_2_.refs_1_, bf16[1,128,1152]{2,1,0:T(8,128)(2,1)} %get-tuple-element.81.refs_2_, ...), custom_call_target="tpu_custom_call" | custom-call | flops 603979776 | bytes 3538944 | tf_op jit(solution)/shard_map/combine/pallas_call | solution.py:42
  127.0 4.1 %collective-permute-start.14 = (bf16[2,64,1152]{2,1,0:T(8,128)(2,1)}, bf16[2,64,1152]{2,1,0:T(8,128)(2,1)S(1)}, u32[]{:S(2)}, u32[]{:S(2)}) collective-permute-start(bf16[2,64,1152]{2,1,0:T(8,128)(2,1)} %get-tuple-element.92), channel_id=1, source_target_pairs={{0,4},{1,5},{2,6},{3,7},{4,0},{5,1},{6,2},{7,3},{8,12},{9,13},{10,... | collective-permute-start | bytes 884744 | tf_op jit(solution)/shard_map/ppermute | solution.py:86
  133.0 15.9 %expert.3 = (bf16[1,128,1152]{2,1,0:T(8,128)(2,1)}, bf16[1,128,1152]{2,1,0:T(8,128)(2,1)}, bf16[1,128,1152]{2,1,0:T(8,128)(2,1)}, bf16[1,128,1152]{2,1,0:T(8,128...) custom-call(f32[512,1]{1,0:T(8,128)} %get-tuple-element.133.refs_0_,, ...), custom_call_target="tpu_custom_call" | custom-call | flops 8153726976 | bytes 20054016 | tf_op jit(solution)/shard_map/expert/pallas_call | solution.py:42
  150.8 9.6 %weight_gradient.2.refs_8_ = bf16[1152,2304]{1,0:T(8,128)(2,1)} custom-call(bf16[512,1152]{1,0:T(8,128)(2,1)} %get-tuple-element.94.refs_0_, bf16[512,2304]{1,0:T(8,128)(2,1)} %get-tuple-element.95.refs_1_, bf16[512,1152]{1,0:T(8,128)(2,1)} %get-tuple-element.96.refs_2_, bf16[512,2304]{1,0:T(8,128)(2,1)} %get-tuple-element.97.refs_3_), custom_call_target="tpu_custom_call" | custom-call | flops 5435817984 | bytes 5308416 | tf_op jit(solution)/shard_map/weight_gradient/pallas_call | solution.py:42
  160.5 3.9 %collective-permute-done.13.refs_5_ = bf16[1,128,1152]{2,1,0:T(8,128)(2,1)S(1)} collective-permute-done((bf16[1,128,1152]{2,1,0:T(8,128)(2,1)}, bf16[1,128,1152]{2,1,0:T(8,128)(2,1)S(1)}, u32[]{:S(2)}, u32[]{:S(2)}) %collective-permute-start.13) | collective-permute-done | bytes 294944 | tf_op jit(solution)/shard_map/ppermute | solution.py:101
  174.4 10.6 %weight_gradient.3.refs_8_ = bf16[2304,1152]{1,0:T(8,128)(2,1)} custom-call(bf16[512,2304]{1,0:T(8,128)(2,1)} %get-tuple-element.104.refs_0_, bf16[512,1152]{1,0:T(8,128)(2,1)} %get-tuple-element.105.refs_1_, bf16[512,2304]{1,0:T(8,128)(2,1)} %get-tuple-element.106.refs_2_, bf16[512,1152]{1,0:T(8,128)(2,1)} %get-tuple-element.107.refs_3_, ...), custom_call_target="tpu_custom_call" | custom-call | flops 5435817984 | bytes 5308416 | tf_op jit(solution)/shard_map/weight_gradient/pallas_call | solution.py:42
  185.5 6.4 %collective-permute-done.17.refs_5_.refs_8_ = bf16[2,64,1152]{2,1,0:T(8,128)(2,1)S(1)} collective-permute-done((bf16[2,64,1152]{2,1,0:T(8,128)(2,1)S(1)}, bf16[2,64,1152]{2,1,0:T(8,128)(2,1)S(1)}, u32[]{:S(2)}, u32[]{:S(2)}) %collective-permute-start.17) | collective-permute-done | bytes 294944 | tf_op jit(solution)/shard_map/ppermute | solution.py:86
  191.9 6.0 %collective-permute-done.19.refs_7_.refs_10_ = bf16[2,64,1152]{2,1,0:T(8,128)(2,1)S(1)} collective-permute-done((bf16[2,64,1152]{2,1,0:T(8,128)(2,1)S(1)}, bf16[2,64,1152]{2,1,0:T(8,128)(2,1)S(1)}, u32[]{:S(2)}, u32[]{:S(2)}) %collective-permute-start.19) | collective-permute-done | bytes 294944 | tf_op jit(solution)/shard_map/ppermute | solution.py:86
  204.8 4.7 %value_gradient.1 = (bf16[1,64,1152]{2,1,0:T(8,128)(2,1)}, bf16[1,64,1152]{2,1,0:T(8,128)(2,1)}, bf16[1,64,1152]{2,1,0:T(8,128)(2,1)}, bf16[1,64,1152]{2,1,0:T(8...) custom-call(s32[1]{0:T(128)} %bitcast.refs_0_, ...), custom_call_target="tpu_custom_call" | custom-call | flops 301989888 | bytes 4718592 | tf_op jit(solution)/shard_map/value_gradient/pallas_call | solution.py:42
  215.2 12.9 %pair_gradients.1 = (bf16[1,2,64,1152]{3,2,1,0:T(8,128)(2,1)}, bf16[1,2,64,1152]{3,2,1,0:T(8,128)(2,1)}, bf16[1,2,64,1152]{3,2,1,0:T(8,128)(2,1)}, bf16[1,2,64,1...) custom-call(s32[1]{0:T(128)} %bitcast.refs_0_, ...), custom_call_target="tpu_custom_call" | custom-call | flops 905969664 | bytes 9437184 | tf_op jit(solution)/shard_map/pair_gradients/pallas_call | solution.py:42
  233.4 16.2 %collective-permute-start.33 = (bf16[1,64,1152]{2,1,0:T(8,128)(2,1)S(1)}, bf16[1,64,1152]{2,1,0:T(8,128)(2,1)S(1)}, u32[]{:S(2)}, u32[]{:S(2)}) collective-permute-start(bf16[1,64,1152]{2,1,0:T(8,128)(2,1)S(1)} %copy-done.50), channel_id=1, source_target_pairs={{0,2},{1,3},{2,0},{3,1},{4,6},{5,7},{6,4},{7,5},{8,10},{9,11},{10,... | collective-permute-start | bytes 442376 | tf_op jit(solution)/shard_map/ppermute | solution.py:101
  260.3 11.3 %collective-permute-start.26 = (bf16[1,2,64,1152]{3,2,1,0:T(8,128)(2,1)S(1)}, bf16[1,2,64,1152]{3,2,1,0:T(8,128)(2,1)S(1)}, u32[]{:S(2)}, u32[]{:S(2)}) collective-permute-start(bf16[1,2,64,1152]{3,2,1,0:T(8,128)(2,1)S(1)} %copy-done.44), channel_id=1, source_target_pairs={{0,2},{1,3},{2,0},{3,1},{4,6},{5,7},{6,4},{7,5},{8,10},{9,11},{10,... | collective-permute-start | bytes 884744 | tf_op jit(solution)/shard_map/ppermute | solution.py:101
  271.5 6.1 %collective-permute-done.22.refs_2_ = bf16[1,2,64,1152]{3,2,1,0:T(8,128)(2,1)S(1)} collective-permute-done((bf16[1,2,64,1152]{3,2,1,0:T(8,128)(2,1)}, bf16[1,2,64,1152]{3,2,1,0:T(8,128)(2,1)S(1)}, u32[]{:S(2)}, u32[]{:S(2)}) %collective-permute-start.22) | collective-permute-done | bytes 294944 | tf_op jit(solution)/shard_map/ppermute | solution.py:101
  277.7 4.2 %fusion = (f32[288,2304]{1,0:T(8,128)}, f32[1,288,2304]{2,1,0:T(8,128)}) fusion(bf16[288,2304]{1,0:T(8,128)(2,1)} %reduce-scatter.3.cloned.1.call-done), kind=kLoop, calls=%fused_computation.5 | loop fusion | flops 663552 | bytes 6635520 | tf_op jit(solution)/shard_map/convert_element_type | solution.py:641
  281.9 8.3 %collective-permute-done.24.refs_4_ = bf16[1,2,64,1152]{3,2,1,0:T(8,128)(2,1)S(1)} collective-permute-done((bf16[1,2,64,1152]{3,2,1,0:T(8,128)(2,1)}, bf16[1,2,64,1152]{3,2,1,0:T(8,128)(2,1)S(1)}, u32[]{:S(2)}, u32[]{:S(2)}) %collective-permute-start.24) | collective-permute-done | bytes 294944 | tf_op jit(solution)/shard_map/ppermute | solution.py:101
  (176 shorter events, 64.9 us)
Async XLA Ops:
  7.2 270.5 %reduce-scatter.3.cloned.1.call-start = ((), (), s32[]{:S(2)}) async-start(), calls=%async_computation.2 | async-start | bytes 6635520 | tf_op jit(solution)/shard_map/reduce_scatter | solution.py:641
  15.6 29.7 %collective-permute-start.1 = (bf16[1,256,1152]{2,1,0:T(8,128)(2,1)}, bf16[1,256,1152]{2,1,0:T(8,128)(2,1)S(1)}, u32[]{:S(2)}, u32[]{:S(2)}) collective-permute-start(bf16[1,256,1152]{2,1,0:T(8,128)(2,1)} %get-tuple-element.72), channel_id=1, source_target_pairs={{0,2},{1,3},{2,0},{3,1},{4,6},{5,7},{6,4},{7,5},{8,10},{9,11},{10,... | collective-permute-start | bytes 1769480 | tf_op jit(solution)/shard_map/ppermute | solution.py:101
  18.2 39.1 %collective-permute-start.2 = (bf16[1,256,1152]{2,1,0:T(8,128)(2,1)}, bf16[1,256,1152]{2,1,0:T(8,128)(2,1)S(1)}, u32[]{:S(2)}, u32[]{:S(2)}) collective-permute-start(bf16[1,256,1152]{2,1,0:T(8,128)(2,1)} %get-tuple-element.73), channel_id=1, source_target_pairs={{0,3},{1,2},{2,1},{3,0},{4,7},{5,6},{6,5},{7,4},{8,11},{9,10},{10,... | collective-permute-start | bytes 1769480 | tf_op jit(solution)/shard_map/ppermute | solution.py:101
  18.3 55.1 %collective-permute-start.3 = (bf16[1,256,1152]{2,1,0:T(8,128)(2,1)}, bf16[1,256,1152]{2,1,0:T(8,128)(2,1)S(1)}, u32[]{:S(2)}, u32[]{:S(2)}) collective-permute-start(bf16[1,256,1152]{2,1,0:T(8,128)(2,1)} %get-tuple-element.76), channel_id=1, source_target_pairs={{0,4},{1,5},{2,6},{3,7},{4,0},{5,1},{6,2},{7,3},{8,12},{9,13},{10,... | collective-permute-start | bytes 1769480 | tf_op jit(solution)/shard_map/ppermute | solution.py:101
  21.0 52.4 %collective-permute-start.4 = (bf16[1,256,1152]{2,1,0:T(8,128)(2,1)}, bf16[1,256,1152]{2,1,0:T(8,128)(2,1)S(1)}, u32[]{:S(2)}, u32[]{:S(2)}) collective-permute-start(bf16[1,256,1152]{2,1,0:T(8,128)(2,1)} %get-tuple-element.77), channel_id=1, source_target_pairs={{0,6},{1,7},{6,0},{7,1},{8,14},{9,15},{14,8},{15,9},{16,22},{17,23... | collective-permute-start | bytes 1769480 | tf_op jit(solution)/shard_map/ppermute | solution.py:108
  34.4 78.1 %collective-permute-start.7 = (bf16[1,256,1152]{2,1,0:T(8,128)(2,1)S(1)}, bf16[1,256,1152]{2,1,0:T(8,128)(2,1)S(1)}, u32[]{:S(2)}, u32[]{:S(2)}) collective-permute-start(bf16[1,256,1152]{2,1,0:T(8,128)(2,1)S(1)} %copy-done.36), channel_id=1, source_target_pairs={{2,4},{3,5},{4,2},{5,3},{10,12},{11,13},{12,10},{13,11},{18,20},{1... | collective-permute-start | bytes 1769480 | tf_op jit(solution)/shard_map/ppermute | solution.py:108
  45.2 67.2 %collective-permute-start.5 = (bf16[1,256,1152]{2,1,0:T(8,128)(2,1)S(1)}, bf16[1,256,1152]{2,1,0:T(8,128)(2,1)S(1)}, u32[]{:S(2)}, u32[]{:S(2)}) collective-permute-start(bf16[1,256,1152]{2,1,0:T(8,128)(2,1)S(1)} %copy-done.38), channel_id=1, source_target_pairs={{0,5},{1,4},{2,7},{3,6},{4,1},{5,0},{6,3},{7,2},{8,13},{9,12},{10,... | collective-permute-start | bytes 1769480 | tf_op jit(solution)/shard_map/ppermute | solution.py:101
  57.4 55.1 %collective-permute-start.6 = (bf16[1,256,1152]{2,1,0:T(8,128)(2,1)S(1)}, bf16[1,256,1152]{2,1,0:T(8,128)(2,1)S(1)}, u32[]{:S(2)}, u32[]{:S(2)}) collective-permute-start(bf16[1,256,1152]{2,1,0:T(8,128)(2,1)S(1)} %copy-done.37), channel_id=1, source_target_pairs={{0,7},{1,6},{2,5},{3,4},{4,3},{5,2},{6,1},{7,0},{8,15},{9,14},{10,... | collective-permute-start | bytes 1769480 | tf_op jit(solution)/shard_map/ppermute | solution.py:101
  90.2 22.3 %collective-permute-start.8 = (bf16[1,128,1152]{2,1,0:T(8,128)(2,1)}, bf16[1,128,1152]{2,1,0:T(8,128)(2,1)S(1)}, u32[]{:S(2)}, u32[]{:S(2)}) collective-permute-start(bf16[1,128,1152]{2,1,0:T(8,128)(2,1)} %get-tuple-element.82), channel_id=1, source_target_pairs={{0,1},{1,0},{2,3},{3,2},{4,5},{5,4},{6,7},{7,6},{8,9},{9,8},{10,11... | collective-permute-start | bytes 884744 | tf_op jit(solution)/shard_map/ppermute | solution.py:101
  90.2 26.6 %collective-permute-start.9 = (bf16[1,128,1152]{2,1,0:T(8,128)(2,1)}, bf16[1,128,1152]{2,1,0:T(8,128)(2,1)S(1)}, u32[]{:S(2)}, u32[]{:S(2)}) collective-permute-start(bf16[1,128,1152]{2,1,0:T(8,128)(2,1)} %get-tuple-element.83), channel_id=1, source_target_pairs={{0,2},{1,3},{2,0},{3,1},{4,6},{5,7},{6,4},{7,5},{8,10},{9,11},{10,... | collective-permute-start | bytes 884744 | tf_op jit(solution)/shard_map/ppermute | solution.py:101
  127.0 33.4 %collective-permute-start.14 = (bf16[2,64,1152]{2,1,0:T(8,128)(2,1)}, bf16[2,64,1152]{2,1,0:T(8,128)(2,1)S(1)}, u32[]{:S(2)}, u32[]{:S(2)}) collective-permute-start(bf16[2,64,1152]{2,1,0:T(8,128)(2,1)} %get-tuple-element.92), channel_id=1, source_target_pairs={{0,4},{1,5},{2,6},{3,7},{4,0},{5,1},{6,2},{7,3},{8,12},{9,13},{10,... | collective-permute-start | bytes 884744 | tf_op jit(solution)/shard_map/ppermute | solution.py:86
  131.1 29.4 %collective-permute-start.15 = (bf16[2,64,1152]{2,1,0:T(8,128)(2,1)}, bf16[2,64,1152]{2,1,0:T(8,128)(2,1)S(1)}, u32[]{:S(2)}, u32[]{:S(2)}) collective-permute-start(bf16[2,64,1152]{2,1,0:T(8,128)(2,1)} %get-tuple-element.93), channel_id=1, source_target_pairs={{0,6},{1,7},{2,4},{3,5},{4,2},{5,3},{6,0},{7,1},{8,14},{9,15},{10,... | collective-permute-start | bytes 884744 | tf_op jit(solution)/shard_map/ppermute | solution.py:86
  168.4 126.8 %reduce-scatter.5.cloned.1.call-start = ((), (), s32[]{:S(2)}) async-start(), calls=%async_computation.3 | async-start | bytes 6635520 | tf_op jit(solution)/shard_map/reduce_scatter | solution.py:651
  170.0 22.0 %collective-permute-start.17 = (bf16[2,64,1152]{2,1,0:T(8,128)(2,1)S(1)}, bf16[2,64,1152]{2,1,0:T(8,128)(2,1)S(1)}, u32[]{:S(2)}, u32[]{:S(2)}) collective-permute-start(bf16[2,64,1152]{2,1,0:T(8,128)(2,1)S(1)} %copy-done.48), channel_id=1, source_target_pairs={{0,2},{1,3},{2,0},{3,1},{4,6},{5,7},{6,4},{7,5},{8,10},{9,11},{10,... | collective-permute-start | bytes 884744 | tf_op jit(solution)/shard_map/ppermute | solution.py:86
  172.4 25.5 %collective-permute-start.19 = (bf16[2,64,1152]{2,1,0:T(8,128)(2,1)S(1)}, bf16[2,64,1152]{2,1,0:T(8,128)(2,1)S(1)}, u32[]{:S(2)}, u32[]{:S(2)}) collective-permute-start(bf16[2,64,1152]{2,1,0:T(8,128)(2,1)S(1)} %copy-done.46), channel_id=1, source_target_pairs={{0,6},{1,7},{2,4},{3,5},{4,2},{5,3},{6,0},{7,1},{8,14},{9,15},{10,... | collective-permute-start | bytes 884744 | tf_op jit(solution)/shard_map/ppermute | solution.py:86
  211.6 21.8 %collective-permute-start.29 = (bf16[1,64,1152]{2,1,0:T(8,128)(2,1)}, bf16[1,64,1152]{2,1,0:T(8,128)(2,1)S(1)}, u32[]{:S(2)}, u32[]{:S(2)}) collective-permute-start(bf16[1,64,1152]{2,1,0:T(8,128)(2,1)} %get-tuple-element.123), channel_id=1, source_target_pairs={{0,4},{1,5},{2,6},{3,7},{4,0},{5,1},{6,2},{7,3},{8,12},{9,13},{10,... | collective-permute-start | bytes 442376 | tf_op jit(solution)/shard_map/ppermute | solution.py:101
  214.9 37.3 %collective-permute-start.31 = (bf16[1,64,1152]{2,1,0:T(8,128)(2,1)}, bf16[1,64,1152]{2,1,0:T(8,128)(2,1)S(1)}, u32[]{:S(2)}, u32[]{:S(2)}) collective-permute-start(bf16[1,64,1152]{2,1,0:T(8,128)(2,1)} %get-tuple-element.125), channel_id=1, source_target_pairs={{0,5},{1,4},{2,7},{3,6},{4,1},{5,0},{6,3},{7,2},{8,13},{9,12},{10,... | collective-permute-start | bytes 442376 | tf_op jit(solution)/shard_map/ppermute | solution.py:101
  228.1 32.1 %collective-permute-start.21 = (bf16[1,2,64,1152]{3,2,1,0:T(8,128)(2,1)}, bf16[1,2,64,1152]{3,2,1,0:T(8,128)(2,1)S(1)}, u32[]{:S(2)}, u32[]{:S(2)}) collective-permute-start(bf16[1,2,64,1152]{3,2,1,0:T(8,128)(2,1)} %get-tuple-element.112), channel_id=1, source_target_pairs={{0,6},{1,7},{2,4},{3,5},{4,2},{5,3},{6,0},{7,1},{8,14},{9,15},{10,... | collective-permute-start | bytes 884744 | tf_op jit(solution)/shard_map/ppermute | solution.py:101
  230.2 47.4 %collective-permute-start.22 = (bf16[1,2,64,1152]{3,2,1,0:T(8,128)(2,1)}, bf16[1,2,64,1152]{3,2,1,0:T(8,128)(2,1)S(1)}, u32[]{:S(2)}, u32[]{:S(2)}) collective-permute-start(bf16[1,2,64,1152]{3,2,1,0:T(8,128)(2,1)} %get-tuple-element.113), channel_id=1, source_target_pairs={{0,4},{1,5},{2,6},{3,7},{4,0},{5,1},{6,2},{7,3},{8,12},{9,13},{10,... | collective-permute-start | bytes 884744 | tf_op jit(solution)/shard_map/ppermute | solution.py:101
  233.4 22.0 %collective-permute-start.33 = (bf16[1,64,1152]{2,1,0:T(8,128)(2,1)S(1)}, bf16[1,64,1152]{2,1,0:T(8,128)(2,1)S(1)}, u32[]{:S(2)}, u32[]{:S(2)}) collective-permute-start(bf16[1,64,1152]{2,1,0:T(8,128)(2,1)S(1)} %copy-done.50), channel_id=1, source_target_pairs={{0,2},{1,3},{2,0},{3,1},{4,6},{5,7},{6,4},{7,5},{8,10},{9,11},{10,... | collective-permute-start | bytes 442376 | tf_op jit(solution)/shard_map/ppermute | solution.py:101
  253.2 28.6 %collective-permute-start.23 = (bf16[1,2,64,1152]{3,2,1,0:T(8,128)(2,1)}, bf16[1,2,64,1152]{3,2,1,0:T(8,128)(2,1)S(1)}, u32[]{:S(2)}, u32[]{:S(2)}) collective-permute-start(bf16[1,2,64,1152]{3,2,1,0:T(8,128)(2,1)} %get-tuple-element.114), channel_id=1, source_target_pairs={{0,7},{1,6},{2,5},{3,4},{4,3},{5,2},{6,1},{7,0},{8,15},{9,14},{10,... | collective-permute-start | bytes 884744 | tf_op jit(solution)/shard_map/ppermute | solution.py:101
  255.4 34.7 %collective-permute-start.24 = (bf16[1,2,64,1152]{3,2,1,0:T(8,128)(2,1)}, bf16[1,2,64,1152]{3,2,1,0:T(8,128)(2,1)S(1)}, u32[]{:S(2)}, u32[]{:S(2)}) collective-permute-start(bf16[1,2,64,1152]{3,2,1,0:T(8,128)(2,1)} %get-tuple-element.115), channel_id=1, source_target_pairs={{0,5},{1,4},{2,7},{3,6},{4,1},{5,0},{6,3},{7,2},{8,13},{9,12},{10,... | collective-permute-start | bytes 884744 | tf_op jit(solution)/shard_map/ppermute | solution.py:101
  255.5 34.6 %collective-permute-start.25 = (bf16[1,2,64,1152]{3,2,1,0:T(8,128)(2,1)}, bf16[1,2,64,1152]{3,2,1,0:T(8,128)(2,1)S(1)}, u32[]{:S(2)}, u32[]{:S(2)}) collective-permute-start(bf16[1,2,64,1152]{3,2,1,0:T(8,128)(2,1)} %get-tuple-element.116), channel_id=1, source_target_pairs={{0,3},{1,2},{2,1},{3,0},{4,7},{5,6},{6,5},{7,4},{8,11},{9,10},{10,... | collective-permute-start | bytes 884744 | tf_op jit(solution)/shard_map/ppermute | solution.py:101
  260.3 29.8 %collective-permute-start.26 = (bf16[1,2,64,1152]{3,2,1,0:T(8,128)(2,1)S(1)}, bf16[1,2,64,1152]{3,2,1,0:T(8,128)(2,1)S(1)}, u32[]{:S(2)}, u32[]{:S(2)}) collective-permute-start(bf16[1,2,64,1152]{3,2,1,0:T(8,128)(2,1)S(1)} %copy-done.44), channel_id=1, source_target_pairs={{0,2},{1,3},{2,0},{3,1},{4,6},{5,7},{6,4},{7,5},{8,10},{9,11},{10,... | collective-permute-start | bytes 884744 | tf_op jit(solution)/shard_map/ppermute | solution.py:101
  (65 other events, 804.7 us)
Sparse Core Ops, SparseCore 0:
  168.6 61.6 reduce-scatter.2
  233.2 61.9 reduce-scatter.4

commit v4 on v3

--- a/solution.py
+++ b/solution.py
@@ -148,22 +148,27 @@
                 (column == tok_ids).astype(F32).astype(BF)
             )
 
-    hits(me, range(count), mine_ref)
-    for half, source in enumerate((x_ref, y_ref)):
+    def send(source):
         rows = dot(mine_ref[...], source[...]).astype(BF)
         for k in range(count):
-            send_refs[k][0, half * slots : (half + 1) * slots, :] = rows[
-                k * slots : (k + 1) * slots
-            ]
-    hits(me ^ group, range(group), other_ref)
-
-    mine_row = table_ref[pl.ds(me, 1), :]
-    frames = (lax.broadcasted_iota(jnp.int32, (width, cap), 0) ^ me) * tok
-    key = ranked((mine_row >= frames) & (mine_row < frames + tok))
-    key_out[...] = key
-    for k in range(count):
-        found = jnp.where(key[k : k + 1, :] == slot_ids, gate_ref[...], 0.0)
-        gate_out[k * slots : (k + 1) * slots, :] = jnp.sum(found, axis=1, keepdims=True)
+            send_refs[k][0] = rows[k * slots : (k + 1) * slots]
+
+    @pl.when(pl.program_id(0) == 0)
+    def _():
+        hits(me, range(count), mine_ref)
+        send(x_ref)
+
+    @pl.when(pl.program_id(0) == 1)
+    def _():
+        send(y_ref)
+        hits(me ^ group, range(group), other_ref)
+        mine_row = table_ref[pl.ds(me, 1), :]
+        frames = (lax.broadcasted_iota(jnp.int32, (width, cap), 0) ^ me) * tok
+        key = ranked((mine_row >= frames) & (mine_row < frames + tok))
+        key_out[...] = key
+        for k in range(count):
+            found = jnp.where(key[k : k + 1, :] == slot_ids, gate_ref[...], 0.0)
+            gate_out[k * slots : (k + 1) * slots, :] = jnp.sum(found, axis=1, keepdims=True)
 
 
 def prep(me, table, gate_row, x, y, group):
@@ -179,11 +184,19 @@
             shape((count * slots, 1), F32),
             shape((count, cap), jnp.int32),
         ],
-        [SMEM, WHOLE, WHOLE, WHOLE, WHOLE],
+        [SMEM]
+        + [pl.BlockSpec(a.shape, lambda i: (0, 0)) for a in (table, gate_row, x, y)],
         [me, table, gate_row, x, y],
         flops=4 * count * slots * tok * width,
         nbytes=8 * count * slots * width,
-        out_specs=[WHOLE] * (count + 4),
+        grid=(2,),
+        out_specs=[pl.BlockSpec((1, slots, width), lambda i: (0, i, 0))] * count
+        + [
+            pl.BlockSpec((count * slots, tok), lambda i: (0, 0)),
+            pl.BlockSpec((group * slots, tok), lambda i: (0, 0)),
+            pl.BlockSpec((count * slots, 1), lambda i: (0, 0)),
+            pl.BlockSpec((count, cap), lambda i: (0, 0)),
+        ],
         scratch_shapes=[pltpu.VMEM((count, cap), jnp.int32)],
         name="prep",
     )

time: 306 us -> 306 us (level)
  transfers between devices with their start and end apart: 37 -> 37, of which waited for: 15 -> 16; matrix products, arithmetic and copies ran while one was open for 2% -> 2% of each run, Pallas kernels for 28% -> 28%
where the time goes in v4:
time: 306 us
  Pallas kernels  102 us (33%)
  waiting for transfers between devices  90.8 us (30%)
  starting transfers between devices  82.3 us (27%)
  between operations  14.5 us (5%)
  other arithmetic  8.11 us (3%)
  local copies, waits for them, and re-layouts  7.85 us (3%)
    pallas_call x13, Pallas kernels, call(): pl.pallas_call(run, out_shape=out_shape, in_specs=list(in_specs) + [ANY]...  102 us
    ppermute x26, waiting for transfers between devices, exchange_single(): lax.ppermute(b, 'dev', pairs[k])  74.8 us
    ppermute x26, starting transfers between devices, exchange_single(): lax.ppermute(b, 'dev', pairs[k])  66.9 us
    ppermute x6, waiting for transfers between devices, exchange_pairs(): lax.ppermute(pair, 'dev', [(d, d ^ 2 * i) for d in range(count)])  12.9 us
    ppermute x6, starting transfers between devices, exchange_pairs(): lax.ppermute(pair, 'dev', [(d, d ^ 2 * i) for d in range(count)])  11 us
    unnamed x104, local copies, waits for them, and re-layouts  6.78 us
  transfers between devices with their start and end apart: 37, of which 16 were waited for; matrix products, arithmetic and copies ran while one was open for 2% of the time, Pallas kernels for 28%

profile of v4, /device:TPU:0, one launch (start us, length us, event | category | flops | bytes accessed | tf_op | source)
XLA Modules:
  0.0 305.6 jit_solution(4314877778210249035)
XLA Ops:
  7.2 8.2 %prep.1 = (bf16[1,256,1152]{2,1,0:T(8,128)(2,1)}, bf16[1,256,1152]{2,1,0:T(8,128)(2,1)}, bf16[1,256,1152]{2,1,0:T(8,128)(2,1)}, bf16[1,256,1152]{2,1,0:T(8,128)(...) custom-call(s32[1]{0:T(128)} %bitcast.refs_0_, ...), custom_call_target="tpu_custom_call" | custom-call | flops 2415919104 | bytes 9437184 | tf_op jit(solution)/shard_map/prep/pallas_call | solution.py:42
  24.7 9.2 %probs.1 = (f32[4,16,128,128]{3,2,1,0:T(8,128)}, bf16[4,16,128,128]{3,2,1,0:T(8,128)(2,1)}) custom-call(bf16[8,64,1152]{2,1,0:T(8,128)(2,1)} %refs_3_.1, bf16[8,64,1152]{2,1,0:T(8,128)(2,1)} %refs_4_.1, bf16[1024,512]{1,0:T(8,128)(2,1)} %get-tuple-element.74.refs_2_.refs_1_), custom_call_target="tpu_custom_call" | custom-call | flops 603979776 | bytes 8650752 | tf_op jit(solution)/shard_map/probs/pallas_call | solution.py:42
  35.7 10.0 %collective-permute-done.1.refs_5_ = bf16[1,256,1152]{2,1,0:T(8,128)(2,1)S(1)} collective-permute-done((bf16[1,256,1152]{2,1,0:T(8,128)(2,1)}, bf16[1,256,1152]{2,1,0:T(8,128)(2,1)S(1)}, u32[]{:S(2)}, u32[]{:S(2)}) %collective-permute-start.1) | collective-permute-done | bytes 589856 | tf_op jit(solution)/shard_map/ppermute | solution.py:101
  46.7 11.1 %collective-permute-done.2.refs_6_ = bf16[1,256,1152]{2,1,0:T(8,128)(2,1)S(1)} collective-permute-done((bf16[1,256,1152]{2,1,0:T(8,128)(2,1)}, bf16[1,256,1152]{2,1,0:T(8,128)(2,1)S(1)}, u32[]{:S(2)}, u32[]{:S(2)}) %collective-permute-start.2) | collective-permute-done | bytes 589856 | tf_op jit(solution)/shard_map/ppermute | solution.py:101
  57.8 16.0 %collective-permute-start.6 = (bf16[1,256,1152]{2,1,0:T(8,128)(2,1)S(1)}, bf16[1,256,1152]{2,1,0:T(8,128)(2,1)S(1)}, u32[]{:S(2)}, u32[]{:S(2)}) collective-permute-start(bf16[1,256,1152]{2,1,0:T(8,128)(2,1)S(1)} %copy-done.37), channel_id=1, source_target_pairs={{0,7},{1,6},{2,5},{3,4},{4,3},{5,2},{6,1},{7,0},{8,15},{9,14},{10,... | collective-permute-start | bytes 1769480 | tf_op jit(solution)/shard_map/ppermute | solution.py:101
  74.9 15.7 %expert.2 = (bf16[1,128,1152]{2,1,0:T(8,128)(2,1)}, bf16[1,128,1152]{2,1,0:T(8,128)(2,1)}, bf16[1,128,1152]{2,1,0:T(8,128)(2,1)}, bf16[1,128,1152]{2,1,0:T(8,128...) custom-call(f32[512,1]{1,0:T(8,128)} %get-tuple-element.132.refs_0_,, ...), custom_call_target="tpu_custom_call" | custom-call | flops 8153726976 | bytes 20054016 | tf_op jit(solution)/shard_map/expert/pallas_call | solution.py:42
  90.8 22.1 %collective-permute-done.5.refs_7_.refs_4_ = bf16[1,256,1152]{2,1,0:T(8,128)(2,1)S(1)} collective-permute-done((bf16[1,256,1152]{2,1,0:T(8,128)(2,1)S(1)}, bf16[1,256,1152]{2,1,0:T(8,128)(2,1)S(1)}, u32[]{:S(2)}, u32[]{:S(2)}) %collective-permute-start.5) | collective-permute-done | bytes 589856 | tf_op jit(solution)/shard_map/ppermute | solution.py:101
  112.9 4.3 %collective-permute-done.9.refs_4_ = bf16[1,128,1152]{2,1,0:T(8,128)(2,1)S(1)} collective-permute-done((bf16[1,128,1152]{2,1,0:T(8,128)(2,1)}, bf16[1,128,1152]{2,1,0:T(8,128)(2,1)S(1)}, u32[]{:S(2)}, u32[]{:S(2)}) %collective-permute-start.9) | collective-permute-done | bytes 294944 | tf_op jit(solution)/shard_map/ppermute | solution.py:101
  117.3 5.7 %collective-permute-done.10.refs_5_ = bf16[1,128,1152]{2,1,0:T(8,128)(2,1)S(1)} collective-permute-done((bf16[1,128,1152]{2,1,0:T(8,128)(2,1)}, bf16[1,128,1152]{2,1,0:T(8,128)(2,1)S(1)}, u32[]{:S(2)}, u32[]{:S(2)}) %collective-permute-start.10) | collective-permute-done | bytes 294944 | tf_op jit(solution)/shard_map/ppermute | solution.py:101
  123.7 3.7 %combine.2 = (bf16[2,64,1152]{2,1,0:T(8,128)(2,1)}, bf16[2,64,1152]{2,1,0:T(8,128)(2,1)}, bf16[2,64,1152]{2,1,0:T(8,128)(2,1)}, bf16[2,64,1152]{2,1,0:T(8,128)(2,1)}) custom-call(s32[1]{0:T(128)} %bitcast.refs_0_, bf16[1024,512]{1,0:T(8,128)(2,1)} %get-tuple-element.74.refs_2_.refs_1_, bf16[1,128,1152]{2,1,0:T(8,128)(2,1)} %get-tuple-element.81.refs_2_, ...), custom_call_target="tpu_custom_call" | custom-call | flops 603979776 | bytes 3538944 | tf_op jit(solution)/shard_map/combine/pallas_call | solution.py:42
  127.4 4.1 %collective-permute-start.14 = (bf16[2,64,1152]{2,1,0:T(8,128)(2,1)}, bf16[2,64,1152]{2,1,0:T(8,128)(2,1)S(1)}, u32[]{:S(2)}, u32[]{:S(2)}) collective-permute-start(bf16[2,64,1152]{2,1,0:T(8,128)(2,1)} %get-tuple-element.92), channel_id=1, source_target_pairs={{0,4},{1,5},{2,6},{3,7},{4,0},{5,1},{6,2},{7,3},{8,12},{9,13},{10,... | collective-permute-start | bytes 884744 | tf_op jit(solution)/shard_map/ppermute | solution.py:86
  133.5 15.9 %expert.3 = (bf16[1,128,1152]{2,1,0:T(8,128)(2,1)}, bf16[1,128,1152]{2,1,0:T(8,128)(2,1)}, bf16[1,128,1152]{2,1,0:T(8,128)(2,1)}, bf16[1,128,1152]{2,1,0:T(8,128...) custom-call(f32[512,1]{1,0:T(8,128)} %get-tuple-element.133.refs_0_,, ...), custom_call_target="tpu_custom_call" | custom-call | flops 8153726976 | bytes 20054016 | tf_op jit(solution)/shard_map/expert/pallas_call | solution.py:42
  151.3 9.6 %weight_gradient.2.refs_8_ = bf16[1152,2304]{1,0:T(8,128)(2,1)} custom-call(bf16[512,1152]{1,0:T(8,128)(2,1)} %get-tuple-element.94.refs_0_, bf16[512,2304]{1,0:T(8,128)(2,1)} %get-tuple-element.95.refs_1_, bf16[512,1152]{1,0:T(8,128)(2,1)} %get-tuple-element.96.refs_2_, bf16[512,2304]{1,0:T(8,128)(2,1)} %get-tuple-element.97.refs_3_), custom_call_target="tpu_custom_call" | custom-call | flops 5435817984 | bytes 5308416 | tf_op jit(solution)/shard_map/weight_gradient/pallas_call | solution.py:42
  160.9 3.9 %collective-permute-done.13.refs_5_ = bf16[1,128,1152]{2,1,0:T(8,128)(2,1)S(1)} collective-permute-done((bf16[1,128,1152]{2,1,0:T(8,128)(2,1)}, bf16[1,128,1152]{2,1,0:T(8,128)(2,1)S(1)}, u32[]{:S(2)}, u32[]{:S(2)}) %collective-permute-start.13) | collective-permute-done | bytes 294944 | tf_op jit(solution)/shard_map/ppermute | solution.py:101
  174.7 10.7 %weight_gradient.3.refs_8_ = bf16[2304,1152]{1,0:T(8,128)(2,1)} custom-call(bf16[512,2304]{1,0:T(8,128)(2,1)} %get-tuple-element.104.refs_0_, bf16[512,1152]{1,0:T(8,128)(2,1)} %get-tuple-element.105.refs_1_, bf16[512,2304]{1,0:T(8,128)(2,1)} %get-tuple-element.106.refs_2_, bf16[512,1152]{1,0:T(8,128)(2,1)} %get-tuple-element.107.refs_3_, ...), custom_call_target="tpu_custom_call" | custom-call | flops 5435817984 | bytes 5308416 | tf_op jit(solution)/shard_map/weight_gradient/pallas_call | solution.py:42
  185.9 6.4 %collective-permute-done.17.refs_5_.refs_8_ = bf16[2,64,1152]{2,1,0:T(8,128)(2,1)S(1)} collective-permute-done((bf16[2,64,1152]{2,1,0:T(8,128)(2,1)S(1)}, bf16[2,64,1152]{2,1,0:T(8,128)(2,1)S(1)}, u32[]{:S(2)}, u32[]{:S(2)}) %collective-permute-start.17) | collective-permute-done | bytes 294944 | tf_op jit(solution)/shard_map/ppermute | solution.py:86
  192.4 5.9 %collective-permute-done.19.refs_7_.refs_10_ = bf16[2,64,1152]{2,1,0:T(8,128)(2,1)S(1)} collective-permute-done((bf16[2,64,1152]{2,1,0:T(8,128)(2,1)S(1)}, bf16[2,64,1152]{2,1,0:T(8,128)(2,1)S(1)}, u32[]{:S(2)}, u32[]{:S(2)}) %collective-permute-start.19) | collective-permute-done | bytes 294944 | tf_op jit(solution)/shard_map/ppermute | solution.py:86
  205.3 4.7 %value_gradient.1 = (bf16[1,64,1152]{2,1,0:T(8,128)(2,1)}, bf16[1,64,1152]{2,1,0:T(8,128)(2,1)}, bf16[1,64,1152]{2,1,0:T(8,128)(2,1)}, bf16[1,64,1152]{2,1,0:T(8...) custom-call(s32[1]{0:T(128)} %bitcast.refs_0_, ...), custom_call_target="tpu_custom_call" | custom-call | flops 301989888 | bytes 4718592 | tf_op jit(solution)/shard_map/value_gradient/pallas_call | solution.py:42
  215.6 12.9 %pair_gradients.1 = (bf16[1,2,64,1152]{3,2,1,0:T(8,128)(2,1)}, bf16[1,2,64,1152]{3,2,1,0:T(8,128)(2,1)}, bf16[1,2,64,1152]{3,2,1,0:T(8,128)(2,1)}, bf16[1,2,64,1...) custom-call(s32[1]{0:T(128)} %bitcast.refs_0_, ...), custom_call_target="tpu_custom_call" | custom-call | flops 905969664 | bytes 9437184 | tf_op jit(solution)/shard_map/pair_gradients/pallas_call | solution.py:42
  233.8 16.2 %collective-permute-start.33 = (bf16[1,64,1152]{2,1,0:T(8,128)(2,1)S(1)}, bf16[1,64,1152]{2,1,0:T(8,128)(2,1)S(1)}, u32[]{:S(2)}, u32[]{:S(2)}) collective-permute-start(bf16[1,64,1152]{2,1,0:T(8,128)(2,1)S(1)} %copy-done.50), channel_id=1, source_target_pairs={{0,2},{1,3},{2,0},{3,1},{4,6},{5,7},{6,4},{7,5},{8,10},{9,11},{10,... | collective-permute-start | bytes 442376 | tf_op jit(solution)/shard_map/ppermute | solution.py:101
  260.7 11.3 %collective-permute-start.26 = (bf16[1,2,64,1152]{3,2,1,0:T(8,128)(2,1)S(1)}, bf16[1,2,64,1152]{3,2,1,0:T(8,128)(2,1)S(1)}, u32[]{:S(2)}, u32[]{:S(2)}) collective-permute-start(bf16[1,2,64,1152]{3,2,1,0:T(8,128)(2,1)S(1)} %copy-done.44), channel_id=1, source_target_pairs={{0,2},{1,3},{2,0},{3,1},{4,6},{5,7},{6,4},{7,5},{8,10},{9,11},{10,... | collective-permute-start | bytes 884744 | tf_op jit(solution)/shard_map/ppermute | solution.py:101
  272.0 6.1 %collective-permute-done.22.refs_2_ = bf16[1,2,64,1152]{3,2,1,0:T(8,128)(2,1)S(1)} collective-permute-done((bf16[1,2,64,1152]{3,2,1,0:T(8,128)(2,1)}, bf16[1,2,64,1152]{3,2,1,0:T(8,128)(2,1)S(1)}, u32[]{:S(2)}, u32[]{:S(2)}) %collective-permute-start.22) | collective-permute-done | bytes 294944 | tf_op jit(solution)/shard_map/ppermute | solution.py:101
  278.1 4.2 %fusion = (f32[288,2304]{1,0:T(8,128)}, f32[1,288,2304]{2,1,0:T(8,128)}) fusion(bf16[288,2304]{1,0:T(8,128)(2,1)} %reduce-scatter.3.cloned.1.call-done), kind=kLoop, calls=%fused_computation.5 | loop fusion | flops 663552 | bytes 6635520 | tf_op jit(solution)/shard_map/convert_element_type | solution.py:654
  282.3 8.3 %collective-permute-done.24.refs_4_ = bf16[1,2,64,1152]{3,2,1,0:T(8,128)(2,1)S(1)} collective-permute-done((bf16[1,2,64,1152]{3,2,1,0:T(8,128)(2,1)}, bf16[1,2,64,1152]{3,2,1,0:T(8,128)(2,1)S(1)}, u32[]{:S(2)}, u32[]{:S(2)}) %collective-permute-start.24) | collective-permute-done | bytes 294944 | tf_op jit(solution)/shard_map/ppermute | solution.py:101
  (176 shorter events, 64.9 us)
Async XLA Ops:
  7.2 270.9 %reduce-scatter.3.cloned.1.call-start = ((), (), s32[]{:S(2)}) async-start(), calls=%async_computation.2 | async-start | bytes 6635520 | tf_op jit(solution)/shard_map/reduce_scatter | solution.py:654
  16.0 29.7 %collective-permute-start.1 = (bf16[1,256,1152]{2,1,0:T(8,128)(2,1)}, bf16[1,256,1152]{2,1,0:T(8,128)(2,1)S(1)}, u32[]{:S(2)}, u32[]{:S(2)}) collective-permute-start(bf16[1,256,1152]{2,1,0:T(8,128)(2,1)} %get-tuple-element.72), channel_id=1, source_target_pairs={{0,2},{1,3},{2,0},{3,1},{4,6},{5,7},{6,4},{7,5},{8,10},{9,11},{10,... | collective-permute-start | bytes 1769480 | tf_op jit(solution)/shard_map/ppermute | solution.py:101
  18.6 39.1 %collective-permute-start.2 = (bf16[1,256,1152]{2,1,0:T(8,128)(2,1)}, bf16[1,256,1152]{2,1,0:T(8,128)(2,1)S(1)}, u32[]{:S(2)}, u32[]{:S(2)}) collective-permute-start(bf16[1,256,1152]{2,1,0:T(8,128)(2,1)} %get-tuple-element.73), channel_id=1, source_target_pairs={{0,3},{1,2},{2,1},{3,0},{4,7},{5,6},{6,5},{7,4},{8,11},{9,10},{10,... | collective-permute-start | bytes 1769480 | tf_op jit(solution)/shard_map/ppermute | solution.py:101
  18.7 55.1 %collective-permute-start.3 = (bf16[1,256,1152]{2,1,0:T(8,128)(2,1)}, bf16[1,256,1152]{2,1,0:T(8,128)(2,1)S(1)}, u32[]{:S(2)}, u32[]{:S(2)}) collective-permute-start(bf16[1,256,1152]{2,1,0:T(8,128)(2,1)} %get-tuple-element.76), channel_id=1, source_target_pairs={{0,4},{1,5},{2,6},{3,7},{4,0},{5,1},{6,2},{7,3},{8,12},{9,13},{10,... | collective-permute-start | bytes 1769480 | tf_op jit(solution)/shard_map/ppermute | solution.py:101
  21.5 52.4 %collective-permute-start.4 = (bf16[1,256,1152]{2,1,0:T(8,128)(2,1)}, bf16[1,256,1152]{2,1,0:T(8,128)(2,1)S(1)}, u32[]{:S(2)}, u32[]{:S(2)}) collective-permute-start(bf16[1,256,1152]{2,1,0:T(8,128)(2,1)} %get-tuple-element.77), channel_id=1, source_target_pairs={{0,6},{1,7},{6,0},{7,1},{8,14},{9,15},{14,8},{15,9},{16,22},{17,23... | collective-permute-start | bytes 1769480 | tf_op jit(solution)/shard_map/ppermute | solution.py:108
  34.8 78.1 %collective-permute-start.7 = (bf16[1,256,1152]{2,1,0:T(8,128)(2,1)S(1)}, bf16[1,256,1152]{2,1,0:T(8,128)(2,1)S(1)}, u32[]{:S(2)}, u32[]{:S(2)}) collective-permute-start(bf16[1,256,1152]{2,1,0:T(8,128)(2,1)S(1)} %copy-done.36), channel_id=1, source_target_pairs={{2,4},{3,5},{4,2},{5,3},{10,12},{11,13},{12,10},{13,11},{18,20},{1... | collective-permute-start | bytes 1769480 | tf_op jit(solution)/shard_map/ppermute | solution.py:108
  45.7 67.2 %collective-permute-start.5 = (bf16[1,256,1152]{2,1,0:T(8,128)(2,1)S(1)}, bf16[1,256,1152]{2,1,0:T(8,128)(2,1)S(1)}, u32[]{:S(2)}, u32[]{:S(2)}) collective-permute-start(bf16[1,256,1152]{2,1,0:T(8,128)(2,1)S(1)} %copy-done.38), channel_id=1, source_target_pairs={{0,5},{1,4},{2,7},{3,6},{4,1},{5,0},{6,3},{7,2},{8,13},{9,12},{10,... | collective-permute-start | bytes 1769480 | tf_op jit(solution)/shard_map/ppermute | solution.py:101
  57.8 55.1 %collective-permute-start.6 = (bf16[1,256,1152]{2,1,0:T(8,128)(2,1)S(1)}, bf16[1,256,1152]{2,1,0:T(8,128)(2,1)S(1)}, u32[]{:S(2)}, u32[]{:S(2)}) collective-permute-start(bf16[1,256,1152]{2,1,0:T(8,128)(2,1)S(1)} %copy-done.37), channel_id=1, source_target_pairs={{0,7},{1,6},{2,5},{3,4},{4,3},{5,2},{6,1},{7,0},{8,15},{9,14},{10,... | collective-permute-start | bytes 1769480 | tf_op jit(solution)/shard_map/ppermute | solution.py:101
  90.6 22.3 %collective-permute-start.8 = (bf16[1,128,1152]{2,1,0:T(8,128)(2,1)}, bf16[1,128,1152]{2,1,0:T(8,128)(2,1)S(1)}, u32[]{:S(2)}, u32[]{:S(2)}) collective-permute-start(bf16[1,128,1152]{2,1,0:T(8,128)(2,1)} %get-tuple-element.82), channel_id=1, source_target_pairs={{0,1},{1,0},{2,3},{3,2},{4,5},{5,4},{6,7},{7,6},{8,9},{9,8},{10,11... | collective-permute-start | bytes 884744 | tf_op jit(solution)/shard_map/ppermute | solution.py:101
  90.7 26.6 %collective-permute-start.9 = (bf16[1,128,1152]{2,1,0:T(8,128)(2,1)}, bf16[1,128,1152]{2,1,0:T(8,128)(2,1)S(1)}, u32[]{:S(2)}, u32[]{:S(2)}) collective-permute-start(bf16[1,128,1152]{2,1,0:T(8,128)(2,1)} %get-tuple-element.83), channel_id=1, source_target_pairs={{0,2},{1,3},{2,0},{3,1},{4,6},{5,7},{6,4},{7,5},{8,10},{9,11},{10,... | collective-permute-start | bytes 884744 | tf_op jit(solution)/shard_map/ppermute | solution.py:101
  127.4 33.5 %collective-permute-start.14 = (bf16[2,64,1152]{2,1,0:T(8,128)(2,1)}, bf16[2,64,1152]{2,1,0:T(8,128)(2,1)S(1)}, u32[]{:S(2)}, u32[]{:S(2)}) collective-permute-start(bf16[2,64,1152]{2,1,0:T(8,128)(2,1)} %get-tuple-element.92), channel_id=1, source_target_pairs={{0,4},{1,5},{2,6},{3,7},{4,0},{5,1},{6,2},{7,3},{8,12},{9,13},{10,... | collective-permute-start | bytes 884744 | tf_op jit(solution)/shard_map/ppermute | solution.py:86
  131.5 29.4 %collective-permute-start.15 = (bf16[2,64,1152]{2,1,0:T(8,128)(2,1)}, bf16[2,64,1152]{2,1,0:T(8,128)(2,1)S(1)}, u32[]{:S(2)}, u32[]{:S(2)}) collective-permute-start(bf16[2,64,1152]{2,1,0:T(8,128)(2,1)} %get-tuple-element.93), channel_id=1, source_target_pairs={{0,6},{1,7},{2,4},{3,5},{4,2},{5,3},{6,0},{7,1},{8,14},{9,15},{10,... | collective-permute-start | bytes 884744 | tf_op jit(solution)/shard_map/ppermute | solution.py:86
  168.9 126.8 %reduce-scatter.5.cloned.1.call-start = ((), (), s32[]{:S(2)}) async-start(), calls=%async_computation.3 | async-start | bytes 6635520 | tf_op jit(solution)/shard_map/reduce_scatter | solution.py:664
  170.3 22.1 %collective-permute-start.17 = (bf16[2,64,1152]{2,1,0:T(8,128)(2,1)S(1)}, bf16[2,64,1152]{2,1,0:T(8,128)(2,1)S(1)}, u32[]{:S(2)}, u32[]{:S(2)}) collective-permute-start(bf16[2,64,1152]{2,1,0:T(8,128)(2,1)S(1)} %copy-done.48), channel_id=1, source_target_pairs={{0,2},{1,3},{2,0},{3,1},{4,6},{5,7},{6,4},{7,5},{8,10},{9,11},{10,... | collective-permute-start | bytes 884744 | tf_op jit(solution)/shard_map/ppermute | solution.py:86
  172.8 25.5 %collective-permute-start.19 = (bf16[2,64,1152]{2,1,0:T(8,128)(2,1)S(1)}, bf16[2,64,1152]{2,1,0:T(8,128)(2,1)S(1)}, u32[]{:S(2)}, u32[]{:S(2)}) collective-permute-start(bf16[2,64,1152]{2,1,0:T(8,128)(2,1)S(1)} %copy-done.46), channel_id=1, source_target_pairs={{0,6},{1,7},{2,4},{3,5},{4,2},{5,3},{6,0},{7,1},{8,14},{9,15},{10,... | collective-permute-start | bytes 884744 | tf_op jit(solution)/shard_map/ppermute | solution.py:86
  212.0 21.8 %collective-permute-start.29 = (bf16[1,64,1152]{2,1,0:T(8,128)(2,1)}, bf16[1,64,1152]{2,1,0:T(8,128)(2,1)S(1)}, u32[]{:S(2)}, u32[]{:S(2)}) collective-permute-start(bf16[1,64,1152]{2,1,0:T(8,128)(2,1)} %get-tuple-element.123), channel_id=1, source_target_pairs={{0,4},{1,5},{2,6},{3,7},{4,0},{5,1},{6,2},{7,3},{8,12},{9,13},{10,... | collective-permute-start | bytes 442376 | tf_op jit(solution)/shard_map/ppermute | solution.py:101
  215.4 37.3 %collective-permute-start.31 = (bf16[1,64,1152]{2,1,0:T(8,128)(2,1)}, bf16[1,64,1152]{2,1,0:T(8,128)(2,1)S(1)}, u32[]{:S(2)}, u32[]{:S(2)}) collective-permute-start(bf16[1,64,1152]{2,1,0:T(8,128)(2,1)} %get-tuple-element.125), channel_id=1, source_target_pairs={{0,5},{1,4},{2,7},{3,6},{4,1},{5,0},{6,3},{7,2},{8,13},{9,12},{10,... | collective-permute-start | bytes 442376 | tf_op jit(solution)/shard_map/ppermute | solution.py:101
  228.6 32.1 %collective-permute-start.21 = (bf16[1,2,64,1152]{3,2,1,0:T(8,128)(2,1)}, bf16[1,2,64,1152]{3,2,1,0:T(8,128)(2,1)S(1)}, u32[]{:S(2)}, u32[]{:S(2)}) collective-permute-start(bf16[1,2,64,1152]{3,2,1,0:T(8,128)(2,1)} %get-tuple-element.112), channel_id=1, source_target_pairs={{0,6},{1,7},{2,4},{3,5},{4,2},{5,3},{6,0},{7,1},{8,14},{9,15},{10,... | collective-permute-start | bytes 884744 | tf_op jit(solution)/shard_map/ppermute | solution.py:101
  230.6 47.4 %collective-permute-start.22 = (bf16[1,2,64,1152]{3,2,1,0:T(8,128)(2,1)}, bf16[1,2,64,1152]{3,2,1,0:T(8,128)(2,1)S(1)}, u32[]{:S(2)}, u32[]{:S(2)}) collective-permute-start(bf16[1,2,64,1152]{3,2,1,0:T(8,128)(2,1)} %get-tuple-element.113), channel_id=1, source_target_pairs={{0,4},{1,5},{2,6},{3,7},{4,0},{5,1},{6,2},{7,3},{8,12},{9,13},{10,... | collective-permute-start | bytes 884744 | tf_op jit(solution)/shard_map/ppermute | solution.py:101
  233.8 22.0 %collective-permute-start.33 = (bf16[1,64,1152]{2,1,0:T(8,128)(2,1)S(1)}, bf16[1,64,1152]{2,1,0:T(8,128)(2,1)S(1)}, u32[]{:S(2)}, u32[]{:S(2)}) collective-permute-start(bf16[1,64,1152]{2,1,0:T(8,128)(2,1)S(1)} %copy-done.50), channel_id=1, source_target_pairs={{0,2},{1,3},{2,0},{3,1},{4,6},{5,7},{6,4},{7,5},{8,10},{9,11},{10,... | collective-permute-start | bytes 442376 | tf_op jit(solution)/shard_map/ppermute | solution.py:101
  253.7 28.6 %collective-permute-start.23 = (bf16[1,2,64,1152]{3,2,1,0:T(8,128)(2,1)}, bf16[1,2,64,1152]{3,2,1,0:T(8,128)(2,1)S(1)}, u32[]{:S(2)}, u32[]{:S(2)}) collective-permute-start(bf16[1,2,64,1152]{3,2,1,0:T(8,128)(2,1)} %get-tuple-element.114), channel_id=1, source_target_pairs={{0,7},{1,6},{2,5},{3,4},{4,3},{5,2},{6,1},{7,0},{8,15},{9,14},{10,... | collective-permute-start | bytes 884744 | tf_op jit(solution)/shard_map/ppermute | solution.py:101
  255.8 34.7 %collective-permute-start.24 = (bf16[1,2,64,1152]{3,2,1,0:T(8,128)(2,1)}, bf16[1,2,64,1152]{3,2,1,0:T(8,128)(2,1)S(1)}, u32[]{:S(2)}, u32[]{:S(2)}) collective-permute-start(bf16[1,2,64,1152]{3,2,1,0:T(8,128)(2,1)} %get-tuple-element.115), channel_id=1, source_target_pairs={{0,5},{1,4},{2,7},{3,6},{4,1},{5,0},{6,3},{7,2},{8,13},{9,12},{10,... | collective-permute-start | bytes 884744 | tf_op jit(solution)/shard_map/ppermute | solution.py:101
  255.9 34.6 %collective-permute-start.25 = (bf16[1,2,64,1152]{3,2,1,0:T(8,128)(2,1)}, bf16[1,2,64,1152]{3,2,1,0:T(8,128)(2,1)S(1)}, u32[]{:S(2)}, u32[]{:S(2)}) collective-permute-start(bf16[1,2,64,1152]{3,2,1,0:T(8,128)(2,1)} %get-tuple-element.116), channel_id=1, source_target_pairs={{0,3},{1,2},{2,1},{3,0},{4,7},{5,6},{6,5},{7,4},{8,11},{9,10},{10,... | collective-permute-start | bytes 884744 | tf_op jit(solution)/shard_map/ppermute | solution.py:101
  260.7 29.9 %collective-permute-start.26 = (bf16[1,2,64,1152]{3,2,1,0:T(8,128)(2,1)S(1)}, bf16[1,2,64,1152]{3,2,1,0:T(8,128)(2,1)S(1)}, u32[]{:S(2)}, u32[]{:S(2)}) collective-permute-start(bf16[1,2,64,1152]{3,2,1,0:T(8,128)(2,1)S(1)} %copy-done.44), channel_id=1, source_target_pairs={{0,2},{1,3},{2,0},{3,1},{4,6},{5,7},{6,4},{7,5},{8,10},{9,11},{10,... | collective-permute-start | bytes 884744 | tf_op jit(solution)/shard_map/ppermute | solution.py:101
  (65 other events, 804.4 us)
Sparse Core Ops, SparseCore 0:
  169.0 61.6 reduce-scatter.2
  233.7 61.9 reduce-scatter.4

commit v5 on v3

--- a/solution.py
+++ b/solution.py
@@ -310,6 +310,43 @@
     )
 
 
+def release_kernel(token_ref):
+    token_ref[...] = jnp.zeros_like(token_ref)
+
+
+def release(term, after):
+    return call(
+        release_kernel,
+        [shape((8, LANES), F32)],
+        [],
+        [],
+        out_specs=[WHOLE],
+        after=after,
+        carry=term,
+        name="release",
+    )
+
+
+def widen_kernel(term_ref, out_ref):
+    out_ref[...] = term_ref[...].astype(F32)
+
+
+def widen(term):
+    rows, width = term.shape
+    tile = rows // 4 if rows % 64 == 0 else rows
+    block = pl.BlockSpec((tile, width), lambda i: (i, 0))
+    return call(
+        widen_kernel,
+        shape(term.shape, F32),
+        [block],
+        [term],
+        nbytes=6 * rows * width,
+        grid=(rows // tile,),
+        out_specs=block,
+        name="widen",
+    )
+
+
 def combine_kernel(count, parts, plus, me_ref, hit_ref, *refs):
     rows = jnp.concatenate([ref[...] for ref in refs[:parts]], axis=0)
     refs = refs[parts:]
@@ -417,7 +454,7 @@
 
 
 def meet_kernel(chips, *refs):
-    near, far, out_ref = refs[:chips], refs[chips : 2 * chips], refs[2 * chips]
+    far, near, out_ref = refs[:chips][::-1], refs[chips : 2 * chips][::-1], refs[2 * chips]
     for i in range(chips):
         value = near[i][...].astype(F32) + far[i ^ (chips // 2)][...].astype(F32)
         out_ref[i] = value.astype(BF)
@@ -431,7 +468,7 @@
         functools.partial(meet_kernel, chips),
         [shape((chips, piece, width))],
         [spec] * (2 * chips),
-        [*near, *far],
+        [*far[::-1], *near[::-1]],
         nbytes=6 * chips * piece * width,
         carry=carry,
         grid=(1,),
@@ -635,10 +672,9 @@
     x_far, scaled_far, act_far, pre_far, sums_far = rest_far
     crossed = grad_near[2:]
     in_term = weight_gradient((x_near, pre_near), (x_far, pre_far), False)
-    *send_far, in_term = combine(
-        me, hit_other, back_far, None, count, after=crossed, carry=in_term
-    )
+    token, in_term = release(in_term, [*arrays(back_far), *crossed])
     in_share = lax.psum_scatter(in_term, "slab", scatter_dimension=0, tiled=True).astype(F32)
+    send_far = combine(me, hit_other, back_far, None, count, after=[token])
     grad_far = pairs(send_far)
     out_term = weight_gradient(
         (scaled_near, act_near), (scaled_far, act_far), True, after=send_far[:1]
@@ -648,7 +684,7 @@
     gate_grad = jnp.sum(jnp.where(key[:, None, :] == slot_ids, slot_sums, 0.0), axis=(0, 1))
 
     odd, out_term = meet(grad_near, grad_far, out_term)
-    out_share = lax.psum_scatter(out_term, "slab", scatter_dimension=0, tiled=True).astype(F32)
+    out_share = widen(lax.psum_scatter(out_term, "slab", scatter_dimension=0, tiled=True))
     odd = other_core(odd, count)
     value_send, grad_attn = value_gradient(me, turned, odd, grad_near, grad_far, count)
     pair_send = pair_gradients(me, probs, grad_attn, query_rows, key_rows, value_rows, count)

time: 306 us -> 305 us (level)
  Pallas kernels: 102 us -> 106 us
  starting transfers between devices: 82.3 us -> 78.9 us
    pallas_call x13 -> x15, Pallas kernels: 102 us -> 106 us  [call(): pl.pallas_call(run, out_shape=out_shape, in_specs=list(in_specs) + [ANY]...]
    ppermute x26, starting transfers between devices: 66.9 us -> 63.2 us  [exchange_single(): lax.ppermute(b, 'dev', pairs[k])]
    unnamed x104 -> x98, local copies, waits for them, and re-layouts: 6.78 us -> 7.49 us
  transfers between devices with their start and end apart: 37 -> 37, of which waited for: 15 -> 13; matrix products, arithmetic and copies ran while one was open for 2% -> 2% of each run, Pallas kernels for 28% -> 29%
where the time goes in v5:
time: 305 us
  Pallas kernels  106 us (35%)
  waiting for transfers between devices  92.2 us (30%)
  starting transfers between devices  78.9 us (26%)
  between operations  14.5 us (5%)
  local copies, waits for them, and re-layouts  8.6 us (3%)
  other arithmetic  5.07 us (2%)
    pallas_call x15, Pallas kernels, call(): pl.pallas_call(run, out_shape=out_shape, in_specs=list(in_specs) + [ANY]...  106 us
    ppermute x26, waiting for transfers between devices, exchange_single(): lax.ppermute(b, 'dev', pairs[k])  75.6 us
    ppermute x26, starting transfers between devices, exchange_single(): lax.ppermute(b, 'dev', pairs[k])  63.2 us
    ppermute x6, waiting for transfers between devices, exchange_pairs(): lax.ppermute(pair, 'dev', [(d, d ^ 2 * i) for d in range(count)])  14.6 us
    ppermute x6, starting transfers between devices, exchange_pairs(): lax.ppermute(pair, 'dev', [(d, d ^ 2 * i) for d in range(count)])  11.2 us
    unnamed x98, local copies, waits for them, and re-layouts  7.49 us
  transfers between devices with their start and end apart: 37, of which 13 were waited for; matrix products, arithmetic and copies ran while one was open for 2% of the time, Pallas kernels for 29%

profile of v5, /device:TPU:0, one launch (start us, length us, event | category | flops | bytes accessed | tf_op | source)
XLA Modules:
  0.0 304.8 jit_solution(10907041489590563800)
XLA Ops:
  7.2 7.8 %prep.1 = (bf16[1,256,1152]{2,1,0:T(8,128)(2,1)}, bf16[1,256,1152]{2,1,0:T(8,128)(2,1)}, bf16[1,256,1152]{2,1,0:T(8,128)(2,1)}, bf16[1,256,1152]{2,1,0:T(8,128)(...) custom-call(s32[1]{0:T(128)} %bitcast.refs_0_, ...), custom_call_target="tpu_custom_call" | custom-call | flops 2415919104 | bytes 9437184 | tf_op jit(solution)/shard_map/prep/pallas_call | solution.py:42
  24.3 9.2 %probs.1 = (f32[4,16,128,128]{3,2,1,0:T(8,128)}, bf16[4,16,128,128]{3,2,1,0:T(8,128)(2,1)}) custom-call(bf16[8,64,1152]{2,1,0:T(8,128)(2,1)} %refs_3_.1, bf16[8,64,1152]{2,1,0:T(8,128)(2,1)} %refs_4_.1, bf16[1024,512]{1,0:T(8,128)(2,1)} %get-tuple-element.75.refs_2_.refs_1_), custom_call_target="tpu_custom_call" | custom-call | flops 603979776 | bytes 8650752 | tf_op jit(solution)/shard_map/probs/pallas_call | solution.py:42
  35.3 9.9 %collective-permute-done.1.refs_5_ = bf16[1,256,1152]{2,1,0:T(8,128)(2,1)S(1)} collective-permute-done((bf16[1,256,1152]{2,1,0:T(8,128)(2,1)}, bf16[1,256,1152]{2,1,0:T(8,128)(2,1)S(1)}, u32[]{:S(2)}, u32[]{:S(2)}) %collective-permute-start.1) | collective-permute-done | bytes 589856 | tf_op jit(solution)/shard_map/ppermute | solution.py:101
  46.2 11.1 %collective-permute-done.2.refs_6_ = bf16[1,256,1152]{2,1,0:T(8,128)(2,1)S(1)} collective-permute-done((bf16[1,256,1152]{2,1,0:T(8,128)(2,1)}, bf16[1,256,1152]{2,1,0:T(8,128)(2,1)S(1)}, u32[]{:S(2)}, u32[]{:S(2)}) %collective-permute-start.2) | collective-permute-done | bytes 589856 | tf_op jit(solution)/shard_map/ppermute | solution.py:101
  57.3 16.0 %collective-permute-start.6 = (bf16[1,256,1152]{2,1,0:T(8,128)(2,1)S(1)}, bf16[1,256,1152]{2,1,0:T(8,128)(2,1)S(1)}, u32[]{:S(2)}, u32[]{:S(2)}) collective-permute-start(bf16[1,256,1152]{2,1,0:T(8,128)(2,1)S(1)} %copy-done.37), channel_id=1, source_target_pairs={{0,7},{1,6},{2,5},{3,4},{4,3},{5,2},{6,1},{7,0},{8,15},{9,14},{10,... | collective-permute-start | bytes 1769480 | tf_op jit(solution)/shard_map/ppermute | solution.py:101
  74.4 15.7 %expert.2 = (bf16[1,128,1152]{2,1,0:T(8,128)(2,1)}, bf16[1,128,1152]{2,1,0:T(8,128)(2,1)}, bf16[1,128,1152]{2,1,0:T(8,128)(2,1)}, bf16[1,128,1152]{2,1,0:T(8,128...) custom-call(f32[512,1]{1,0:T(8,128)} %get-tuple-element.134.refs_0_,, ...), custom_call_target="tpu_custom_call" | custom-call | flops 8153726976 | bytes 20054016 | tf_op jit(solution)/shard_map/expert/pallas_call | solution.py:42
  90.2 22.2 %collective-permute-done.5.refs_7_.refs_4_ = bf16[1,256,1152]{2,1,0:T(8,128)(2,1)S(1)} collective-permute-done((bf16[1,256,1152]{2,1,0:T(8,128)(2,1)S(1)}, bf16[1,256,1152]{2,1,0:T(8,128)(2,1)S(1)}, u32[]{:S(2)}, u32[]{:S(2)}) %collective-permute-start.5) | collective-permute-done | bytes 589856 | tf_op jit(solution)/shard_map/ppermute | solution.py:101
  112.5 4.3 %collective-permute-done.9.refs_4_ = bf16[1,128,1152]{2,1,0:T(8,128)(2,1)S(1)} collective-permute-done((bf16[1,128,1152]{2,1,0:T(8,128)(2,1)}, bf16[1,128,1152]{2,1,0:T(8,128)(2,1)S(1)}, u32[]{:S(2)}, u32[]{:S(2)}) %collective-permute-start.9) | collective-permute-done | bytes 294944 | tf_op jit(solution)/shard_map/ppermute | solution.py:101
  116.8 5.6 %collective-permute-done.10.refs_5_ = bf16[1,128,1152]{2,1,0:T(8,128)(2,1)S(1)} collective-permute-done((bf16[1,128,1152]{2,1,0:T(8,128)(2,1)}, bf16[1,128,1152]{2,1,0:T(8,128)(2,1)S(1)}, u32[]{:S(2)}, u32[]{:S(2)}) %collective-permute-start.10) | collective-permute-done | bytes 294944 | tf_op jit(solution)/shard_map/ppermute | solution.py:101
  123.1 3.8 %combine.2 = (bf16[2,64,1152]{2,1,0:T(8,128)(2,1)}, bf16[2,64,1152]{2,1,0:T(8,128)(2,1)}, bf16[2,64,1152]{2,1,0:T(8,128)(2,1)}, bf16[2,64,1152]{2,1,0:T(8,128)(2,1)}) custom-call(s32[1]{0:T(128)} %bitcast.refs_0_, bf16[1024,512]{1,0:T(8,128)(2,1)} %get-tuple-element.75.refs_2_.refs_1_, bf16[1,128,1152]{2,1,0:T(8,128)(2,1)} %get-tuple-element.82.refs_2_, ...), custom_call_target="tpu_custom_call" | custom-call | flops 603979776 | bytes 3538944 | tf_op jit(solution)/shard_map/combine/pallas_call | solution.py:42
  126.9 4.1 %collective-permute-start.14 = (bf16[2,64,1152]{2,1,0:T(8,128)(2,1)}, bf16[2,64,1152]{2,1,0:T(8,128)(2,1)S(1)}, u32[]{:S(2)}, u32[]{:S(2)}) collective-permute-start(bf16[2,64,1152]{2,1,0:T(8,128)(2,1)} %get-tuple-element.92), channel_id=1, source_target_pairs={{0,4},{1,5},{2,6},{3,7},{4,0},{5,1},{6,2},{7,3},{8,12},{9,13},{10,... | collective-permute-start | bytes 884744 | tf_op jit(solution)/shard_map/ppermute | solution.py:86
  133.1 15.9 %expert.3 = (bf16[1,128,1152]{2,1,0:T(8,128)(2,1)}, bf16[1,128,1152]{2,1,0:T(8,128)(2,1)}, bf16[1,128,1152]{2,1,0:T(8,128)(2,1)}, bf16[1,128,1152]{2,1,0:T(8,128...) custom-call(f32[512,1]{1,0:T(8,128)} %get-tuple-element.135.refs_0_,, ...), custom_call_target="tpu_custom_call" | custom-call | flops 8153726976 | bytes 20054016 | tf_op jit(solution)/shard_map/expert/pallas_call | solution.py:42
  150.9 9.5 %weight_gradient.2.refs_6_ = bf16[1152,2304]{1,0:T(8,128)(2,1)} custom-call(bf16[512,1152]{1,0:T(8,128)(2,1)} %get-tuple-element.94.refs_0_, bf16[512,2304]{1,0:T(8,128)(2,1)} %get-tuple-element.95.refs_1_, bf16[512,1152]{1,0:T(8,128)(2,1)} %get-tuple-element.96.refs_2_, bf16[512,2304]{1,0:T(8,128)(2,1)} %get-tuple-element.97.refs_3_), custom_call_target="tpu_custom_call" | custom-call | flops 5435817984 | bytes 5308416 | tf_op jit(solution)/shard_map/weight_gradient/pallas_call | solution.py:42
  160.5 3.9 %collective-permute-done.13.refs_3_.refs_5_ = bf16[1,128,1152]{2,1,0:T(8,128)(2,1)S(1)} collective-permute-done((bf16[1,128,1152]{2,1,0:T(8,128)(2,1)}, bf16[1,128,1152]{2,1,0:T(8,128)(2,1)S(1)}, u32[]{:S(2)}, u32[]{:S(2)}) %collective-permute-start.13) | collective-permute-done | bytes 294944 | tf_op jit(solution)/shard_map/ppermute | solution.py:101
  175.1 10.1 %weight_gradient.3.refs_8_ = bf16[2304,1152]{1,0:T(8,128)(2,1)} custom-call(bf16[512,2304]{1,0:T(8,128)(2,1)} %get-tuple-element.106.refs_0_, bf16[512,1152]{1,0:T(8,128)(2,1)} %get-tuple-element.107.refs_1_, bf16[512,2304]{1,0:T(8,128)(2,1)} %get-tuple-element.108.refs_2_, bf16[512,1152]{1,0:T(8,128)(2,1)} %get-tuple-element.109.refs_3_, ...), custom_call_target="tpu_custom_call" | custom-call | flops 5435817984 | bytes 5308416 | tf_op jit(solution)/shard_map/weight_gradient/pallas_call | solution.py:42
  185.2 14.6 %collective-permute-done.17.refs_1_.refs_9_ = bf16[2,64,1152]{2,1,0:T(8,128)(2,1)S(1)} collective-permute-done((bf16[2,64,1152]{2,1,0:T(8,128)(2,1)}, bf16[2,64,1152]{2,1,0:T(8,128)(2,1)S(1)}, u32[]{:S(2)}, u32[]{:S(2)}) %collective-permute-start.17) | collective-permute-done | bytes 294944 | tf_op jit(solution)/shard_map/ppermute | solution.py:86
  207.4 5.0 %value_gradient.1 = (bf16[1,64,1152]{2,1,0:T(8,128)(2,1)}, bf16[1,64,1152]{2,1,0:T(8,128)(2,1)}, bf16[1,64,1152]{2,1,0:T(8,128)(2,1)}, bf16[1,64,1152]{2,1,0:T(8...) custom-call(s32[1]{0:T(128)} %bitcast.refs_0_, ...), custom_call_target="tpu_custom_call" | custom-call | flops 301989888 | bytes 4718592 | tf_op jit(solution)/shard_map/value_gradient/pallas_call | solution.py:42
  218.1 12.9 %pair_gradients.1 = (bf16[1,2,64,1152]{3,2,1,0:T(8,128)(2,1)}, bf16[1,2,64,1152]{3,2,1,0:T(8,128)(2,1)}, bf16[1,2,64,1152]{3,2,1,0:T(8,128)(2,1)}, bf16[1,2,64,1...) custom-call(s32[1]{0:T(128)} %bitcast.refs_0_, ...), custom_call_target="tpu_custom_call" | custom-call | flops 905969664 | bytes 9437184 | tf_op jit(solution)/shard_map/pair_gradients/pallas_call | solution.py:42
  234.6 14.2 %collective-permute-start.33 = (bf16[1,64,1152]{2,1,0:T(8,128)(2,1)S(1)}, bf16[1,64,1152]{2,1,0:T(8,128)(2,1)S(1)}, u32[]{:S(2)}, u32[]{:S(2)}) collective-permute-start(bf16[1,64,1152]{2,1,0:T(8,128)(2,1)S(1)} %copy-done.47), channel_id=1, source_target_pairs={{0,2},{1,3},{2,0},{3,1},{4,6},{5,7},{6,4},{7,5},{8,10},{9,11},{10,... | collective-permute-start | bytes 442376 | tf_op jit(solution)/shard_map/ppermute | solution.py:101
  259.7 11.7 %collective-permute-start.26 = (bf16[1,2,64,1152]{3,2,1,0:T(8,128)(2,1)S(1)}, bf16[1,2,64,1152]{3,2,1,0:T(8,128)(2,1)S(1)}, u32[]{:S(2)}, u32[]{:S(2)}) collective-permute-start(bf16[1,2,64,1152]{3,2,1,0:T(8,128)(2,1)S(1)} %copy-done.44), channel_id=1, source_target_pairs={{0,2},{1,3},{2,0},{3,1},{4,6},{5,7},{6,4},{7,5},{8,10},{9,11},{10,... | collective-permute-start | bytes 884744 | tf_op jit(solution)/shard_map/ppermute | solution.py:101
  271.5 6.0 %collective-permute-done.22.refs_2_ = bf16[1,2,64,1152]{3,2,1,0:T(8,128)(2,1)S(1)} collective-permute-done((bf16[1,2,64,1152]{3,2,1,0:T(8,128)(2,1)}, bf16[1,2,64,1152]{3,2,1,0:T(8,128)(2,1)S(1)}, u32[]{:S(2)}, u32[]{:S(2)}) %collective-permute-start.22) | collective-permute-done | bytes 294944 | tf_op jit(solution)/shard_map/ppermute | solution.py:101
  277.5 4.1 %fusion = (f32[288,2304]{1,0:T(8,128)}, f32[1,288,2304]{2,1,0:T(8,128)}) fusion(bf16[288,2304]{1,0:T(8,128)(2,1)} %reduce-scatter.3.cloned.1.call-done), kind=kLoop, calls=%fused_computation.4 | loop fusion | flops 663552 | bytes 6635520 | tf_op jit(solution)/shard_map/convert_element_type | solution.py:676
  281.7 8.3 %collective-permute-done.24.refs_4_ = bf16[1,2,64,1152]{3,2,1,0:T(8,128)(2,1)S(1)} collective-permute-done((bf16[1,2,64,1152]{3,2,1,0:T(8,128)(2,1)}, bf16[1,2,64,1152]{3,2,1,0:T(8,128)(2,1)S(1)}, u32[]{:S(2)}, u32[]{:S(2)}) %collective-permute-start.24) | collective-permute-done | bytes 294944 | tf_op jit(solution)/shard_map/ppermute | solution.py:101
  294.2 3.7 %widen.1 = f32[576,1152]{1,0:T(8,128)} custom-call(bf16[576,1152]{1,0:T(8,128)(2,1)} %reduce-scatter.5.cloned.1.call-done.refs_0_), custom_call_target="tpu_custom_call" | custom-call | bytes 3981312 | tf_op jit(solution)/shard_map/widen/pallas_call | solution.py:42
  (171 shorter events, 60.4 us)
Async XLA Ops:
  7.2 270.4 %reduce-scatter.3.cloned.1.call-start = ((), (), s32[]{:S(2)}) async-start(), calls=%async_computation.2 | async-start | bytes 6635520 | tf_op jit(solution)/shard_map/reduce_scatter | solution.py:676
  15.5 29.7 %collective-permute-start.1 = (bf16[1,256,1152]{2,1,0:T(8,128)(2,1)}, bf16[1,256,1152]{2,1,0:T(8,128)(2,1)S(1)}, u32[]{:S(2)}, u32[]{:S(2)}) collective-permute-start(bf16[1,256,1152]{2,1,0:T(8,128)(2,1)} %get-tuple-element.73), channel_id=1, source_target_pairs={{0,2},{1,3},{2,0},{3,1},{4,6},{5,7},{6,4},{7,5},{8,10},{9,11},{10,... | collective-permute-start | bytes 1769480 | tf_op jit(solution)/shard_map/ppermute | solution.py:101
  18.2 39.1 %collective-permute-start.2 = (bf16[1,256,1152]{2,1,0:T(8,128)(2,1)}, bf16[1,256,1152]{2,1,0:T(8,128)(2,1)S(1)}, u32[]{:S(2)}, u32[]{:S(2)}) collective-permute-start(bf16[1,256,1152]{2,1,0:T(8,128)(2,1)} %get-tuple-element.74), channel_id=1, source_target_pairs={{0,3},{1,2},{2,1},{3,0},{4,7},{5,6},{6,5},{7,4},{8,11},{9,10},{10,... | collective-permute-start | bytes 1769480 | tf_op jit(solution)/shard_map/ppermute | solution.py:101
  18.2 55.1 %collective-permute-start.3 = (bf16[1,256,1152]{2,1,0:T(8,128)(2,1)}, bf16[1,256,1152]{2,1,0:T(8,128)(2,1)S(1)}, u32[]{:S(2)}, u32[]{:S(2)}) collective-permute-start(bf16[1,256,1152]{2,1,0:T(8,128)(2,1)} %get-tuple-element.77), channel_id=1, source_target_pairs={{0,4},{1,5},{2,6},{3,7},{4,0},{5,1},{6,2},{7,3},{8,12},{9,13},{10,... | collective-permute-start | bytes 1769480 | tf_op jit(solution)/shard_map/ppermute | solution.py:101
  21.0 52.4 %collective-permute-start.4 = (bf16[1,256,1152]{2,1,0:T(8,128)(2,1)}, bf16[1,256,1152]{2,1,0:T(8,128)(2,1)S(1)}, u32[]{:S(2)}, u32[]{:S(2)}) collective-permute-start(bf16[1,256,1152]{2,1,0:T(8,128)(2,1)} %get-tuple-element.78), channel_id=1, source_target_pairs={{0,6},{1,7},{6,0},{7,1},{8,14},{9,15},{14,8},{15,9},{16,22},{17,23... | collective-permute-start | bytes 1769480 | tf_op jit(solution)/shard_map/ppermute | solution.py:108
  34.4 78.1 %collective-permute-start.7 = (bf16[1,256,1152]{2,1,0:T(8,128)(2,1)S(1)}, bf16[1,256,1152]{2,1,0:T(8,128)(2,1)S(1)}, u32[]{:S(2)}, u32[]{:S(2)}) collective-permute-start(bf16[1,256,1152]{2,1,0:T(8,128)(2,1)S(1)} %copy-done.36), channel_id=1, source_target_pairs={{2,4},{3,5},{4,2},{5,3},{10,12},{11,13},{12,10},{13,11},{18,20},{1... | collective-permute-start | bytes 1769480 | tf_op jit(solution)/shard_map/ppermute | solution.py:108
  45.2 67.2 %collective-permute-start.5 = (bf16[1,256,1152]{2,1,0:T(8,128)(2,1)S(1)}, bf16[1,256,1152]{2,1,0:T(8,128)(2,1)S(1)}, u32[]{:S(2)}, u32[]{:S(2)}) collective-permute-start(bf16[1,256,1152]{2,1,0:T(8,128)(2,1)S(1)} %copy-done.38), channel_id=1, source_target_pairs={{0,5},{1,4},{2,7},{3,6},{4,1},{5,0},{6,3},{7,2},{8,13},{9,12},{10,... | collective-permute-start | bytes 1769480 | tf_op jit(solution)/shard_map/ppermute | solution.py:101
  57.3 55.1 %collective-permute-start.6 = (bf16[1,256,1152]{2,1,0:T(8,128)(2,1)S(1)}, bf16[1,256,1152]{2,1,0:T(8,128)(2,1)S(1)}, u32[]{:S(2)}, u32[]{:S(2)}) collective-permute-start(bf16[1,256,1152]{2,1,0:T(8,128)(2,1)S(1)} %copy-done.37), channel_id=1, source_target_pairs={{0,7},{1,6},{2,5},{3,4},{4,3},{5,2},{6,1},{7,0},{8,15},{9,14},{10,... | collective-permute-start | bytes 1769480 | tf_op jit(solution)/shard_map/ppermute | solution.py:101
  90.1 22.4 %collective-permute-start.8 = (bf16[1,128,1152]{2,1,0:T(8,128)(2,1)}, bf16[1,128,1152]{2,1,0:T(8,128)(2,1)S(1)}, u32[]{:S(2)}, u32[]{:S(2)}) collective-permute-start(bf16[1,128,1152]{2,1,0:T(8,128)(2,1)} %get-tuple-element.83), channel_id=1, source_target_pairs={{0,1},{1,0},{2,3},{3,2},{4,5},{5,4},{6,7},{7,6},{8,9},{9,8},{10,11... | collective-permute-start | bytes 884744 | tf_op jit(solution)/shard_map/ppermute | solution.py:101
  90.1 26.7 %collective-permute-start.9 = (bf16[1,128,1152]{2,1,0:T(8,128)(2,1)}, bf16[1,128,1152]{2,1,0:T(8,128)(2,1)S(1)}, u32[]{:S(2)}, u32[]{:S(2)}) collective-permute-start(bf16[1,128,1152]{2,1,0:T(8,128)(2,1)} %get-tuple-element.84), channel_id=1, source_target_pairs={{0,2},{1,3},{2,0},{3,1},{4,6},{5,7},{6,4},{7,5},{8,10},{9,11},{10,... | collective-permute-start | bytes 884744 | tf_op jit(solution)/shard_map/ppermute | solution.py:101
  126.9 33.5 %collective-permute-start.14 = (bf16[2,64,1152]{2,1,0:T(8,128)(2,1)}, bf16[2,64,1152]{2,1,0:T(8,128)(2,1)S(1)}, u32[]{:S(2)}, u32[]{:S(2)}) collective-permute-start(bf16[2,64,1152]{2,1,0:T(8,128)(2,1)} %get-tuple-element.92), channel_id=1, source_target_pairs={{0,4},{1,5},{2,6},{3,7},{4,0},{5,1},{6,2},{7,3},{8,12},{9,13},{10,... | collective-permute-start | bytes 884744 | tf_op jit(solution)/shard_map/ppermute | solution.py:86
  131.1 29.4 %collective-permute-start.15 = (bf16[2,64,1152]{2,1,0:T(8,128)(2,1)}, bf16[2,64,1152]{2,1,0:T(8,128)(2,1)S(1)}, u32[]{:S(2)}, u32[]{:S(2)}) collective-permute-start(bf16[2,64,1152]{2,1,0:T(8,128)(2,1)} %get-tuple-element.93), channel_id=1, source_target_pairs={{0,6},{1,7},{2,4},{3,5},{4,2},{5,3},{6,0},{7,1},{8,14},{9,15},{10,... | collective-permute-start | bytes 884744 | tf_op jit(solution)/shard_map/ppermute | solution.py:86
  165.8 128.4 %reduce-scatter.5.cloned.1.call-start = ((), (), s32[]{:S(2)}) async-start(), calls=%async_computation.3 | async-start | bytes 6635520 | tf_op jit(solution)/shard_map/reduce_scatter | solution.py:687
  172.4 27.3 %collective-permute-start.17 = (bf16[2,64,1152]{2,1,0:T(8,128)(2,1)}, bf16[2,64,1152]{2,1,0:T(8,128)(2,1)S(1)}, u32[]{:S(2)}, u32[]{:S(2)}) collective-permute-start(bf16[2,64,1152]{2,1,0:T(8,128)(2,1)} %get-tuple-element.102), channel_id=1, source_target_pairs={{0,4},{1,5},{2,6},{3,7},{4,0},{5,1},{6,2},{7,3},{8,12},{9,13},{10,... | collective-permute-start | bytes 884744 | tf_op jit(solution)/shard_map/ppermute | solution.py:86
  173.6 26.2 %collective-permute-start.18 = (bf16[2,64,1152]{2,1,0:T(8,128)(2,1)}, bf16[2,64,1152]{2,1,0:T(8,128)(2,1)S(1)}, u32[]{:S(2)}, u32[]{:S(2)}) collective-permute-start(bf16[2,64,1152]{2,1,0:T(8,128)(2,1)} %get-tuple-element.103), channel_id=1, source_target_pairs={{0,2},{1,3},{2,0},{3,1},{4,6},{5,7},{6,4},{7,5},{8,10},{9,11},{10,... | collective-permute-start | bytes 884744 | tf_op jit(solution)/shard_map/ppermute | solution.py:86
  213.9 20.6 %collective-permute-start.30 = (bf16[1,64,1152]{2,1,0:T(8,128)(2,1)}, bf16[1,64,1152]{2,1,0:T(8,128)(2,1)S(1)}, u32[]{:S(2)}, u32[]{:S(2)}) collective-permute-start(bf16[1,64,1152]{2,1,0:T(8,128)(2,1)} %get-tuple-element.126), channel_id=1, source_target_pairs={{0,7},{1,6},{2,5},{3,4},{4,3},{5,2},{6,1},{7,0},{8,15},{9,14},{10,... | collective-permute-start | bytes 442376 | tf_op jit(solution)/shard_map/ppermute | solution.py:101
  215.8 36.2 %collective-permute-start.31 = (bf16[1,64,1152]{2,1,0:T(8,128)(2,1)}, bf16[1,64,1152]{2,1,0:T(8,128)(2,1)S(1)}, u32[]{:S(2)}, u32[]{:S(2)}) collective-permute-start(bf16[1,64,1152]{2,1,0:T(8,128)(2,1)} %get-tuple-element.127), channel_id=1, source_target_pairs={{0,5},{1,4},{2,7},{3,6},{4,1},{5,0},{6,3},{7,2},{8,13},{9,12},{10,... | collective-permute-start | bytes 442376 | tf_op jit(solution)/shard_map/ppermute | solution.py:101
  231.0 28.7 %collective-permute-start.21 = (bf16[1,2,64,1152]{3,2,1,0:T(8,128)(2,1)}, bf16[1,2,64,1152]{3,2,1,0:T(8,128)(2,1)S(1)}, u32[]{:S(2)}, u32[]{:S(2)}) collective-permute-start(bf16[1,2,64,1152]{3,2,1,0:T(8,128)(2,1)} %get-tuple-element.114), channel_id=1, source_target_pairs={{0,6},{1,7},{2,4},{3,5},{4,2},{5,3},{6,0},{7,1},{8,14},{9,15},{10,... | collective-permute-start | bytes 884744 | tf_op jit(solution)/shard_map/ppermute | solution.py:101
  232.6 44.9 %collective-permute-start.22 = (bf16[1,2,64,1152]{3,2,1,0:T(8,128)(2,1)}, bf16[1,2,64,1152]{3,2,1,0:T(8,128)(2,1)S(1)}, u32[]{:S(2)}, u32[]{:S(2)}) collective-permute-start(bf16[1,2,64,1152]{3,2,1,0:T(8,128)(2,1)} %get-tuple-element.115), channel_id=1, source_target_pairs={{0,4},{1,5},{2,6},{3,7},{4,0},{5,1},{6,2},{7,3},{8,12},{9,13},{10,... | collective-permute-start | bytes 884744 | tf_op jit(solution)/shard_map/ppermute | solution.py:101
  234.6 20.7 %collective-permute-start.33 = (bf16[1,64,1152]{2,1,0:T(8,128)(2,1)S(1)}, bf16[1,64,1152]{2,1,0:T(8,128)(2,1)S(1)}, u32[]{:S(2)}, u32[]{:S(2)}) collective-permute-start(bf16[1,64,1152]{2,1,0:T(8,128)(2,1)S(1)} %copy-done.47), channel_id=1, source_target_pairs={{0,2},{1,3},{2,0},{3,1},{4,6},{5,7},{6,4},{7,5},{8,10},{9,11},{10,... | collective-permute-start | bytes 442376 | tf_op jit(solution)/shard_map/ppermute | solution.py:101
  253.0 28.6 %collective-permute-start.23 = (bf16[1,2,64,1152]{3,2,1,0:T(8,128)(2,1)}, bf16[1,2,64,1152]{3,2,1,0:T(8,128)(2,1)S(1)}, u32[]{:S(2)}, u32[]{:S(2)}) collective-permute-start(bf16[1,2,64,1152]{3,2,1,0:T(8,128)(2,1)} %get-tuple-element.116), channel_id=1, source_target_pairs={{0,7},{1,6},{2,5},{3,4},{4,3},{5,2},{6,1},{7,0},{8,15},{9,14},{10,... | collective-permute-start | bytes 884744 | tf_op jit(solution)/shard_map/ppermute | solution.py:101
  255.2 34.7 %collective-permute-start.24 = (bf16[1,2,64,1152]{3,2,1,0:T(8,128)(2,1)}, bf16[1,2,64,1152]{3,2,1,0:T(8,128)(2,1)S(1)}, u32[]{:S(2)}, u32[]{:S(2)}) collective-permute-start(bf16[1,2,64,1152]{3,2,1,0:T(8,128)(2,1)} %get-tuple-element.117), channel_id=1, source_target_pairs={{0,5},{1,4},{2,7},{3,6},{4,1},{5,0},{6,3},{7,2},{8,13},{9,12},{10,... | collective-permute-start | bytes 884744 | tf_op jit(solution)/shard_map/ppermute | solution.py:101
  255.2 34.7 %collective-permute-start.25 = (bf16[1,2,64,1152]{3,2,1,0:T(8,128)(2,1)}, bf16[1,2,64,1152]{3,2,1,0:T(8,128)(2,1)S(1)}, u32[]{:S(2)}, u32[]{:S(2)}) collective-permute-start(bf16[1,2,64,1152]{3,2,1,0:T(8,128)(2,1)} %get-tuple-element.118), channel_id=1, source_target_pairs={{0,3},{1,2},{2,1},{3,0},{4,7},{5,6},{6,5},{7,4},{8,11},{9,10},{10,... | collective-permute-start | bytes 884744 | tf_op jit(solution)/shard_map/ppermute | solution.py:101
  259.7 30.2 %collective-permute-start.26 = (bf16[1,2,64,1152]{3,2,1,0:T(8,128)(2,1)S(1)}, bf16[1,2,64,1152]{3,2,1,0:T(8,128)(2,1)S(1)}, u32[]{:S(2)}, u32[]{:S(2)}) collective-permute-start(bf16[1,2,64,1152]{3,2,1,0:T(8,128)(2,1)S(1)} %copy-done.44), channel_id=1, source_target_pairs={{0,2},{1,3},{2,0},{3,1},{4,6},{5,7},{6,4},{7,5},{8,10},{9,11},{10,... | collective-permute-start | bytes 884744 | tf_op jit(solution)/shard_map/ppermute | solution.py:101
  (62 other events, 768.4 us)
Sparse Core Ops, SparseCore 0:
  165.9 61.5 reduce-scatter.2
  230.5 62.0 reduce-scatter.4
